TPU v7x, 32 devices: a whole 2x2x4 slice. The times are simulated.
32 devices in a mesh: seq: 2 (over x), tok: 16 (over z, y, core).
Axes of the slice: x: 2, y: 2, z: 4, core: 2. Of those that a mesh axis runs over, the one named last changes fastest.
Arguments:
- tokens: bfloat16 [6, 4096, 768], P('seq', 'tok'), may hold values from -6 to 6
- skip_features: bfloat16 [6, 4096, 8, 128], P('seq', 'tok'), may hold values from -6 to 6
- crop_sides: int32 [6, 45], P('seq'), may hold values from 0 to 6, as said below
- ln1_gain: float32 [768], replicated, may hold values from 0.5 to 1.5
- ln1_bias: float32 [768], replicated, may hold values from -1.25 to 1.25
- qkv_weight: bfloat16 [768, 2304], replicated, may hold values from -0.21875 to 0.21875
- qv_bias: float32 [2, 768], replicated, may hold values from -1.25 to 1.25
- out_weight: bfloat16 [768, 768], replicated, may hold values from -2 to 2
- out_bias: float32 [768], replicated, may hold values from -1.25 to 1.25
- ln2_gain: float32 [768], replicated, may hold values from 0.5 to 1.5
- ln2_bias: float32 [768], replicated, may hold values from -1.25 to 1.25
- fc1_weight: bfloat16 [768, 3072], replicated, may hold values from -0.21875 to 0.21875
- fc1_bias: float32 [3072], replicated, may hold values from -1.25 to 1.25
- fc2_weight: bfloat16 [3072, 768], replicated, may hold values from -0.109375 to 0.109375
- fc2_bias: float32 [768], replicated, may hold values from -1.25 to 1.25
- deconv_weight: bfloat16 [768, 1024], replicated, may hold values from -0.21875 to 0.21875
- conv1_weight: bfloat16 [27, 256, 128], replicated, may hold values from -0.078125 to 0.078125
- conv2_weight: bfloat16 [27, 128, 128], replicated, may hold values from -0.109375 to 0.109375
- conv3_weight: bfloat16 [256, 128], replicated, may hold values from -0.375 to 0.375
- cotangent: bfloat16 [6, 4096, 8, 128], P('seq', 'tok'), may hold values from -6 to 6
Outputs:
- section_out: bfloat16 [6, 4096, 8, 128], P('seq', 'tok')
- token_grad: float32 [6, 4096, 768], P('seq', 'tok')
- skip_grad: float32 [6, 4096, 8, 128], P('seq', 'tok')
- ln1_gain_grad: float32 [768], P('tok')
- ln1_bias_grad: float32 [768], P('tok')
- qkv_grad: float32 [768, 2304], P('tok')
- qv_bias_grad: float32 [2, 768], P(None, 'tok')
- out_grad: float32 [768, 768], P('tok')
- out_bias_grad: float32 [768], P('tok')
- ln2_gain_grad: float32 [768], P('tok')
- ln2_bias_grad: float32 [768], P('tok')
- fc1_grad: float32 [768, 3072], P('tok')
- fc1_bias_grad: float32 [3072], P('tok')
- fc2_grad: float32 [3072, 768], P('tok')
- fc2_bias_grad: float32 [768], P('tok')
- deconv_grad: float32 [768, 1024], P('tok')
- conv1_grad: float32 [27, 256, 128], P(None, None, 'tok')
- conv2_grad: float32 [27, 128, 128], P(None, None, 'tok')
- conv3_grad: float32 [256, 128], P(None, 'tok')
Inputs may be any that keep to these rules, and one draw needn't show every extreme that they name: `crop_sides`: row by row, the sides in patches of the crops packed in order into one sequence: 4 or 6, then zeros; the crops' sizes side * side * side add up to exactly 4096, and a row holds a positive multiple of 8 crops of side 6.
All inputs are finite; a program needn't handle non-finite values.
Results may differ from a plain program's by a relative error of at most 0.028.
Values may be sent and summed in bfloat16 or wider, within the bound.
A program may use at most 640 MiB of HBM per device.

v0:
```python
from functools import partial
import math

import jax
import jax.numpy as jnp
import numpy as np
from jax import lax
from jax.sharding import PartitionSpec as P

HEADS = 12
HEAD_DIM = 64


side_small = 4
side_big = 6
halo_rows = 43
key_reach = 215
norm_eps = 1e-05
far_below = -1e30
highest = lax.Precision.HIGHEST
in_part = {-1: (1, 2), 0: (0, 2), 1: (0, 1)}
out_part = {-1: (0, 1), 0: (0, 2), 1: (1, 2)}


def padded_2(shard, sides, width):
    for axis, dim in sides:
        count, length = (lax.axis_size(axis), shard.shape[dim])
        up = [(i, (i + 1) % count) for i in range(count - 1)]
        down = [(j, i) for i, j in up]
        last = lax.slice_in_dim(shard, length - width, length, axis=dim)
        leading = lax.slice_in_dim(shard, 0, width, axis=dim)
        before = lax.ppermute(last, axis, up)
        after = lax.ppermute(leading, axis, down)
        shard = jnp.concatenate([before, shard, after], axis=dim)
    return shard


def passed_along(block, axis, distance):
    devices = range(lax.axis_size(axis))
    route = [(i - distance, i) for i in devices if i - distance in devices]
    return lax.ppermute(block, axis, route)


def all_offsets():
    step_values = (-1, 0, 1)
    return [
        (step_x, step_y, step_z)
        for step_x in step_values
        for step_y in step_values
        for step_z in step_values
    ]


def index_tuples(table_shape):
    tuples_out = [()]
    for extent in table_shape:
        tuples_out = [prefix + (position,) for prefix in tuples_out for position in range(extent)]
    return tuples_out


def tap_table(offset):
    in_lists = [
        list(range(in_part[offset_entry][0], in_part[offset_entry][1])) for offset_entry in offset
    ]
    out_lists = [
        list(range(out_part[offset_entry][0], out_part[offset_entry][1])) for offset_entry in offset
    ]
    table_shape = tuple((len(members) for members in in_lists)) + tuple(
        (len(members) for members in out_lists)
    )
    tap_index = np.zeros(table_shape, dtype=np.int32)
    for entry_index in index_tuples(table_shape):
        flat_tap = 0
        for axis_id in range(3):
            source_sub = in_lists[axis_id][entry_index[axis_id]]
            target_sub = out_lists[axis_id][entry_index[3 + axis_id]]
            flat_tap = flat_tap * 3 + 2 * offset[axis_id] + source_sub - target_sub + 1
        tap_index[entry_index] = flat_tap
    return tap_index


def sub_cut(array_in, parts, offset):
    begins = [parts[offset_entry][0] for offset_entry in offset]
    finish = [parts[offset_entry][1] for offset_entry in offset]
    return array_in[:, :, begins[0] : finish[0], begins[1] : finish[1], begins[2] : finish[2]]


def sub_pad(array_in, parts, offset):
    widths = (
        [(0, 0), (0, 0)]
        + [(parts[offset_entry][0], 2 - parts[offset_entry][1]) for offset_entry in offset]
        + [(0, 0)]
    )
    return jnp.pad(array_in, widths)


def crop_bounds(sides):
    volumes = sides * sides * sides
    ends_at = jnp.cumsum(volumes, axis=-1, dtype=jnp.int32)
    return (ends_at - volumes, ends_at)


def locate(sides, places):
    starts, ends_at = crop_bounds(sides)
    inside = (places[:, :, None] >= starts[:, None, :]) & (places[:, :, None] < ends_at[:, None, :])
    numbers = jnp.arange(sides.shape[-1], dtype=jnp.int32)
    found = jnp.any(inside, axis=-1)
    segment = jnp.sum(jnp.where(inside, numbers, 0), axis=-1, dtype=jnp.int32)
    segment = jnp.where(found, segment, -1)
    side_of = jnp.sum(jnp.where(inside, sides[:, None, :], 0), axis=-1, dtype=jnp.int32)
    first_of = jnp.sum(jnp.where(inside, starts[:, None, :], 0), axis=-1, dtype=jnp.int32)
    return (inside, segment, side_of, first_of)


def geometry(side_of, first_of, places):
    local_pos = places - first_of
    safe_side = jnp.maximum(side_of, 1)
    return (
        local_pos // (safe_side * safe_side),
        local_pos // safe_side % safe_side,
        local_pos % safe_side,
        side_of,
        side_of == side_big,
    )


def step_sizes(offset):
    near_step = offset[0] * side_small * side_small + offset[1] * side_small + offset[2]
    far_step = offset[0] * side_big * side_big + offset[1] * side_big + offset[2]
    return (near_step, far_step)


def in_crop(shape_info, offset):
    row_pos, column, depth_pos, side_of, is_big = shape_info
    inside_crop = (row_pos + offset[0] >= 0) & (row_pos + offset[0] < side_of)
    inside_crop = inside_crop & (column + offset[1] >= 0) & (column + offset[1] < side_of)
    return inside_crop & (depth_pos + offset[2] >= 0) & (depth_pos + offset[2] < side_of)


def shifted(padded, offset, shape_info, length):
    near_step, far_step = step_sizes(offset)
    small_view = lax.slice_in_dim(
        padded, halo_rows + near_step, halo_rows + near_step + length, axis=1
    )
    big_view = lax.slice_in_dim(padded, halo_rows + far_step, halo_rows + far_step + length, axis=1)
    is_big = shape_info[4][:, :, None, None, None, None]
    inside_crop = in_crop(shape_info, offset)[:, :, None, None, None, None]
    picked = jnp.where(is_big, big_view, small_view)
    return jnp.where(inside_crop, picked, jnp.zeros((), padded.dtype))


def conv_forward(padded, kernel, shape_info, length):
    result_sum = 0.0
    for offset in all_offsets():
        source = sub_cut(shifted(padded, offset, shape_info, length), in_part, offset)
        kernel_block = kernel[tap_table(offset)]
        term_part = jnp.einsum(
            "stxyzc,xyzXYZcd->stXYZd", source, kernel_block, preferred_element_type=jnp.float32
        )
        result_sum = result_sum + sub_pad(term_part, out_part, offset)
    return result_sum


def unshift(grad_pad, grad_source, offset, shape_info, length):
    near_step, far_step = step_sizes(offset)
    inside_crop = in_crop(shape_info, offset)[:, :, None, None, None, None]
    is_big = shape_info[4][:, :, None, None, None, None]
    grad_pad = grad_pad.at[:, halo_rows + near_step : halo_rows + near_step + length].add(
        jnp.where(inside_crop & ~is_big, grad_source, 0.0)
    )
    return grad_pad.at[:, halo_rows + far_step : halo_rows + far_step + length].add(
        jnp.where(inside_crop & is_big, grad_source, 0.0)
    )


def conv_backward(padded, kernel, shape_info, grad_out):
    length = grad_out.shape[1]
    grad_pad = jnp.zeros(padded.shape, jnp.float32)
    grad_kernel = jnp.zeros(kernel.shape, jnp.float32)
    for offset in all_offsets():
        tap_index = tap_table(offset)
        source = sub_cut(shifted(padded, offset, shape_info, length), in_part, offset)
        target = sub_cut(grad_out, out_part, offset)
        kernel_block = kernel[tap_index]
        grad_block = jnp.einsum(
            "stxyzc,stXYZd->xyzXYZcd", source, target, preferred_element_type=jnp.float32
        )
        grad_kernel = grad_kernel.at[tap_index.reshape(-1)].add(
            grad_block.reshape(-1, kernel.shape[1], kernel.shape[2])
        )
        grad_source = jnp.einsum(
            "stXYZd,xyzXYZcd->stxyzc", target, kernel_block, preferred_element_type=jnp.float32
        )
        grad_pad = unshift(
            grad_pad, sub_pad(grad_source, in_part, offset), offset, shape_info, length
        )
    return (grad_pad, grad_kernel)


def with_rims(field):
    return padded_2(field, (("tok", 1),), halo_rows)


def fold_rims(grad_pad):
    edges = jnp.concatenate(
        [grad_pad[:, :halo_rows], grad_pad[:, grad_pad.shape[1] - halo_rows :]], axis=1
    )
    widened = padded_2(edges.astype(jnp.bfloat16), (("tok", 1),), halo_rows).astype(edges.dtype)
    owned = grad_pad[:, halo_rows : grad_pad.shape[1] - halo_rows]
    owned = owned.at[:, :halo_rows].add(widened[:, :halo_rows])
    return owned.at[:, owned.shape[1] - halo_rows :].add(widened[:, 3 * halo_rows :])


def chain_total(own, reaches, passer):
    total = own
    for direction in (1, -1):
        carried = jnp.zeros_like(own)
        for step_number in range(reaches):
            carried = passer(own + carried, direction)
        total = total + carried
    return total


def layer_norm(values_in, gain, shift):
    centered = values_in - jnp.mean(values_in, axis=-1, keepdims=True)
    variance = jnp.mean(centered * centered, axis=-1, keepdims=True)
    return centered * lax.rsqrt(variance + norm_eps) * gain + shift


def crop_totals(inside_float, field):
    return jnp.einsum(
        "stk,stc->skc", inside_float, jnp.sum(field, axis=(2, 3, 4)), precision=highest
    )


def spread(inside_float, crop_values):
    return jnp.einsum("stk,skc->stc", inside_float, crop_values, precision=highest)[
        :, :, None, None, None, :
    ]


def norm_forward(fields, inside_float, counts, reaches):
    sums = jnp.stack([crop_totals(inside_float, field) for field in fields])
    squares = jnp.stack([crop_totals(inside_float, field * field) for field in fields])

    def passer(partial_sums, direction):
        return passed_along(partial_sums.astype(jnp.bfloat16), "tok", direction).astype(
            partial_sums.dtype
        )

    both = chain_total(jnp.stack([sums, squares]), reaches, passer)
    sums, squares = (both[0], both[1])
    means = sums / counts[None, :, :, None]
    scales = lax.rsqrt(squares / counts[None, :, :, None] - means * means + norm_eps)
    normed = []
    scale_rows = []
    for number in range(len(fields)):
        scale_row = spread(inside_float, scales[number])
        normed.append((fields[number] - spread(inside_float, means[number])) * scale_row)
        scale_rows.append(scale_row)
    return (normed, scale_rows)


def norm_backward(grads, normed, scale_rows, inside_float, counts, reaches):
    firsts = jnp.stack([crop_totals(inside_float, grads[number]) for number in range(len(grads))])
    seconds = jnp.stack(
        [crop_totals(inside_float, grads[number] * normed[number]) for number in range(len(grads))]
    )

    def passer(partial_sums, direction):
        return passed_along(partial_sums.astype(jnp.bfloat16), "tok", direction).astype(
            partial_sums.dtype
        )

    both = chain_total(jnp.stack([firsts, seconds]), reaches, passer)
    firsts = both[0] / counts[None, :, :, None]
    seconds = both[1] / counts[None, :, :, None]
    results = []
    for number in range(len(grads)):
        results.append(
            scale_rows[number]
            * (
                grads[number]
                - spread(inside_float, firsts[number])
                - normed[number] * spread(inside_float, seconds[number])
            )
        )
    return results


def crop_scores(query_heads, key_heads, same_crop):
    raw_scores = jnp.einsum(
        "sqhd,skhd->shqk", query_heads, key_heads, preferred_element_type=jnp.float32
    )
    return jnp.where(same_crop, raw_scores * (1.0 / math.sqrt(HEAD_DIM)), far_below)


def local(
    tokens,
    skip_features,
    crop_sides,
    ln1_gain,
    ln1_bias,
    qkv_weight,
    qv_bias,
    out_weight,
    out_bias,
    ln2_gain,
    ln2_bias,
    fc1_weight,
    fc1_bias,
    fc2_weight,
    fc2_bias,
    deconv_weight,
    conv1_weight,
    conv2_weight,
    conv3_weight,
    cotangent,
):
    seq_count, row_count, model_width = tokens.shape
    channels = conv2_weight.shape[2]
    score_scale = 1.0 / math.sqrt(HEAD_DIM)
    first_row = lax.axis_index("tok") * row_count
    places = jnp.broadcast_to(
        first_row + jnp.arange(row_count, dtype=jnp.int32), (seq_count, row_count)
    )
    inside, segment, side_of, first_of = locate(crop_sides, places)
    shape_info = geometry(side_of, first_of, places)
    inside_float = inside.astype(jnp.float32)
    counts = jnp.maximum(8.0 * (crop_sides * crop_sides * crop_sides).astype(jnp.float32), 1.0)
    reaches = (key_reach + row_count - 1) // row_count
    token_values = tokens.astype(jnp.float32)
    normed_low = layer_norm(token_values, ln1_gain, ln1_bias).astype(jnp.bfloat16)
    qkv_bias = jnp.concatenate([qv_bias[0], jnp.zeros_like(qv_bias[0]), qv_bias[1]])
    projected = (
        jnp.einsum("std,de->ste", normed_low, qkv_weight, preferred_element_type=jnp.float32)
        + qkv_bias
    ).astype(jnp.bfloat16)
    queries = projected[:, :, :model_width]
    keys = projected[:, :, model_width : 2 * model_width]
    values = projected[:, :, 2 * model_width :]
    key_parts = [keys]
    value_parts = [values]
    place_parts = [places]
    moves = []
    for distance in range(1, reaches + 1):
        row_take = row_count
        for shift_by in (distance, -distance):
            if shift_by > 0:
                key_send = keys
                value_send = values
                got_first = first_row - (distance - 1) * row_count - row_take
            else:
                key_send = keys
                value_send = values
                got_first = first_row + distance * row_count
            got_keys, got_values = passed_along((key_send, value_send), "tok", shift_by)
            key_parts.append(got_keys)
            value_parts.append(got_values)
            place_parts.append(
                jnp.broadcast_to(
                    got_first + jnp.arange(row_take, dtype=jnp.int32), (seq_count, row_take)
                )
            )
            moves.append((shift_by, row_take))
    window_keys = jnp.concatenate(key_parts, axis=1).reshape(seq_count, -1, HEADS, HEAD_DIM)
    window_values = jnp.concatenate(value_parts, axis=1).reshape(seq_count, -1, HEADS, HEAD_DIM)
    key_crop = locate(crop_sides, jnp.concatenate(place_parts, axis=1))[1]
    same_crop = segment[:, None, :, None] == key_crop[:, None, None, :]
    query_heads = queries.reshape(seq_count, row_count, HEADS, HEAD_DIM)
    scores = crop_scores(query_heads, window_keys, same_crop)
    row_max = jnp.max(scores, axis=-1, keepdims=True)
    weights = jnp.exp(scores - row_max)
    totals = jnp.sum(weights, axis=-1, keepdims=True)
    log_total = row_max + jnp.log(totals)
    probs_low = (weights / totals).astype(jnp.bfloat16)
    attended = jnp.einsum(
        "shqk,skhd->sqhd", probs_low, window_values, preferred_element_type=jnp.float32
    )
    attended = attended.astype(jnp.bfloat16).reshape(seq_count, row_count, model_width)
    resid_one = (
        token_values
        + jnp.einsum("std,de->ste", attended, out_weight, preferred_element_type=jnp.float32)
        + out_bias
    )
    normed_two = layer_norm(resid_one, ln2_gain, ln2_bias).astype(jnp.bfloat16)
    pre_act = (
        jnp.einsum("std,df->stf", normed_two, fc1_weight, preferred_element_type=jnp.float32)
        + fc1_bias
    )
    act_low = jax.nn.gelu(pre_act, approximate=False).astype(jnp.bfloat16)
    resid_two = (
        resid_one
        + jnp.einsum("stf,fd->std", act_low, fc2_weight, preferred_element_type=jnp.float32)
        + fc2_bias
    )
    resid_low = resid_two.astype(jnp.bfloat16)
    upsampled = jnp.einsum(
        "std,de->ste", resid_low, deconv_weight, preferred_element_type=jnp.float32
    )
    upsampled = upsampled.astype(jnp.bfloat16).reshape(seq_count, row_count, 2, 2, 2, channels)
    joined = jnp.concatenate(
        [upsampled, skip_features.reshape(seq_count, row_count, 2, 2, 2, channels)], axis=-1
    )
    joined_pad = with_rims(joined)
    first_conv = conv_forward(joined_pad, conv1_weight, shape_info, row_count)
    side_conv = jnp.einsum(
        "stxyzc,cd->stxyzd", joined, conv3_weight, preferred_element_type=jnp.float32
    )
    normed_pair, scale_pair = norm_forward([first_conv, side_conv], inside_float, counts, reaches)
    first_norm, side_norm = normed_pair
    hidden_low = jax.nn.silu(first_norm).astype(jnp.bfloat16)
    hidden_pad = with_rims(hidden_low)
    second_conv = conv_forward(hidden_pad, conv2_weight, shape_info, row_count)
    normed_last, scale_last = norm_forward([second_conv], inside_float, counts, reaches)
    second_norm = normed_last[0]
    summed = second_norm + side_norm
    section_out = (
        jax.nn.silu(summed).astype(jnp.bfloat16).reshape(seq_count, row_count, 8, channels)
    )
    grad_out = cotangent.astype(jnp.float32).reshape(seq_count, row_count, 2, 2, 2, channels)
    silu_pull = jax.vjp(jax.nn.silu, summed)[1]
    grad_sum = silu_pull(grad_out)[0]
    second_grad, side_grad = norm_backward(
        [grad_sum, grad_sum],
        [second_norm, side_norm],
        [scale_last[0], scale_pair[1]],
        inside_float,
        counts,
        reaches,
    )
    second_low = second_grad.astype(jnp.bfloat16)
    side_low = side_grad.astype(jnp.bfloat16)
    hidden_pad_grad, conv2_grad = conv_backward(hidden_pad, conv2_weight, shape_info, second_low)
    hidden_grad = fold_rims(hidden_pad_grad)
    first_pull = jax.vjp(jax.nn.silu, first_norm)[1]
    first_norm_grad = first_pull(hidden_grad)[0]
    first_grad = norm_backward(
        [first_norm_grad], [first_norm], [scale_pair[0]], inside_float, counts, reaches
    )[0]
    first_low = first_grad.astype(jnp.bfloat16)
    joined_pad_grad, conv1_grad = conv_backward(joined_pad, conv1_weight, shape_info, first_low)
    joined_grad = fold_rims(joined_pad_grad) + jnp.einsum(
        "stxyzd,cd->stxyzc", side_low, conv3_weight, preferred_element_type=jnp.float32
    )
    conv3_grad = jnp.einsum(
        "stxyzc,stxyzd->cd", joined, side_low, preferred_element_type=jnp.float32
    )
    skip_grad = joined_grad[..., channels:].reshape(seq_count, row_count, 8, channels)
    up_grad = (
        joined_grad[..., :channels].reshape(seq_count, row_count, 8 * channels).astype(jnp.bfloat16)
    )
    deconv_grad = jnp.einsum("std,ste->de", resid_low, up_grad, preferred_element_type=jnp.float32)
    resid_two_grad = jnp.einsum(
        "ste,de->std", up_grad, deconv_weight, preferred_element_type=jnp.float32
    )
    branch_low = resid_two_grad.astype(jnp.bfloat16)
    fc2_bias_grad = jnp.sum(branch_low.astype(jnp.float32), axis=(0, 1))
    fc2_grad = jnp.einsum("stf,std->fd", act_low, branch_low, preferred_element_type=jnp.float32)
    act_grad = jnp.einsum("std,fd->stf", branch_low, fc2_weight, preferred_element_type=jnp.float32)
    gelu_pull = jax.vjp(partial(jax.nn.gelu, approximate=False), pre_act)[1]
    pre_low = gelu_pull(act_grad)[0].astype(jnp.bfloat16)
    fc1_bias_grad = jnp.sum(pre_low.astype(jnp.float32), axis=(0, 1))
    fc1_grad = jnp.einsum("std,stf->df", normed_two, pre_low, preferred_element_type=jnp.float32)
    normed_two_grad = jnp.einsum(
        "stf,df->std", pre_low, fc1_weight, preferred_element_type=jnp.float32
    )
    second_ln_pull = jax.vjp(layer_norm, resid_one, ln2_gain, ln2_bias)[1]
    resid_part, ln2_gain_grad, ln2_bias_grad = second_ln_pull(normed_two_grad)
    resid_one_grad = resid_two_grad + resid_part
    mixed_low = resid_one_grad.astype(jnp.bfloat16)
    out_bias_grad = jnp.sum(mixed_low.astype(jnp.float32), axis=(0, 1))
    out_grad = jnp.einsum("std,ste->de", attended, mixed_low, preferred_element_type=jnp.float32)
    attended_grad = jnp.einsum(
        "ste,de->std", mixed_low, out_weight, preferred_element_type=jnp.float32
    )
    attended_grad = attended_grad.astype(jnp.bfloat16).reshape(
        seq_count, row_count, HEADS, HEAD_DIM
    )
    scores_again = crop_scores(query_heads, window_keys, same_crop)
    attn_probs = jnp.exp(scores_again - log_total)
    probs_again = attn_probs.astype(jnp.bfloat16)
    probs_grad = jnp.einsum(
        "sqhd,skhd->shqk", attended_grad, window_values, preferred_element_type=jnp.float32
    )
    row_inner = jnp.sum(attn_probs * probs_grad, axis=-1, keepdims=True)
    score_low = (attn_probs * (probs_grad - row_inner)).astype(jnp.bfloat16)
    query_grad = (
        jnp.einsum("shqk,skhd->sqhd", score_low, window_keys, preferred_element_type=jnp.float32)
        * score_scale
    )
    key_grad = (
        jnp.einsum("shqk,sqhd->skhd", score_low, query_heads, preferred_element_type=jnp.float32)
        * score_scale
    )
    value_grad = jnp.einsum(
        "shqk,sqhd->skhd", probs_again, attended_grad, preferred_element_type=jnp.float32
    )
    key_grad = key_grad.reshape(seq_count, -1, model_width)
    value_grad = value_grad.reshape(seq_count, -1, model_width)
    key_own = key_grad[:, :row_count]
    value_own = value_grad[:, :row_count]
    cursor = row_count
    for shift_by, row_take in moves:
        key_piece = key_grad[:, cursor : cursor + row_take]
        value_piece = value_grad[:, cursor : cursor + row_take]
        cursor = cursor + row_take
        back_keys, back_values = (
            passed_along(key_piece.astype(jnp.bfloat16), "tok", -shift_by).astype(key_piece.dtype),
            passed_along(value_piece.astype(jnp.bfloat16), "tok", -shift_by).astype(
                value_piece.dtype
            ),
        )
        if shift_by > 0:
            key_own = key_own.at[:, row_count - row_take :].add(back_keys)
            value_own = value_own.at[:, row_count - row_take :].add(back_values)
        else:
            key_own = key_own.at[:, :row_take].add(back_keys)
            value_own = value_own.at[:, :row_take].add(back_values)
    qkv_grad_low = jnp.concatenate(
        [query_grad.reshape(seq_count, row_count, model_width), key_own, value_own], axis=-1
    ).astype(jnp.bfloat16)
    qkv_grad = jnp.einsum(
        "std,ste->de", normed_low, qkv_grad_low, preferred_element_type=jnp.float32
    )
    column_sums = jnp.sum(qkv_grad_low.astype(jnp.float32), axis=(0, 1))
    qv_bias_grad = jnp.stack([column_sums[:model_width], column_sums[2 * model_width :]])
    normed_one_grad = jnp.einsum(
        "ste,de->std", qkv_grad_low, qkv_weight, preferred_element_type=jnp.float32
    )
    first_ln_pull = jax.vjp(layer_norm, token_values, ln1_gain, ln1_bias)[1]
    token_part, ln1_gain_grad, ln1_bias_grad = first_ln_pull(normed_one_grad)
    token_grad = resid_one_grad + token_part
    weight_shares = (
        lax.psum_scatter(
            ln1_gain_grad.astype(jnp.bfloat16), "tok", scatter_dimension=0, tiled=True
        ).astype(jnp.float32),
        lax.psum_scatter(
            ln1_bias_grad.astype(jnp.bfloat16), "tok", scatter_dimension=0, tiled=True
        ).astype(jnp.float32),
        lax.psum_scatter(
            qkv_grad.astype(jnp.bfloat16), "tok", scatter_dimension=0, tiled=True
        ).astype(jnp.float32),
        lax.psum_scatter(
            qv_bias_grad.astype(jnp.bfloat16), "tok", scatter_dimension=1, tiled=True
        ).astype(jnp.float32),
        lax.psum_scatter(
            out_grad.astype(jnp.bfloat16), "tok", scatter_dimension=0, tiled=True
        ).astype(jnp.float32),
        lax.psum_scatter(
            out_bias_grad.astype(jnp.bfloat16), "tok", scatter_dimension=0, tiled=True
        ).astype(jnp.float32),
        lax.psum_scatter(
            ln2_gain_grad.astype(jnp.bfloat16), "tok", scatter_dimension=0, tiled=True
        ).astype(jnp.float32),
        lax.psum_scatter(
            ln2_bias_grad.astype(jnp.bfloat16), "tok", scatter_dimension=0, tiled=True
        ).astype(jnp.float32),
        lax.psum_scatter(
            fc1_grad.astype(jnp.bfloat16), "tok", scatter_dimension=0, tiled=True
        ).astype(jnp.float32),
        lax.psum_scatter(
            fc1_bias_grad.astype(jnp.bfloat16), "tok", scatter_dimension=0, tiled=True
        ).astype(jnp.float32),
        lax.psum_scatter(
            fc2_grad.astype(jnp.bfloat16), "tok", scatter_dimension=0, tiled=True
        ).astype(jnp.float32),
        lax.psum_scatter(
            fc2_bias_grad.astype(jnp.bfloat16), "tok", scatter_dimension=0, tiled=True
        ).astype(jnp.float32),
        lax.psum_scatter(
            deconv_grad.astype(jnp.bfloat16), "tok", scatter_dimension=0, tiled=True
        ).astype(jnp.float32),
        lax.psum_scatter(
            conv1_grad.astype(jnp.bfloat16), "tok", scatter_dimension=2, tiled=True
        ).astype(jnp.float32),
        lax.psum_scatter(
            conv2_grad.astype(jnp.bfloat16), "tok", scatter_dimension=2, tiled=True
        ).astype(jnp.float32),
        lax.psum_scatter(
            conv3_grad.astype(jnp.bfloat16), "tok", scatter_dimension=1, tiled=True
        ).astype(jnp.float32),
    )
    finished = (
        lax.psum(weight_shares[0].astype(jnp.bfloat16), "seq").astype(jnp.float32),
        lax.psum(weight_shares[1].astype(jnp.bfloat16), "seq").astype(jnp.float32),
        lax.psum(weight_shares[2].astype(jnp.bfloat16), "seq").astype(jnp.float32),
        lax.psum(weight_shares[3].astype(jnp.bfloat16), "seq").astype(jnp.float32),
        lax.psum(weight_shares[4].astype(jnp.bfloat16), "seq").astype(jnp.float32),
        lax.psum(weight_shares[5].astype(jnp.bfloat16), "seq").astype(jnp.float32),
        lax.psum(weight_shares[6].astype(jnp.bfloat16), "seq").astype(jnp.float32),
        lax.psum(weight_shares[7].astype(jnp.bfloat16), "seq").astype(jnp.float32),
        lax.psum(weight_shares[8].astype(jnp.bfloat16), "seq").astype(jnp.float32),
        lax.psum(weight_shares[9].astype(jnp.bfloat16), "seq").astype(jnp.float32),
        lax.psum(weight_shares[10].astype(jnp.bfloat16), "seq").astype(jnp.float32),
        lax.psum(weight_shares[11].astype(jnp.bfloat16), "seq").astype(jnp.float32),
        lax.psum(weight_shares[12].astype(jnp.bfloat16), "seq").astype(jnp.float32),
        lax.psum(weight_shares[13].astype(jnp.bfloat16), "seq").astype(jnp.float32),
        lax.psum(weight_shares[14].astype(jnp.bfloat16), "seq").astype(jnp.float32),
        lax.psum(weight_shares[15].astype(jnp.bfloat16), "seq").astype(jnp.float32),
    )
    return (
        section_out,
        token_grad,
        skip_grad,
        finished[0],
        finished[1],
        finished[2],
        finished[3],
        finished[4],
        finished[5],
        finished[6],
        finished[7],
        finished[8],
        finished[9],
        finished[10],
        finished[11],
        finished[12],
        finished[13],
        finished[14],
        finished[15],
    )


def solution(mesh):
    in_specs = (
        P("seq", "tok", None),
        P("seq", "tok", None, None),
        P("seq", None),
        P(),
        P(),
        P(),
        P(),
        P(),
        P(),
        P(),
        P(),
        P(),
        P(),
        P(),
        P(),
        P(),
        P(),
        P(),
        P(),
        P("seq", "tok", None, None),
    )
    out_specs = (
        P("seq", "tok", None, None),
        P("seq", "tok", None),
        P("seq", "tok", None, None),
        P("tok"),
        P("tok"),
        P("tok", None),
        P(None, "tok"),
        P("tok", None),
        P("tok"),
        P("tok"),
        P("tok"),
        P("tok", None),
        P("tok"),
        P("tok", None),
        P("tok"),
        P("tok", None),
        P(None, None, "tok"),
        P(None, None, "tok"),
        P(None, "tok"),
    )
    return jax.shard_map(local, mesh=mesh, in_specs=in_specs, out_specs=out_specs, check_vma=False)
```

profile of v0, /device:TPU:30, one launch (start us, length us, event | category | flops | bytes accessed | tf_op | source)
XLA Modules:
  0.0 4426.2 jit_solution(6044193407350746402)
XLA Ops:
  252.6 23.2 multiply_convert_fusion.1
  309.7 50.1 %fusion.898 = (bf16[3,256,2,2,2,256]{5,1,0,4,3,2:T(8,128)(2,1)}, bf16[3,256,2,2,2,256]{5,1,0,4,3,2:T(8,128)(2,1)}, bf16[3,256,2,2,2,256]{5,1,0,4,3,2:T(8,128)(2,...) fusion(bf16[3,299,2,2,2,256]{5,1,0,4,3,2:T(8,128)(2,1)} %get-tu, ...), kind=kLoop, calls=%fused_computation.1651 | loop fusion | bytes 119537664 | tf_op jit(solution)/shard_map/slice | solution.py:145
  359.8 30.5 fusion.897
  390.3 49.5 %fusion.896 = (bf16[3,256,2,2,2,256]{5,1,0,4,3,2:T(8,128)(2,1)}, bf16[3,256,2,2,2,256]{5,1,0,4,3,2:T(8,128)(2,1)}, bf16[3,256,2,2,2,256]{5,1,0,4,3,2:T(8,128)(2,...) fusion(bf16[3,299,2,2,2,256]{5,1,0,4,3,2:T(8,128)(2,1)} %get-tu, ...), kind=kLoop, calls=%fused_computation.1649 | loop fusion | bytes 119537664 | tf_op jit(solution)/shard_map/slice | solution.py:145
  696.9 19.8 scatter-add.684
  720.9 19.8 scatter-add.685
  748.9 19.8 scatter-add.689
  772.9 19.7 scatter-add.690
  796.9 19.8 scatter-add.691
  821.2 19.7 scatter-add.694
  845.4 19.8 scatter-add.695
  921.4 20.0 scatter-add.701
  945.6 19.7 scatter-add.704
  969.6 19.8 scatter-add.705
  997.6 19.8 scatter-add.709
  1342.9 20.0 scatter-add.735
  1882.8 30.2 scatter-add.776
  1919.8 30.3 scatter-add.779
  1961.5 30.3 scatter-add.781
  2000.7 30.2 scatter-add.784
  2037.6 30.3 scatter-add.785
  2073.8 30.2 scatter-add.786
  2110.4 30.3 scatter-add.789
  2149.6 30.2 scatter-add.790
  2191.5 30.2 scatter-add.794
  2228.3 30.2 scatter-add.795
  2267.5 30.2 scatter-add.796
  2304.4 30.2 scatter-add.799
  2346.1 30.2 scatter-add.801
  2385.2 30.1 scatter-add.804
  2422.1 30.1 scatter-add.805
  2458.2 30.1 scatter-add.806
  2494.3 30.1 scatter-add.809
  2537.2 30.1 scatter-add.811
  2575.1 30.1 scatter-add.814
  2605.2 30.3 scatter-add.815
  2648.4 30.1 scatter-add.816
  2678.5 30.1 scatter-add.819
  2716.3 30.1 scatter-add.820
  2749.0 30.1 scatter-add.821
  2785.9 30.1 scatter-add.824
  2826.6 30.1 scatter-add.826
  2862.7 30.1 scatter-add.829
  2905.6 30.0 scatter-add.831
  2942.2 30.0 scatter-add.834
  2985.2 30.0 scatter-add.836
  3022.0 29.9 scatter-add.839
  3063.3 30.1 scatter-add.841
  3102.3 30.0 scatter-add.844
  3139.1 29.9 scatter-add.845
  3175.0 30.0 scatter-add.846
  3211.0 29.9 scatter-add.849
  3249.9 30.0 scatter-add.1020
  3291.7 30.0 scatter-add.1022
  3328.3 29.9 scatter-add.1023
  3367.2 30.0 scatter-add.1024
  3404.0 29.9 scatter-add.1025
  3445.4 29.9 scatter-add.1027
  3801.5 23.4 multiply_reduce_fusion
  3843.8 24.2 multiply_convert_fusion
  4209.7 52.7 %all-reduce.113 = (bf16[768]{0:T(1024)(128)(2,1)}, bf16[768]{0:T(1024)(128)(2,1)}, bf16[768]{0:T(1024)(128)(2,1)}, bf16[768]{0:T(1024)(128)(2,1)}, bf16[768]{0:T...) all-reduce(bf16[768]{0:T(1024)(128)(2,1)} %get-tuple-element.1912, ...), channel_id=2, replica_groups=mesh['seq'=2,'tok'=16] {'tok'}, use_global_device_ids=true, to_apply=%region_30.31.clone | all-reduce | flops 7680 | bytes 30720
  4277.7 25.8 reduce-scatter.26.cloned.1.call-done
  4303.5 60.5 %reduce-scatter.24.cloned.1.call-done = bf16[27,128,8]{1,0,2:T(8,128)(2,1)} async-done(((bf16[27,128,128]{1,0,2:T(8,128)(2,1)}), bf16[27,128,8]{1,0,2:T(8,128)(2,1)}) %reduce-scatter.24.cloned.1.call-update) | async-done | bytes 55312 | tf_op jit(solution)/shard_map/reduce_scatter | solution.py:577
  4383.7 25.2 all-reduce.118.cloned.1.call-done
  (1733 shorter events, 2538.5 us)
Async XLA Ops:
  7.2 4198.6 %reduce-scatter.14.cloned.1.call-start = ((), (), s32[]{:S(2)}) async-start(), calls=%async_computation.10 | async-start | bytes 1253376 | tf_op jit(solution)/shard_map/reduce_scatter | solution.py:547
  18.7 162.8 %collective-permute-start.3 = (bf16[3,256,768]{2,1,0:T(8,128)(2,1)}, bf16[3,256,768]{2,1,0:T(8,128)(2,1)}, u32[]{:S(2)}, u32[]{:S(2)}) collective-permute-start(bf16[3,256,768]{2,1,0:T(8,128)(2,1)} %get-tuple-element.2108), channel_id=1, source_target_pairs={{1,0},{2,1},{3,2},{4,3},{5,4},{6,5},{7,6},{8,7},{9,8},{10,9},{11,1... | collective-permute-start | bytes 3538952 | tf_op jit(solution)/shard_map/ppermute | solution.py:41
  20.6 160.9 %collective-permute-start.2 = (bf16[3,256,768]{2,1,0:T(8,128)(2,1)}, bf16[3,256,768]{2,1,0:T(8,128)(2,1)}, u32[]{:S(2)}, u32[]{:S(2)}) collective-permute-start(bf16[3,256,768]{2,1,0:T(8,128)(2,1)} %get-tuple-element.2108), channel_id=1, source_target_pairs={{0,1},{1,2},{2,3},{3,4},{4,5},{5,6},{6,7},{7,8},{8,9},{9,10},{10,1... | collective-permute-start | bytes 3538952 | tf_op jit(solution)/shard_map/ppermute | solution.py:41
  24.1 167.0 %collective-permute-start.1 = (bf16[3,256,768]{2,1,0:T(8,128)(2,1)}, bf16[3,256,768]{2,1,0:T(8,128)(2,1)}, u32[]{:S(2)}, u32[]{:S(2)}) collective-permute-start(bf16[3,256,768]{2,1,0:T(8,128)(2,1)} %get-tuple-element.2110), channel_id=1, source_target_pairs={{1,0},{2,1},{3,2},{4,3},{5,4},{6,5},{7,6},{8,7},{9,8},{10,9},{11,1... | collective-permute-start | bytes 3538952 | tf_op jit(solution)/shard_map/ppermute | solution.py:41
  26.2 164.9 %collective-permute-start = (bf16[3,256,768]{2,1,0:T(8,128)(2,1)}, bf16[3,256,768]{2,1,0:T(8,128)(2,1)}, u32[]{:S(2)}, u32[]{:S(2)}) collective-permute-start(bf16[3,256,768]{2,1,0:T(8,128)(2,1)} %get-tuple-element.2110), channel_id=1, source_target_pairs={{0,1},{1,2},{2,3},{3,4},{4,5},{5,6},{6,7},{7,8},{8,9},{9,10},{10,1... | collective-permute-start | bytes 3538952 | tf_op jit(solution)/shard_map/ppermute | solution.py:41
  29.4 630.6 %copy-start.213 = (s32[256]{0:T(256)}, s32[256]{0:T(256)S(1)}, u32[]{:S(2)}) copy-start(s32[256]{0:T(256)S(1)} %iota_add_fusion.2) | copy-start | bytes 3076
  29.7 630.4 %copy-start.159 = (s32[3,45]{1,0:T(4,128)}, s32[3,45]{1,0:T(4,128)S(1)}, u32[]{:S(2)}) copy-start(s32[3,45]{1,0:T(4,128)S(1)} %reduce_window_sum.12) | copy-start | bytes 1624
  29.7 630.4 %copy-start.171 = (s32[3,45]{1,0:T(4,128)}, s32[3,45]{1,0:T(4,128)S(1)}, u32[]{:S(2)}) copy-start(s32[3,45]{1,0:T(4,128)S(1)} %fusion.841) | copy-start | bytes 1624
  56.2 121.4 %copy-start.221 = (pred[3,256]{1,0:T(4,128)(4,1)}, pred[3,256]{1,0:T(4,128)(4,1)S(1)}, u32[]{:S(2)}) copy-start(pred[3,256]{1,0:T(4,128)(4,1)S(1)} %get-tuple-element.1965) | copy-start | bytes 2308
  214.9 30.9 slice-start.3
  243.5 32.3 slice-start.1
  244.8 30.9 copy-start.40
  290.1 14.8 collective-permute-start.5
  292.4 12.5 collective-permute-start.4
  390.3 49.6 %copy-start.222 = (pred[3,256]{1,0:T(4,128)(4,1)S(1)}, pred[3,256]{1,0:T(4,128)(4,1)}, u32[]{:S(2)}) copy-start(pred[3,256]{1,0:T(4,128)(4,1)} %copy-done.221) | copy-start | bytes 2308
  499.7 6.5 collective-permute-start.7
  503.5 6.5 collective-permute-start.6
  505.5 152.7 %copy-start.230 = (f32[3,45]{1,0:T(4,128)}, f32[3,45]{1,0:T(4,128)S(1)}, u32[]{:S(2)}) copy-start(f32[3,45]{1,0:T(4,128)S(1)} %multiply_maximum_fusion) | copy-start | bytes 1624
  512.2 110.2 %copy-start.6 = (bf16[3,256,2,2,2,128]{5,1,0,4,3,2:T(8,128)(2,1)}, bf16[3,256,2,2,2,128]{5,1,0,4,3,2:T(8,128)(2,1)S(1)}, u32[]{:S(2)}) copy-start(bf16[3,256,2,2,2,128]{5,1,0,4,3,2:T(8,128)(2,1)S(1)} %multiply_convert_fusion.6) | copy-start | bytes 4718596
  512.3 19.6 collective-permute-start.8
  527.8 22.3 collective-permute-start.9
  634.3 4.9 collective-permute-start.11
  636.6 6.6 collective-permute-start.10
  648.9 5.1 collective-permute-start.13
  650.8 7.4 collective-permute-start.12
  653.9 30.6 copy-start.425
  1743.4 8.5 collective-permute-start.15
  1745.5 9.1 collective-permute-start.14
  1772.0 5.0 collective-permute-start.17
  1774.0 6.5 collective-permute-start.16
  1783.7 86.0 %copy-start.5 = (bf16[3,256,2,2,2,128]{5,1,0,4,3,2:T(8,128)(2,1)}, bf16[3,256,2,2,2,128]{5,1,0,4,3,2:T(8,128)(2,1)S(1)}, u32[]{:S(2)}) copy-start(bf16[3,256,2,2,2,128]{5,1,0,4,3,2:T(8,128)(2,1)S(1)} %multiply_convert_fusion.3) | copy-start | bytes 4718596
  1882.8 30.2 copy-start.380
  1919.8 30.3 copy-start.418
  1961.5 32.9 copy-start.382
  2037.6 30.3 copy-start.307
  2073.8 30.2 copy-start.305
  2110.4 32.9 copy-start.378
  2149.6 30.2 copy-start.396
  2228.3 32.9 copy-start.374
  2304.4 30.3 copy-start.412
  2346.1 32.9 copy-start.372
  2494.3 31.6 copy-start.368
  2605.2 30.3 copy-start.454
  2605.2 30.3 copy-start.456
  2862.7 31.5 copy-start.362
  3063.3 32.7 copy-start.390
  3211.0 32.6 copy-start.388
  3328.3 32.5 copy-start.386
  3572.2 16.3 collective-permute-start.18
  3575.7 13.8 collective-permute-start.19
  3650.4 555.5 %reduce-scatter.22.cloned.1.call-start = ((), (), s32[]{:S(2)}) async-start(), calls=%async_computation.14 | async-start | bytes 2228224 | tf_op jit(solution)/shard_map/reduce_scatter | solution.py:574
  3779.2 426.6 %reduce-scatter.20.cloned.1.call-start = ((), (), s32[]{:S(2)}) async-start(), calls=%async_computation.13 | async-start | bytes 1671168 | tf_op jit(solution)/shard_map/reduce_scatter | solution.py:571
  3837.9 79.1 %collective-permute-start.22 = (bf16[3,256,768]{2,1,0:T(8,128)(2,1)}, bf16[3,256,768]{2,1,0:T(8,128)(2,1)}, u32[]{:S(2)}, u32[]{:S(2)}) collective-permute-start(bf16[3,256,768]{2,1,0:T(8,128)(2,1)} %get-tuple-element.2106), channel_id=1, source_target_pairs={{1,0},{2,1},{3,2},{4,3},{5,4},{6,5},{7,6},{8,7},{9,8},{10,9},{11,1... | collective-permute-start | bytes 3538952 | tf_op jit(solution)/shard_map/ppermute | solution.py:41
  3841.8 75.2 %collective-permute-start.23 = (bf16[3,256,768]{2,1,0:T(8,128)(2,1)}, bf16[3,256,768]{2,1,0:T(8,128)(2,1)}, u32[]{:S(2)}, u32[]{:S(2)}) collective-permute-start(bf16[3,256,768]{2,1,0:T(8,128)(2,1)} %get-tuple-element.2107), channel_id=1, source_target_pairs={{0,1},{1,2},{2,3},{3,4},{4,5},{5,6},{6,7},{7,8},{8,9},{9,10},{10,1... | collective-permute-start | bytes 3538952 | tf_op jit(solution)/shard_map/ppermute | solution.py:41
  3897.5 30.3 collective-permute-start.20
  3901.2 26.7 collective-permute-start.21
  3903.1 302.8 %reduce-scatter.12.cloned.1.call-start = ((), (), s32[]{:S(2)}) async-start(), calls=%async_computation.9 | async-start | bytes 3760128 | tf_op jit(solution)/shard_map/reduce_scatter | solution.py:541
  3937.3 268.7 %reduce-scatter.18.cloned.1.call-start = ((), (), s32[]{:S(2)}) async-start(), calls=%async_computation.12 | async-start | bytes 5013504 | tf_op jit(solution)/shard_map/reduce_scatter | solution.py:565
  3946.8 259.2 %reduce-scatter.16.cloned.1.call-start = ((), (), s32[]{:S(2)}) async-start(), calls=%async_computation.11 | async-start | bytes 5013504 | tf_op jit(solution)/shard_map/reduce_scatter | solution.py:559
  3956.3 320.6 %reduce-scatter.28.cloned.1.call-start = ((), (), s32[]{:S(2)}) async-start(), calls=%async_computation.17 | async-start | bytes 208896
  4179.5 124.1 %reduce-scatter.26.cloned.1.call-start = ((), (), s32[]{:S(2)}) async-start(), calls=%async_computation.16 | async-start | bytes 69632 | tf_op jit(solution)/shard_map/reduce_scatter | solution.py:580
  4183.0 181.0 %reduce-scatter.24.cloned.1.call-start = ((), (), s32[]{:S(2)}) async-start(), calls=%async_computation.15 | async-start | bytes 1114112 | tf_op jit(solution)/shard_map/reduce_scatter | solution.py:577
  4189.8 219.2 %all-reduce.118.cloned.1.call-start = ((), (), s32[]{:S(2)}) async-start(), calls=%async_computation.18 | async-start | bytes 2228224 | tf_op jit(solution)/shard_map/psum | solution.py:598
  4205.8 66.2 %copy-start.244 = (f32[3,256]{1,0:T(4,128)S(1)}, f32[3,256]{1,0:T(4,128)}, u32[]{:S(2)}) copy-start(f32[3,256]{1,0:T(4,128)} %copy-done.243) | copy-start | bytes 9220
  (445 other events, 3789.7 us)
Sparse Core Ops, SparseCore 0:
  3650.5 58.9 reduce-scatter.13
  3779.3 62.3 reduce-scatter.21
  3903.2 60.7 reduce-scatter.19
  3967.7 66.8 reduce-scatter.11
  4038.3 74.3 reduce-scatter.17
  4116.9 74.5 reduce-scatter.15
  4195.6 52.9 reduce-scatter.27
  4252.5 50.9 reduce-scatter.25
  4307.6 56.4 reduce-scatter.23
  4366.5 42.3 all-reduce.117
where the time goes:
time: 4510 us; the launch traced here: 4430 us
  local copies, waits for them, and re-layouts  2730 us (61%)
  other arithmetic  889 us (20%)
  matrix products  517 us (11%)
  waiting for transfers between devices  145 us (3%)
  blocking collectives  62.2 us (1%)
  starting transfers between devices  62 us (1%)
    scatter-add x44, local copies, waits for them, and re-layouts, unshift(): grad_pad.at[:, halo_rows + far_step:halo_rows + far_step + length]  1100 us
    scatter-add x42, local copies, waits for them, and re-layouts, unshift(): grad_pad.at[:, halo_rows + near_step:halo_rows + near_step + length]  997 us
    add x42, other arithmetic, unshift(): grad_pad.at[:, halo_rows + far_step:halo_rows + far_step + length]  225 us
    add x34, other arithmetic, unshift(): grad_pad.at[:, halo_rows + near_step:halo_rows + near_step + length]  172 us
    scatter-add x38, other arithmetic, conv_backward(): grad_kernel.at[tap_index.reshape(-1)]  153 us
    dot_general x54, matrix products, conv_backward(): jnp.einsum('stxyzc,stXYZd->xyzXYZcd', source, target, preferred_element_t...  141 us
    slice x4, local copies, waits for them, and re-layouts, shifted(): lax.slice_in_dim(padded, halo_rows + far_step, halo_rows + far_step + len...  110 us
    gather x38, local copies, waits for them, and re-layouts, conv_forward(): kernel_block = kernel[tap_table(offset)]  108 us
  transfers between devices with their start and end apart: 34, of which 12 were waited for; matrix products, arithmetic and copies ran while one was open for 17% of the time, Pallas kernels for 0%

commit v1 on v0

--- a/solution.py
+++ b/solution.py
@@ -5,6 +5,8 @@
 import jax.numpy as jnp
 import numpy as np
 from jax import lax
+from jax.experimental import pallas as pl
+from jax.experimental.pallas import tpu as pltpu
 from jax.sharding import PartitionSpec as P
 
 HEADS = 12
@@ -22,19 +24,6 @@
 out_part = {-1: (0, 1), 0: (0, 2), 1: (1, 2)}
 
 
-def padded_2(shard, sides, width):
-    for axis, dim in sides:
-        count, length = (lax.axis_size(axis), shard.shape[dim])
-        up = [(i, (i + 1) % count) for i in range(count - 1)]
-        down = [(j, i) for i, j in up]
-        last = lax.slice_in_dim(shard, length - width, length, axis=dim)
-        leading = lax.slice_in_dim(shard, 0, width, axis=dim)
-        before = lax.ppermute(last, axis, up)
-        after = lax.ppermute(leading, axis, down)
-        shard = jnp.concatenate([before, shard, after], axis=dim)
-    return shard
-
-
 def passed_along(block, axis, distance):
     devices = range(lax.axis_size(axis))
     route = [(i - distance, i) for i in devices if i - distance in devices]
@@ -49,49 +38,6 @@
         for step_y in step_values
         for step_z in step_values
     ]
-
-
-def index_tuples(table_shape):
-    tuples_out = [()]
-    for extent in table_shape:
-        tuples_out = [prefix + (position,) for prefix in tuples_out for position in range(extent)]
-    return tuples_out
-
-
-def tap_table(offset):
-    in_lists = [
-        list(range(in_part[offset_entry][0], in_part[offset_entry][1])) for offset_entry in offset
-    ]
-    out_lists = [
-        list(range(out_part[offset_entry][0], out_part[offset_entry][1])) for offset_entry in offset
-    ]
-    table_shape = tuple((len(members) for members in in_lists)) + tuple(
-        (len(members) for members in out_lists)
-    )
-    tap_index = np.zeros(table_shape, dtype=np.int32)
-    for entry_index in index_tuples(table_shape):
-        flat_tap = 0
-        for axis_id in range(3):
-            source_sub = in_lists[axis_id][entry_index[axis_id]]
-            target_sub = out_lists[axis_id][entry_index[3 + axis_id]]
-            flat_tap = flat_tap * 3 + 2 * offset[axis_id] + source_sub - target_sub + 1
-        tap_index[entry_index] = flat_tap
-    return tap_index
-
-
-def sub_cut(array_in, parts, offset):
-    begins = [parts[offset_entry][0] for offset_entry in offset]
-    finish = [parts[offset_entry][1] for offset_entry in offset]
-    return array_in[:, :, begins[0] : finish[0], begins[1] : finish[1], begins[2] : finish[2]]
-
-
-def sub_pad(array_in, parts, offset):
-    widths = (
-        [(0, 0), (0, 0)]
-        + [(parts[offset_entry][0], 2 - parts[offset_entry][1]) for offset_entry in offset]
-        + [(0, 0)]
-    )
-    return jnp.pad(array_in, widths)
 
 
 def crop_bounds(sides):
@@ -137,162 +83,555 @@
     return inside_crop & (depth_pos + offset[2] >= 0) & (depth_pos + offset[2] < side_of)
 
 
-def shifted(padded, offset, shape_info, length):
-    near_step, far_step = step_sizes(offset)
-    small_view = lax.slice_in_dim(
-        padded, halo_rows + near_step, halo_rows + near_step + length, axis=1
-    )
-    big_view = lax.slice_in_dim(padded, halo_rows + far_step, halo_rows + far_step + length, axis=1)
-    is_big = shape_info[4][:, :, None, None, None, None]
-    inside_crop = in_crop(shape_info, offset)[:, :, None, None, None, None]
-    picked = jnp.where(is_big, big_view, small_view)
-    return jnp.where(inside_crop, picked, jnp.zeros((), padded.dtype))
-
-
-def conv_forward(padded, kernel, shape_info, length):
-    result_sum = 0.0
-    for offset in all_offsets():
-        source = sub_cut(shifted(padded, offset, shape_info, length), in_part, offset)
-        kernel_block = kernel[tap_table(offset)]
-        term_part = jnp.einsum(
-            "stxyzc,xyzXYZcd->stXYZd", source, kernel_block, preferred_element_type=jnp.float32
-        )
-        result_sum = result_sum + sub_pad(term_part, out_part, offset)
-    return result_sum
-
-
-def unshift(grad_pad, grad_source, offset, shape_info, length):
-    near_step, far_step = step_sizes(offset)
-    inside_crop = in_crop(shape_info, offset)[:, :, None, None, None, None]
-    is_big = shape_info[4][:, :, None, None, None, None]
-    grad_pad = grad_pad.at[:, halo_rows + near_step : halo_rows + near_step + length].add(
-        jnp.where(inside_crop & ~is_big, grad_source, 0.0)
-    )
-    return grad_pad.at[:, halo_rows + far_step : halo_rows + far_step + length].add(
-        jnp.where(inside_crop & is_big, grad_source, 0.0)
-    )
-
-
-def conv_backward(padded, kernel, shape_info, grad_out):
-    length = grad_out.shape[1]
-    grad_pad = jnp.zeros(padded.shape, jnp.float32)
-    grad_kernel = jnp.zeros(kernel.shape, jnp.float32)
-    for offset in all_offsets():
-        tap_index = tap_table(offset)
-        source = sub_cut(shifted(padded, offset, shape_info, length), in_part, offset)
-        target = sub_cut(grad_out, out_part, offset)
-        kernel_block = kernel[tap_index]
-        grad_block = jnp.einsum(
-            "stxyzc,stXYZd->xyzXYZcd", source, target, preferred_element_type=jnp.float32
-        )
-        grad_kernel = grad_kernel.at[tap_index.reshape(-1)].add(
-            grad_block.reshape(-1, kernel.shape[1], kernel.shape[2])
-        )
-        grad_source = jnp.einsum(
-            "stXYZd,xyzXYZcd->stxyzc", target, kernel_block, preferred_element_type=jnp.float32
-        )
-        grad_pad = unshift(
-            grad_pad, sub_pad(grad_source, in_part, offset), offset, shape_info, length
-        )
-    return (grad_pad, grad_kernel)
-
-
-def with_rims(field):
-    return padded_2(field, (("tok", 1),), halo_rows)
-
-
-def fold_rims(grad_pad):
-    edges = jnp.concatenate(
-        [grad_pad[:, :halo_rows], grad_pad[:, grad_pad.shape[1] - halo_rows :]], axis=1
-    )
-    widened = padded_2(edges.astype(jnp.bfloat16), (("tok", 1),), halo_rows).astype(edges.dtype)
-    owned = grad_pad[:, halo_rows : grad_pad.shape[1] - halo_rows]
-    owned = owned.at[:, :halo_rows].add(widened[:, :halo_rows])
-    return owned.at[:, owned.shape[1] - halo_rows :].add(widened[:, 3 * halo_rows :])
-
-
-def chain_total(own, reaches, passer):
-    total = own
-    for direction in (1, -1):
-        carried = jnp.zeros_like(own)
-        for step_number in range(reaches):
-            carried = passer(own + carried, direction)
-        total = total + carried
-    return total
-
-
 def layer_norm(values_in, gain, shift):
     centered = values_in - jnp.mean(values_in, axis=-1, keepdims=True)
     variance = jnp.mean(centered * centered, axis=-1, keepdims=True)
     return centered * lax.rsqrt(variance + norm_eps) * gain + shift
 
 
-def crop_totals(inside_float, field):
-    return jnp.einsum(
-        "stk,stc->skc", inside_float, jnp.sum(field, axis=(2, 3, 4)), precision=highest
-    )
-
-
-def spread(inside_float, crop_values):
-    return jnp.einsum("stk,skc->stc", inside_float, crop_values, precision=highest)[
-        :, :, None, None, None, :
-    ]
-
-
-def norm_forward(fields, inside_float, counts, reaches):
-    sums = jnp.stack([crop_totals(inside_float, field) for field in fields])
-    squares = jnp.stack([crop_totals(inside_float, field * field) for field in fields])
-
-    def passer(partial_sums, direction):
-        return passed_along(partial_sums.astype(jnp.bfloat16), "tok", direction).astype(
-            partial_sums.dtype
-        )
-
-    both = chain_total(jnp.stack([sums, squares]), reaches, passer)
-    sums, squares = (both[0], both[1])
-    means = sums / counts[None, :, :, None]
-    scales = lax.rsqrt(squares / counts[None, :, :, None] - means * means + norm_eps)
-    normed = []
-    scale_rows = []
-    for number in range(len(fields)):
-        scale_row = spread(inside_float, scales[number])
-        normed.append((fields[number] - spread(inside_float, means[number])) * scale_row)
-        scale_rows.append(scale_row)
-    return (normed, scale_rows)
-
-
-def norm_backward(grads, normed, scale_rows, inside_float, counts, reaches):
-    firsts = jnp.stack([crop_totals(inside_float, grads[number]) for number in range(len(grads))])
-    seconds = jnp.stack(
-        [crop_totals(inside_float, grads[number] * normed[number]) for number in range(len(grads))]
-    )
-
-    def passer(partial_sums, direction):
-        return passed_along(partial_sums.astype(jnp.bfloat16), "tok", direction).astype(
-            partial_sums.dtype
-        )
-
-    both = chain_total(jnp.stack([firsts, seconds]), reaches, passer)
-    firsts = both[0] / counts[None, :, :, None]
-    seconds = both[1] / counts[None, :, :, None]
-    results = []
-    for number in range(len(grads)):
-        results.append(
-            scale_rows[number]
-            * (
-                grads[number]
-                - spread(inside_float, firsts[number])
-                - normed[number] * spread(inside_float, seconds[number])
-            )
-        )
-    return results
-
-
 def crop_scores(query_heads, key_heads, same_crop):
     raw_scores = jnp.einsum(
         "sqhd,skhd->shqk", query_heads, key_heads, preferred_element_type=jnp.float32
     )
     return jnp.where(same_crop, raw_scores * (1.0 / math.sqrt(HEAD_DIM)), far_below)
+
+
+EDGE = 48
+WINDOW = 256
+TILE = 128
+CROP_ROWS = 48
+SUBS = 8
+VMEM_LIMIT = 60 * 1024 * 1024
+lowest_step = {-1: -43, 0: -7, 1: 11}
+low_type = jnp.bfloat16
+wide = jnp.float32
+
+
+def dot(left, right):
+    return jnp.dot(left, right, preferred_element_type=wide)
+
+
+def three_terms(field):
+    first = field.astype(low_type)
+    rest = field - first.astype(wide)
+    second = rest.astype(low_type)
+    third = (rest - second.astype(wide)).astype(low_type)
+    return (first, second, third)
+
+
+def exact_dot(chosen, field):
+    first, second, third = three_terms(field)
+    return dot(chosen, first) + dot(chosen, second) + dot(chosen, third)
+
+
+def sub_lanes(number, width):
+    return slice(number * width, (number + 1) * width)
+
+
+def banded(taps):
+    begin = jnp.pad(taps, ((0, 0), (0, 0), (0, 1), (0, 0), (0, 0)))
+    later = jnp.pad(taps, ((0, 0), (0, 0), (1, 0), (0, 0), (0, 0)))
+    both = jnp.concatenate([begin, later], axis=-1)
+    return both.reshape(3, 12 * taps.shape[3], 2 * taps.shape[4])
+
+
+def forward_band(weight):
+    return banded(weight.reshape((3, 3, 3) + weight.shape[1:]))
+
+
+def backward_band(weight):
+    taps = weight.reshape((3, 3, 3) + weight.shape[1:])
+    return banded(taps[::-1, ::-1, ::-1].swapaxes(3, 4))
+
+
+def window_positions(step):
+    return {-1: ((0, 1),), 0: ((1, 0), (2, 1)), 1: ((3, 0),)}[step]
+
+
+def fill_windows(x_ref, place_ref, p_ref, rows, width):
+    tile = min(rows, TILE)
+    for base in range(0, rows, tile):
+        own = slice(base, base + tile)
+        for number, (step_x, step_y, step_z) in enumerate(all_offsets()):
+            low = (EDGE + base + lowest_step[step_x]) // 16 * 16
+            centre = (step_x, step_y, step_z) == (0, 0, 0)
+            if not centre:
+                lane = lax.broadcasted_iota(jnp.int32, (tile, WINDOW), 1) + low
+                chosen = jnp.where(lane == place_ref[0, own, number : number + 1], 1.0, 0.0)
+                chosen = chosen.astype(low_type)
+            for x_to, x_from in window_positions(step_x):
+                for y_to, y_from in window_positions(step_y):
+                    z_to, z_from = window_positions(step_z)[0]
+                    count = (2 if step_z == 0 else 1) * width
+                    to = ((x_to * 4 + y_to) * 4 + z_to) * width
+                    source = (x_from * 4 + y_from * 2 + z_from) * width
+                    if centre:
+                        got = x_ref[EDGE + base : EDGE + base + tile, source : source + count]
+                    else:
+                        got = dot(chosen, x_ref[low : low + WINDOW, source : source + count])
+                    p_ref[own, to : to + count] = got.astype(low_type)
+
+
+def window_conv(p_ref, band_ref, pair, width):
+    first, second = pair
+    total = None
+    for tap in range(3):
+        begin = ((first + tap) * 4 + second) * 4 * width
+        term = dot(p_ref[:, begin : begin + 12 * width], band_ref[tap])
+        total = term if total is None else total + term
+    return total
+
+
+def all_pairs():
+    return [(first, second) for first in range(2) for second in range(2)]
+
+
+def add_grads(left_ref, p_ref, total_ref, width, channels):
+    for tap_x in range(3):
+        for tap_y in range(3):
+            term = None
+            for number, (first, second) in enumerate(all_pairs()):
+                begin = ((first + tap_x) * 4 + second + tap_y) * 4 * channels
+                left = left_ref[number * 2 * width : (number + 1) * 2 * width, :]
+                part = dot(left, p_ref[:, begin : begin + 4 * channels])
+                term = part if term is None else term + part
+            total_ref[tap_x * 3 + tap_y] += term
+
+
+def fold_grads(total_ref, grad_ref, width, channels):
+    for tap_x in range(3):
+        for tap_y in range(3):
+            for tap_z in range(3):
+                number = tap_x * 3 + tap_y
+                here = total_ref[number, :width, sub_lanes(tap_z, channels)]
+                there = total_ref[number, width:, sub_lanes(tap_z + 1, channels)]
+                grad_ref[26 - (number * 3 + tap_z)] = here + there
+
+
+def kernel_call(body, seqs, inputs, shared, outputs, summed, scratch, flops):
+    def row_spec(shape):
+        return pl.BlockSpec((1,) + tuple(shape[1:]), lambda i: (i,) + (0,) * (len(shape) - 1))
+
+    def whole_spec(shape):
+        return pl.BlockSpec(tuple(shape), lambda i: (0,) * len(shape))
+
+    moved = sum(math.prod(a.shape) * a.dtype.itemsize for a in list(inputs) + list(shared))
+    moved += sum(math.prod(s) * jnp.dtype(t).itemsize for s, t in list(outputs) + list(summed))
+    return pl.pallas_call(
+        body,
+        grid=(seqs,),
+        in_specs=[row_spec(a.shape) for a in inputs] + [whole_spec(a.shape) for a in shared],
+        out_specs=[row_spec(s) for s, _ in outputs] + [whole_spec(s) for s, _ in summed],
+        out_shape=[jax.ShapeDtypeStruct(s, t) for s, t in list(outputs) + list(summed)],
+        scratch_shapes=scratch,
+        compiler_params=pltpu.CompilerParams(vmem_limit_bytes=VMEM_LIMIT),
+        cost_estimate=pl.CostEstimate(flops=flops, bytes_accessed=moved, transcendentals=0),
+    )(*inputs, *shared)
+
+
+def conv_scratch(rows, width):
+    return [
+        pltpu.VMEM((rows + 192, SUBS * width), low_type),
+        pltpu.VMEM((rows, 64 * width), low_type),
+    ]
+
+
+def conv_flops(seqs, rows, inner, outer):
+    return 2 * seqs * rows * (36 * 4 * inner * 2 * outer + 56 * WINDOW * inner)
+
+
+def put_edges(low_pay, high_pay, number, field, channels, rows):
+    lanes = sub_lanes(number, channels)
+    low_pay[0, :, lanes] = field[:EDGE].astype(low_type)
+    high_pay[0, :, lanes] = field[rows - EDGE :].astype(low_type)
+
+
+def put_sums(sums_ref, low_pay, high_pay, number, value, channels):
+    lanes = sub_lanes(number, channels)
+    sums_ref[0, :, lanes] = value
+    pay_lanes = sub_lanes(SUBS + number, channels)
+    low_pay[0, :, pay_lanes] = value.astype(low_type)
+    high_pay[0, :, pay_lanes] = value.astype(low_type)
+
+
+def taken_sums(sums_ref, left_pay, right_pay, number, channels):
+    lanes = sub_lanes(number, channels)
+    pay_lanes = sub_lanes(SUBS + number, channels)
+    total = sums_ref[0, :, lanes] + left_pay[0, :, pay_lanes].astype(wide)
+    return total + right_pay[0, :, pay_lanes].astype(wide)
+
+
+def mean_and_scale(total, square, inverse):
+    mean = total * inverse
+    variance = jnp.maximum(square * inverse - mean * mean, 0.0)
+    return (mean, lax.rsqrt(variance + norm_eps))
+
+
+def silu_parts(value):
+    gate = 1.0 / (1.0 + jnp.exp(-value))
+    return (value * gate, gate * (1.0 + value * (1.0 - gate)))
+
+
+def first_conv_kernel(rows, channels):
+    width = 2 * channels
+
+    def body(
+        up, up_left, up_right, skip, skip_left, skip_right, place, crop_t, band, side,
+        first_out, side_out, sums, low_pay, high_pay, x_ref, p_ref,
+    ):
+        for number in range(SUBS):
+            for half, (own, left, right) in enumerate(
+                ((up, up_left, up_right), (skip, skip_left, skip_right))
+            ):
+                to = sub_lanes(2 * number + half, channels)
+                lanes = sub_lanes(number, channels)
+                x_ref[:EDGE, to] = left[0, :, lanes]
+                x_ref[EDGE : EDGE + rows, to] = own[0, :, lanes]
+                x_ref[EDGE + rows : 2 * EDGE + rows, to] = right[0, :, lanes]
+        x_ref[2 * EDGE + rows :, :] = jnp.zeros((96, SUBS * width), low_type)
+        fill_windows(x_ref, place, p_ref, rows, width)
+        total = [jnp.zeros((rows, channels), wide) for _ in range(4)]
+        for index, pair in enumerate(all_pairs()):
+            result = window_conv(p_ref, band, pair, width)
+            first_out[0, :, sub_lanes(index, width)] = result
+            for half in range(2):
+                number = 2 * index + half
+                value = result[:, sub_lanes(half, channels)]
+                put_edges(low_pay, high_pay, number, value, channels, rows)
+                flat = dot(x_ref[EDGE : EDGE + rows, sub_lanes(number, width)], side[...])
+                side_out[0, :, sub_lanes(number, channels)] = flat
+                terms = (value, value * value, flat, flat * flat)
+                total = [have + term for have, term in zip(total, terms)]
+        for number in range(4):
+            value = exact_dot(crop_t[0], total[number])
+            put_sums(sums, low_pay, high_pay, number, value, channels)
+
+    return body
+
+
+def second_conv_kernel(rows, channels):
+    def body(
+        first, left_pay, right_pay, own_sums, inverse, owner, place, crop_t, band,
+        second_out, stats, sums, low_pay, high_pay, x_ref, p_ref,
+    ):
+        taken = [taken_sums(own_sums, left_pay, right_pay, n, channels) for n in range(4)]
+        mean, scale = mean_and_scale(taken[0], taken[1], inverse[0])
+        side_mean, side_scale = mean_and_scale(taken[2], taken[3], inverse[0])
+        for number, value in enumerate((mean, scale, side_mean, side_scale)):
+            stats[0, :, sub_lanes(number, channels)] = value
+        mean_rows = exact_dot(owner[0], mean)
+        scale_rows = exact_dot(owner[0], scale)
+        parts = (
+            (left_pay, slice(0, EDGE)),
+            (first, slice(EDGE, EDGE + rows)),
+            (right_pay, slice(EDGE + rows, 2 * EDGE + rows)),
+        )
+        for number in range(SUBS):
+            lanes = sub_lanes(number, channels)
+            for field, place_rows in parts:
+                normed = field[0, :, lanes].astype(wide) - mean_rows[place_rows]
+                normed = normed * scale_rows[place_rows]
+                x_ref[place_rows, lanes] = silu_parts(normed)[0].astype(low_type)
+        x_ref[2 * EDGE + rows :, :] = jnp.zeros((96, SUBS * channels), low_type)
+        fill_windows(x_ref, place, p_ref, rows, channels)
+        total = [jnp.zeros((rows, channels), wide) for _ in range(2)]
+        for index, pair in enumerate(all_pairs()):
+            result = window_conv(p_ref, band, pair, channels)
+            second_out[0, :, sub_lanes(index, 2 * channels)] = result
+            for half in range(2):
+                value = result[:, sub_lanes(half, channels)]
+                put_edges(low_pay, high_pay, 2 * index + half, value, channels, rows)
+                total = [total[0] + value, total[1] + value * value]
+        for number in range(2):
+            value = exact_dot(crop_t[0], total[number])
+            put_sums(sums, low_pay, high_pay, number, value, channels)
+
+    return body
+
+
+def output_kernel(rows, channels):
+    def body(
+        second, side_field, cotangent, stats, left_pay, right_pay, own_sums, inverse, owner, crop_t,
+        section, grad_out, second_stats, sums, low_pay, high_pay,
+    ):
+        taken = [taken_sums(own_sums, left_pay, right_pay, n, channels) for n in range(2)]
+        mean, scale = mean_and_scale(taken[0], taken[1], inverse[0])
+        second_stats[0, :, sub_lanes(0, channels)] = mean
+        second_stats[0, :, sub_lanes(1, channels)] = scale
+        own = owner[0, EDGE : EDGE + rows, :]
+        mean_rows = exact_dot(own, mean)
+        scale_rows = exact_dot(own, scale)
+        side_mean = exact_dot(own, stats[0, :, sub_lanes(2, channels)])
+        side_scale = exact_dot(own, stats[0, :, sub_lanes(3, channels)])
+        total = [jnp.zeros((rows, channels), wide) for _ in range(3)]
+        for number in range(SUBS):
+            lanes = sub_lanes(number, channels)
+            normed = (second[0, :, lanes] - mean_rows) * scale_rows
+            side = (side_field[0, :, lanes] - side_mean) * side_scale
+            value, slope = silu_parts(normed + side)
+            section[0, :, lanes] = value.astype(low_type)
+            grad = cotangent[0, :, lanes].astype(wide) * slope
+            grad_out[0, :, lanes] = grad
+            put_edges(low_pay, high_pay, number, grad, channels, rows)
+            terms = (grad, grad * normed, grad * side)
+            total = [have + term for have, term in zip(total, terms)]
+        for number in range(3):
+            value = exact_dot(crop_t[0], total[number])
+            put_sums(sums, low_pay, high_pay, number, value, channels)
+
+    return body
+
+
+def second_back_kernel(rows, channels, seqs):
+    def body(
+        grad, grad_left, grad_right, own_sums, second, second_left, second_right, side_field, first,
+        stats, second_stats, inverse, owner, place, crop_t, band,
+        first_grad, side_grad, sums, low_pay, high_pay, weight_grad,
+        x_ref, p_ref, left_ref, total_ref,
+    ):
+        means = [
+            taken_sums(own_sums, grad_left, grad_right, n, channels) * inverse[0] for n in range(3)
+        ]
+        mean_rows = exact_dot(owner[0], second_stats[0, :, sub_lanes(0, channels)])
+        scale_rows = exact_dot(owner[0], second_stats[0, :, sub_lanes(1, channels)])
+        lead_rows = exact_dot(owner[0], means[0])
+        slope_rows = exact_dot(owner[0], means[1])
+        parts = (
+            (grad_left, second_left, slice(0, EDGE)),
+            (grad, second, slice(EDGE, EDGE + rows)),
+            (grad_right, second_right, slice(EDGE + rows, 2 * EDGE + rows)),
+        )
+        own = slice(EDGE, EDGE + rows)
+        side_mean = exact_dot(owner[0, own, :], stats[0, :, sub_lanes(2, channels)])
+        side_scale = exact_dot(owner[0, own, :], stats[0, :, sub_lanes(3, channels)])
+        side_slope = exact_dot(owner[0, own, :], means[2])
+        first_mean = exact_dot(owner[0, own, :], stats[0, :, sub_lanes(0, channels)])
+        first_scale = exact_dot(owner[0, own, :], stats[0, :, sub_lanes(1, channels)])
+        for number in range(SUBS):
+            lanes = sub_lanes(number, channels)
+            for grad_from, field, at in parts:
+                normed = (field[0, :, lanes].astype(wide) - mean_rows[at]) * scale_rows[at]
+                pulled = grad_from[0, :, lanes].astype(wide) - lead_rows[at]
+                pulled = scale_rows[at] * (pulled - normed * slope_rows[at])
+                x_ref[at, lanes] = pulled.astype(low_type)
+            side = (side_field[0, :, lanes] - side_mean) * side_scale
+            pulled = side_scale * (grad[0, :, lanes] - lead_rows[own] - side * side_slope)
+            side_grad[0, :, lanes] = pulled.astype(low_type)
+            normed = (first[0, :, lanes] - first_mean) * first_scale
+            hidden = silu_parts(normed)[0]
+            left_ref[lanes, :] = jnp.transpose(hidden).astype(low_type)
+        x_ref[2 * EDGE + rows :, :] = jnp.zeros((96, SUBS * channels), low_type)
+        fill_windows(x_ref, place, p_ref, rows, channels)
+        total = [jnp.zeros((rows, channels), wide) for _ in range(2)]
+        for index, pair in enumerate(all_pairs()):
+            result = window_conv(p_ref, band, pair, channels)
+            for half in range(2):
+                number = 2 * index + half
+                lanes = sub_lanes(number, channels)
+                normed = (first[0, :, lanes] - first_mean) * first_scale
+                value = result[:, sub_lanes(half, channels)] * silu_parts(normed)[1]
+                first_grad[0, :, lanes] = value
+                put_edges(low_pay, high_pay, number, value, channels, rows)
+                total = [total[0] + value, total[1] + value * normed]
+        for number in range(2):
+            value = exact_dot(crop_t[0], total[number])
+            put_sums(sums, low_pay, high_pay, number, value, channels)
+
+        @pl.when(pl.program_id(0) == 0)
+        def _():
+            total_ref[...] = jnp.zeros_like(total_ref)
+
+        add_grads(left_ref, p_ref, total_ref, channels, channels)
+
+        @pl.when(pl.program_id(0) == seqs - 1)
+        def _():
+            fold_grads(total_ref, weight_grad, channels, channels)
+
+    return body
+
+
+def first_back_kernel(rows, channels, seqs):
+    width = 2 * channels
+
+    def body(
+        grad, grad_left, grad_right, own_sums, first, first_left, first_right, stats, inverse, owner,
+        place, side_grad, up, skip, band, side_weight,
+        up_grad, skip_grad, weight_grad, side_weight_grad,
+        x_ref, p_ref, left_ref, total_ref,
+    ):
+        means = [
+            taken_sums(own_sums, grad_left, grad_right, n, channels) * inverse[0] for n in range(2)
+        ]
+        mean_rows = exact_dot(owner[0], stats[0, :, sub_lanes(0, channels)])
+        scale_rows = exact_dot(owner[0], stats[0, :, sub_lanes(1, channels)])
+        lead_rows = exact_dot(owner[0], means[0])
+        slope_rows = exact_dot(owner[0], means[1])
+        parts = (
+            (grad_left, first_left, slice(0, EDGE)),
+            (grad, first, slice(EDGE, EDGE + rows)),
+            (grad_right, first_right, slice(EDGE + rows, 2 * EDGE + rows)),
+        )
+        for number in range(SUBS):
+            lanes = sub_lanes(number, channels)
+            for grad_from, field, at in parts:
+                normed = (field[0, :, lanes].astype(wide) - mean_rows[at]) * scale_rows[at]
+                pulled = grad_from[0, :, lanes].astype(wide) - lead_rows[at]
+                pulled = scale_rows[at] * (pulled - normed * slope_rows[at])
+                x_ref[at, lanes] = pulled.astype(low_type)
+            for half, field in enumerate((up, skip)):
+                turned = jnp.transpose(field[0, :, lanes].astype(wide)).astype(low_type)
+                left_ref[sub_lanes(2 * number + half, channels), :] = turned
+        x_ref[2 * EDGE + rows :, :] = jnp.zeros((96, SUBS * channels), low_type)
+        fill_windows(x_ref, place, p_ref, rows, channels)
+        for index, pair in enumerate(all_pairs()):
+            result = window_conv(p_ref, band, pair, channels)
+            for half in range(2):
+                number = 2 * index + half
+                lanes = sub_lanes(number, channels)
+                value = result[:, sub_lanes(half, width)]
+                value = value + dot(side_grad[0, :, lanes], side_weight[...])
+                up_grad[0, :, lanes] = value[:, :channels].astype(low_type)
+                skip_grad[0, :, lanes] = value[:, channels:]
+
+        @pl.when(pl.program_id(0) == 0)
+        def _():
+            total_ref[...] = jnp.zeros_like(total_ref)
+            side_weight_grad[...] = jnp.zeros_like(side_weight_grad)
+
+        for number in range(SUBS):
+            side_weight_grad[...] += dot(
+                left_ref[sub_lanes(number, width), :], side_grad[0, :, sub_lanes(number, channels)]
+            )
+        add_grads(left_ref, p_ref, total_ref, width, channels)
+
+        @pl.when(pl.program_id(0) == seqs - 1)
+        def _():
+            fold_grads(total_ref, weight_grad, width, channels)
+
+    return body
+
+
+def exchanged(low_pay, high_pay):
+    return (passed_along(high_pay, "tok", 1), passed_along(low_pay, "tok", -1))
+
+
+def with_far(sums, reaches):
+    total = sums
+    for distance in range(2, reaches + 1):
+        for shift_by in (distance, -distance):
+            total = total + passed_along(sums.astype(low_type), "tok", shift_by).astype(wide)
+    return total
+
+
+def conv_section(upsampled, skip, cotangent, weights, geometry_in, reaches):
+    conv1_weight, conv2_weight, conv3_weight = weights
+    seqs, rows, lanes = upsampled.shape
+    channels = lanes // SUBS
+    width = 2 * channels
+    place, owner, crop_t, inverse = geometry_in
+    field = ((seqs, rows, lanes), wide)
+    low_field = ((seqs, rows, lanes), low_type)
+
+    def pay(count):
+        return ((seqs, EDGE, (SUBS + count) * channels), low_type)
+
+    def table(count):
+        return ((seqs, CROP_ROWS, count * channels), wide)
+
+    skip_left, skip_right = exchanged(skip[:, :EDGE], skip[:, rows - EDGE :])
+    up_left, up_right = exchanged(upsampled[:, :EDGE], upsampled[:, rows - EDGE :])
+    first, side_field, sums, low_pay, high_pay = kernel_call(
+        first_conv_kernel(rows, channels),
+        seqs,
+        (upsampled, up_left, up_right, skip, skip_left, skip_right, place, crop_t),
+        (forward_band(conv1_weight), conv3_weight),
+        (field, field, table(4), pay(4), pay(4)),
+        (),
+        conv_scratch(rows, width),
+        conv_flops(seqs, rows, width, channels),
+    )
+    first_left, first_right = exchanged(low_pay, high_pay)
+    second, stats, sums, low_pay, high_pay = kernel_call(
+        second_conv_kernel(rows, channels),
+        seqs,
+        (first, first_left, first_right, with_far(sums, reaches), inverse, owner, place, crop_t),
+        (forward_band(conv2_weight),),
+        (field, table(4), table(2), pay(2), pay(2)),
+        (),
+        conv_scratch(rows, channels),
+        conv_flops(seqs, rows, channels, channels),
+    )
+    second_left, second_right = exchanged(low_pay, high_pay)
+    section_out, grad, second_stats, sums, low_pay, high_pay = kernel_call(
+        output_kernel(rows, channels),
+        seqs,
+        (
+            second, side_field, cotangent, stats, second_left, second_right,
+            with_far(sums, reaches), inverse, owner, crop_t,
+        ),
+        (),
+        (low_field, field, table(2), table(3), pay(3), pay(3)),
+        (),
+        [],
+        seqs * rows * lanes * 20,
+    )
+    grad_left, grad_right = exchanged(low_pay, high_pay)
+    first_grad, side_grad, sums, low_pay, high_pay, conv2_grad = kernel_call(
+        second_back_kernel(rows, channels, seqs),
+        seqs,
+        (
+            grad, grad_left, grad_right, with_far(sums, reaches), second, second_left, second_right,
+            side_field, first, stats, second_stats, inverse, owner, place, crop_t,
+        ),
+        (backward_band(conv2_weight),),
+        (field, low_field, table(2), pay(2), pay(2)),
+        (((27, channels, channels), wide),),
+        conv_scratch(rows, channels)
+        + [
+            pltpu.VMEM((SUBS * channels, rows), low_type),
+            pltpu.VMEM((9, 2 * channels, 4 * channels), wide),
+        ],
+        2 * conv_flops(seqs, rows, channels, channels),
+    )
+    back_left, back_right = exchanged(low_pay, high_pay)
+    up_grad, skip_grad, conv1_grad, conv3_grad = kernel_call(
+        first_back_kernel(rows, channels, seqs),
+        seqs,
+        (
+            first_grad, back_left, back_right, with_far(sums, reaches), first, first_left,
+            first_right, stats, inverse, owner, place, side_grad, upsampled, skip,
+        ),
+        (backward_band(conv1_weight), conv3_weight.T),
+        (low_field, field),
+        (((27, width, channels), wide), ((width, channels), wide)),
+        conv_scratch(rows, channels)
+        + [
+            pltpu.VMEM((SUBS * width, rows), low_type),
+            pltpu.VMEM((9, 2 * width, 4 * channels), wide),
+        ],
+        2 * conv_flops(seqs, rows, channels, width),
+    )
+    return (section_out, up_grad, skip_grad, conv1_grad, conv2_grad, conv3_grad)
+
+
+def crop_tables(crop_sides, inside, shape_info, first_row, row_count):
+    seqs, crops = crop_sides.shape
+    spare = CROP_ROWS - crops
+    own = jnp.arange(row_count, dtype=jnp.int32)[None, :] + EDGE
+    columns = []
+    for offset in all_offsets():
+        near_step, far_step = step_sizes(offset)
+        step = jnp.where(shape_info[4], far_step, near_step)
+        columns.append(jnp.where(in_crop(shape_info, offset), own + step, -1))
+    place = jnp.stack(columns, axis=-1).astype(jnp.int32)
+    wide_places = first_row - EDGE + jnp.arange(row_count + 2 * EDGE, dtype=jnp.int32)
+    wide_places = jnp.broadcast_to(wide_places, (seqs, row_count + 2 * EDGE))
+    owner = jnp.pad(locate(crop_sides, wide_places)[0], ((0, 0), (0, 0), (0, spare)))
+    crop_t = jnp.pad(inside.swapaxes(1, 2), ((0, 0), (0, spare), (0, 0)))
+    counts = jnp.maximum(8.0 * (crop_sides * crop_sides * crop_sides).astype(wide), 1.0)
+    inverse = jnp.pad(1.0 / counts, ((0, 0), (0, spare)), constant_values=1.0)
+    inverse = jnp.broadcast_to(inverse[:, :, None], (seqs, CROP_ROWS, 128))
+    return (place, owner.astype(low_type), crop_t.astype(low_type), inverse)
 
 
 def local(
@@ -326,8 +665,6 @@
     )
     inside, segment, side_of, first_of = locate(crop_sides, places)
     shape_info = geometry(side_of, first_of, places)
-    inside_float = inside.astype(jnp.float32)
-    counts = jnp.maximum(8.0 * (crop_sides * crop_sides * crop_sides).astype(jnp.float32), 1.0)
     reaches = (key_reach + row_count - 1) // row_count
     token_values = tokens.astype(jnp.float32)
     normed_low = layer_norm(token_values, ln1_gain, ln1_bias).astype(jnp.bfloat16)
@@ -398,58 +735,18 @@
     upsampled = jnp.einsum(
         "std,de->ste", resid_low, deconv_weight, preferred_element_type=jnp.float32
     )
-    upsampled = upsampled.astype(jnp.bfloat16).reshape(seq_count, row_count, 2, 2, 2, channels)
-    joined = jnp.concatenate(
-        [upsampled, skip_features.reshape(seq_count, row_count, 2, 2, 2, channels)], axis=-1
-    )
-    joined_pad = with_rims(joined)
-    first_conv = conv_forward(joined_pad, conv1_weight, shape_info, row_count)
-    side_conv = jnp.einsum(
-        "stxyzc,cd->stxyzd", joined, conv3_weight, preferred_element_type=jnp.float32
-    )
-    normed_pair, scale_pair = norm_forward([first_conv, side_conv], inside_float, counts, reaches)
-    first_norm, side_norm = normed_pair
-    hidden_low = jax.nn.silu(first_norm).astype(jnp.bfloat16)
-    hidden_pad = with_rims(hidden_low)
-    second_conv = conv_forward(hidden_pad, conv2_weight, shape_info, row_count)
-    normed_last, scale_last = norm_forward([second_conv], inside_float, counts, reaches)
-    second_norm = normed_last[0]
-    summed = second_norm + side_norm
-    section_out = (
-        jax.nn.silu(summed).astype(jnp.bfloat16).reshape(seq_count, row_count, 8, channels)
-    )
-    grad_out = cotangent.astype(jnp.float32).reshape(seq_count, row_count, 2, 2, 2, channels)
-    silu_pull = jax.vjp(jax.nn.silu, summed)[1]
-    grad_sum = silu_pull(grad_out)[0]
-    second_grad, side_grad = norm_backward(
-        [grad_sum, grad_sum],
-        [second_norm, side_norm],
-        [scale_last[0], scale_pair[1]],
-        inside_float,
-        counts,
+    upsampled = upsampled.astype(jnp.bfloat16)
+    geometry_in = crop_tables(crop_sides, inside, shape_info, first_row, row_count)
+    section_out, up_grad, skip_grad, conv1_grad, conv2_grad, conv3_grad = conv_section(
+        upsampled,
+        skip_features.reshape(seq_count, row_count, 8 * channels),
+        cotangent.reshape(seq_count, row_count, 8 * channels),
+        (conv1_weight, conv2_weight, conv3_weight),
+        geometry_in,
         reaches,
     )
-    second_low = second_grad.astype(jnp.bfloat16)
-    side_low = side_grad.astype(jnp.bfloat16)
-    hidden_pad_grad, conv2_grad = conv_backward(hidden_pad, conv2_weight, shape_info, second_low)
-    hidden_grad = fold_rims(hidden_pad_grad)
-    first_pull = jax.vjp(jax.nn.silu, first_norm)[1]
-    first_norm_grad = first_pull(hidden_grad)[0]
-    first_grad = norm_backward(
-        [first_norm_grad], [first_norm], [scale_pair[0]], inside_float, counts, reaches
-    )[0]
-    first_low = first_grad.astype(jnp.bfloat16)
-    joined_pad_grad, conv1_grad = conv_backward(joined_pad, conv1_weight, shape_info, first_low)
-    joined_grad = fold_rims(joined_pad_grad) + jnp.einsum(
-        "stxyzd,cd->stxyzc", side_low, conv3_weight, preferred_element_type=jnp.float32
-    )
-    conv3_grad = jnp.einsum(
-        "stxyzc,stxyzd->cd", joined, side_low, preferred_element_type=jnp.float32
-    )
-    skip_grad = joined_grad[..., channels:].reshape(seq_count, row_count, 8, channels)
-    up_grad = (
-        joined_grad[..., :channels].reshape(seq_count, row_count, 8 * channels).astype(jnp.bfloat16)
-    )
+    section_out = section_out.reshape(seq_count, row_count, 8, channels)
+    skip_grad = skip_grad.reshape(seq_count, row_count, 8, channels)
     deconv_grad = jnp.einsum("std,ste->de", resid_low, up_grad, preferred_element_type=jnp.float32)
     resid_two_grad = jnp.einsum(
         "ste,de->std", up_grad, deconv_weight, preferred_element_type=jnp.float32

time: 4510 us -> 1100 us (0.24); the launches traced: 4430 us -> 1090 us
  local copies, waits for them, and re-layouts: 2730 us -> 115 us
  other arithmetic: 889 us -> 178 us
  matrix products: 517 us -> 176 us
  waiting for transfers between devices: 145 us -> 357 us
  Pallas kernels: 0 us -> 132 us
    scatter-add x106 -> x0, local copies, waits for them, and re-layouts: 2140 us -> none  [the longest x44 1100 us: unshift(): grad_pad.at[:, halo_rows + far_step:halo_rows + far_step + length]]
    add x85 -> x4, other arithmetic: 407 us -> 1.68 us  [the longest x2 1.11 us: crop_tables(): columns.append(jnp.where(in_crop(shape_info, offset), own + step, -1))]
    dot_general x188 -> x0, matrix products: 346 us -> none  [the longest x54 141 us: conv_backward(): jnp.einsum('stxyzc,stXYZd->xyzXYZcd', source, target, preferred_element_t...]
    scatter-add x60 -> x0, other arithmetic: 249 us -> none  [the longest x38 153 us: conv_backward(): grad_kernel.at[tap_index.reshape(-1)]]
    slice x22 -> x2, local copies, waits for them, and re-layouts: 189 us -> 2.02 us  [the longest x1 1.98 us: conv_section(): skip_left, skip_right = exchanged(skip[:, :EDGE], skip[:, rows - EDGE:])]
    pallas_call x0 -> x5, Pallas kernels: none -> 132 us  [kernel_call(): pl.pallas_call(body, grid=(seqs,), in_specs=[row_spec(a.shape) for a in i...]
    gather x38 -> x0, local copies, waits for them, and re-layouts: 108 us -> none  [conv_forward(): kernel_block = kernel[tap_table(offset)]]
    transpose x38 -> x2, local copies, waits for them, and re-layouts: 94.7 us -> 4.14 us  [backward_band(): return banded(taps[::-1, ::-1, ::-1].swapaxes(3, 4))]
  transfers between devices with their start and end apart: 34 -> 30, of which waited for: 12 -> 13; matrix products, arithmetic and copies ran while one was open for 17% -> 37% of each run, Pallas kernels for 0% -> 0%
where the time goes in v1:
time: 1100 us; the launch traced here: 1090 us
  waiting for transfers between devices  357 us (32%)
  other arithmetic  178 us (16%)
  matrix products  176 us (16%)
  Pallas kernels  132 us (12%)
  local copies, waits for them, and re-layouts  115 us (10%)
  blocking collectives  63.6 us (6%)
  starting transfers between devices  55.4 us (5%)
  between operations  16.9 us (2%)
    pallas_call x5, Pallas kernels, kernel_call(): pl.pallas_call(body, grid=(seqs,), in_specs=[row_spec(a.shape) for a in i...  132 us
    reduce_scatter x1, waiting for transfers between devices, local(): lax.psum_scatter(fc2_grad.astype(jnp.bfloat16), 'tok', scatter_dimension=...  78.5 us
    reduce_scatter x1, waiting for transfers between devices, local(): lax.psum_scatter(fc1_grad.astype(jnp.bfloat16), 'tok', scatter_dimension=...  78.5 us
    reduce_scatter x1, waiting for transfers between devices, local(): lax.psum_scatter(qkv_grad.astype(jnp.bfloat16), 'tok', scatter_dimension=...  71.1 us
    ppermute x20, starting transfers between devices, passed_along(): return lax.ppermute(block, axis, route)  54.5 us
    unnamed x1, blocking collectives  53.1 us
    reduce_scatter x1, waiting for transfers between devices, local(): lax.psum_scatter(conv2_grad.astype(jnp.bfloat16), 'tok', scatter_dimensio...  45.9 us
    unnamed x146, local copies, waits for them, and re-layouts  33.5 us
  transfers between devices with their start and end apart: 30, of which 13 were waited for; matrix products, arithmetic and copies ran while one was open for 37% of the time, Pallas kernels for 0%

profile of v1, /device:TPU:30, one launch (start us, length us, event | category | flops | bytes accessed | tf_op | source)
XLA Modules:
  0.0 1094.4 jit_solution(3715003110372119047)
XLA Ops:
  11.5 5.3 add_convert_fusion.1
  20.7 3.4 collective-permute-start.2
  29.5 3.7 reshape.2132.skip
  47.1 17.9 %add_select_fusion.4 = (s32[3,256,1]{2,1,0:T(8,128)}, pred[3,256,1]{2,1,0:T(8,128)(4,1)S(1)}, pred[3,256,1]{2,1,0:T(8,128)(4,1)S(1)}, pred[3,256,1]{2,1,0:T(8,12...) fusion(s32[256]{0:T(256)} %get-tuple-element.407, ...), kind=kLoop, calls=%fused_computation.127 | loop fusion | flops 39936 | bytes 22784 | tf_op jit(solution)/shard_map/jit(_where)/select_n | solution.py:625
  65.0 7.9 add_select_fusion.13
  74.8 3.5 add_select_fusion.9
  80.8 7.3 stack.11.place
  91.4 3.9 fusion.18
  98.0 3.5 pad_maximum_fusion.1
  101.6 6.0 copy.184
  107.6 3.5 pad_maximum_fusion
  111.1 6.1 copy.182
  117.2 14.2 %fusion.6 = (f32[3,12,256]{2,1,0:T(8,128)S(1)}, f32[3,12,256,768]{3,2,1,0:T(8,128)}) fusion(pred[3,256,768]{2,1,0:T(8,128)(4,1)} %broadcast_compare_fusion, bf16[3,256,12,64]{1,3,2,0:T(8,128)(2,1)} %bitcast.120, bf16[3,768,12,64]{1,3,2,0:T(8,128)(2,1)} %bitcast.115), kind=kOutput, calls=%fused_computation.12 | convolution fusion | flops 927194112 | bytes 33656832 | tf_op jit(solution)/shard_map/sqhd,skhd->shqk/dot_general | solution.py:93
  131.4 14.7 %fusion = f32[3,12,256]{2,1,0:T(8,128)S(1)} fusion(f32[3,12,256]{2,1,0:T(8,128)S(1)} %get-tuple-element.394, f32[3,12,256,768]{3,2,1,0:T(8,128)} %get-tuple-element.395, pred[3,256,768]{2,1,0:T(8,128)(4,1)S(1)} %copy-done.4), kind=kLoop, calls=%fused_computation.6 | loop fusion | flops 28302336 | bytes 28975104 | tf_op jit(solution)/shard_map/reduce_sum | solution.py:711
  146.1 13.8 %fusion.58 = bf16[3,12,64,256]{3,2,1,0:T(8,128)(2,1)S(1)} fusion(bf16[3,768,12,64]{1,3,2,0:T(8,128)(2,1)S(1)} %bitcast.119, f32[3,12,256]{2,1,0:T(8,128)S(1)} %fusion, f32[3,12,256]{2,1,0:T(8,128)S(1)} %get-tuple-element.394, f32[3,12,256,768]{3,2,1,0:T(8,128)} %get-tuple-element.395, pred[3,256,768]{2,1,0:T(8,128)(4,1)S(1)} %copy-done.4), kind=kOutput, calls=%fused_computation.110 | convolution fusion | flops 941948928 | bytes 33693696 | tf_op jit(solution)/shard_map/shqk,skhd->sqhd/dot_general | solution.py:714
  162.5 6.5 fusion.52
  169.1 23.1 %multiply_convert_fusion.1 = (bf16[3,256,3072]{2,1,0:T(8,128)(2,1)S(1)}, f32[3,256,3072]{2,1,0:T(8,128)}) fusion(f32[3,256,3072]{2,1,0:T(8,128)S(1)} %get-tuple-element.398, f32[3072]{0:T(1024)S(1)} %copy-done.39, u8[256,3072]{1,0:T(8,128)(4,1)S(1)} %get-tuple-element.247, u8[256,3072]{1,0:T(8,128)(4,1)S(1)} %get-tuple-element.246), kind=kLoop, calls=%fused_computation.26 | loop fusion | flops 167510016 | bytes 25178112 | tf_op jit(solution)/shard_map/convert_element_type | solution.py:728
  192.3 3.9 add_convert_fusion.2
  204.7 3.8 collective-permute-done.4.up_left
  209.3 27.2 %shard_map.359 = (f32[3,256,1024]{2,1,0:T(8,128)}, f32[3,256,1024]{2,1,0:T(8,128)}, f32[3,48,512]{2,1,0:T(8,128)}, bf16[3,48,1536]{2,1,0:T(8,128)(2,1)}, bf16[3,48,1536]{2,1,0:T(8,128)(2,1)}) custom-call(bf16[3,256,1024]{2,1,0:T(8,128)(2,1)} %copy-done.19, bf16[3,48,1024]{2,1,0:T(8,128)(2,1)} %copy-done.50, bf16[3,48,1024]{2,1,0:T(8,128)(2,1)} %copy-done.49, ...), custom_call_target="tpu_custom_call" | custom-call | flops 20132659200 | bytes 16737280 | tf_op jit(solution)/shard_map/pallas_call | solution.py:220
  238.4 3.6 collective-permute-start.9
  246.3 6.6 collective-permute-done.9.right_pay.first_right
  253.7 18.9 %shard_map.360 = (f32[3,256,1024]{2,1,0:T(8,128)}, f32[3,48,512]{2,1,0:T(8,128)}, f32[3,48,256]{2,1,0:T(8,128)}, bf16[3,48,1280]{2,1,0:T(8,128)(2,1)}, bf16[3,48,1280]{2,1,0:T(8,128)(2,1)}) custom-call(f32[3,256,1024]{2,1,0:T(8,128)} %get-tuple-element.125.first, bf16[3,48,1536]{2,1,0:T(8,128)(2,1)} %copy-done.47, bf16[3,48,1536]{2,1,0:T(8,128)(2,1)} %copy-done.48, ...), custom_call_target="tpu_custom_call" | custom-call | flops 10066329600 | bytes 11341824 | tf_op jit(solution)/shard_map/pallas_call | solution.py:220
  274.5 3.7 collective-permute-start.11
  278.2 3.8 copy.200
  282.1 3.7 reshape.2137.cotangent
  285.8 8.0 shard_map.361
  295.7 3.6 collective-permute-start.13
  308.1 31.6 %shard_map.362 = (f32[3,256,1024]{2,1,0:T(8,128)}, bf16[3,256,1024]{2,1,0:T(8,128)(2,1)}, f32[3,48,256]{2,1,0:T(8,128)}, bf16[3,48,1280]{2,1,0:T(8,128)(2,1)}, b...) custom-call(f32[3,256,1024]{2,1,0:T(8,128)} %get-tuple-element.136.grad, ...), custom_call_target="tpu_custom_call" | custom-call | flops 20132659200 | bytes 24858624 | tf_op jit(solution)/shard_map/pallas_call | solution.py:220
  341.7 3.8 collective-permute-start.15
  345.5 4.0 fusion.17
  354.0 46.3 %shard_map.363 = (bf16[3,256,1024]{2,1,0:T(8,128)(2,1)}, f32[3,256,1024]{2,1,0:T(8,128)}, f32[27,256,128]{2,1,0:T(8,128)}, f32[256,128]{1,0:T(8,128)}) custom-call(f32[3,256,1024]{2,1,0:T(8,128)} %get-tuple-element.141.grad, bf16[3,48,1280]{2,1,0:T(8,128)(2,1)} %collective-permute-done.14.grad_left, bf16[3,48,1280]{2,1,0:T(8,128)(2,1)} %collective-permute-done.15.grad_right, ...), custom_call_target="tpu_custom_call" | custom-call | flops 34628173824 | bytes 26505216 | tf_op jit(solution)/shard_map/pallas_call | solution.py:220
  400.3 4.3 bitcast_convert_fusion.3
  404.6 3.5 fusion.53
  408.1 14.5 %fusion.92 = (bf16[3072]{0:T(1024)(128)(2,1)}, bf16[3,256,3072]{2,1,0:T(8,128)(2,1)}) fusion(f32[3,256,3072]{2,1,0:T(8,128)} %get-tuple-element.326, bf16[3072,768]{1,0:T(8,128)(2,1)} %param.49, f32[3,256,768]{2,1,0:T(8,128)S(1)} %fusion.53, f32[3,256,3072]{2,1,0:T(8,128)} %copy-done.9, f32[3072]{0:T(1024)S(1)} %copy-done.40), kind=kOutput, calls=%fused_computation.237 | convolution fusion | flops 3662214144 | bytes 30689280 | tf_op jit(solution)/shard_map/std,fd->stf/dot_general | solution.py:757
  422.7 6.8 multiply_reduce_fusion.1
  436.1 3.8 convolution_convert_fusion.1
  444.9 15.2 %fusion.2 = f32[3,12,64,768]{3,2,1,0:T(8,128)} fusion(bf16[3,256,12,64]{1,3,2,0:T(8,128)(2,1)} %bitcast.128, f32[3,12,256]{2,1,0:T(8,128)} %log_add_fusion, f32[3,12,256,768]{3,2,1,0:T(8,128)} %get-tuple-element.395, pred[3,256,768]{2,1,0:T(8,128)(4,1)} %broadcast_compare_fusion), kind=kOutput, calls=%fused_computation.8 | convolution fusion | flops 934281216 | bytes 37195776 | tf_op jit(solution)/shard_map/shqk,sqhd->skhd/dot_general | solution.py:793
  460.1 8.1 copy.205
  468.1 3.4 convert.33
  475.9 4.4 copy.212
  480.3 3.8 collective-permute-start.18
  486.1 25.5 %multiply_reduce_fusion = (f32[3,12,256]{2,1,0:T(8,128)}, f32[3,12,256,768]{3,2,1,0:T(8,128)}) fusion(f32[3,12,256]{2,1,0:T(8,128)} %log_add_fusion, f32[3,12,256,768]{3,2,1,0:T(8,128)} %get-tuple-element.395, pred[3,256,768]{2,1,0:T(8,128)(4,1)} %broadcast_compare_fusion, bf16[3,256,12,64]{1,3,2,0:T(8,128)(2,1)} %bitcast.129, ...), kind=kOutput, calls=%fused_computation.1 | convolution fusion | flops 941349888 | bytes 62005248 | tf_op jit(solution)/shard_map/sqhd,skhd->shqk/dot_general | solution.py:780
  511.7 24.5 %multiply_convert_fusion = bf16[3,12,256,768]{3,2,1,0:T(8,128)(2,1)} fusion(f32[3,12,256,768]{3,2,1,0:T(8,128)} %get-tuple-element.401, f32[3,12,256]{2,1,0:T(8,128)} %get-tuple-element.400, f32[3,12,256]{2,1,0:T(8,128)} %log_add_fusion, f32[3,12,256,768]{3,2,1,0:T(8,128)} %get-tuple-element.395, pred[3,256,768]{2,1,0:T(8,128)(4,1)} %broadcast_compare_fusion), kind=kLoop, calls=%fused_computation | loop fusion | flops 42467328 | bytes 71442432 | tf_op jit(solution)/shard_map/convert_element_type | solution.py:784
  536.2 10.5 broadcast_multiply_fusion
  546.7 8.1 copy.203
  554.8 5.2 convert.31
  563.3 3.7 collective-permute-start.16
  569.0 11.8 %multiply_convert_fusion.2 = bf16[3,12,64,256]{3,2,1,0:T(8,128)(2,1)} fusion(bf16[3,768,12,64]{1,3,2,0:T(8,128)(2,1)} %bitcast.116, bf16[3,12,256,768]{3,2,1,0:T(8,128)(2,1)} %multiply_convert_fusion), kind=kOutput, calls=%fused_computation.96 | convolution fusion | flops 907149312 | bytes 18874368 | tf_op jit(solution)/shard_map/shqk,skhd->sqhd/dot_general | solution.py:786
  585.9 12.0 %collective-permute-done.16 = bf16[3,256,768]{2,1,0:T(8,128)(2,1)} collective-permute-done((bf16[3,256,768]{2,1,0:T(8,128)(2,1)}, bf16[3,256,768]{2,1,0:T(8,128)(2,1)}, u32[]{:S(2)}, u32[]{:S(2)}) %collective-permute-start.16) | collective-permute-done | bytes 1179680 | tf_op jit(solution)/shard_map/ppermute | solution.py:30
  601.8 5.6 bitcast_convert_fusion.2
  607.7 9.3 bitcast_convert_fusion
  617.0 9.6 bitcast_convert_fusion.1
  646.4 7.3 fusion.80
  653.8 32.3 %reduce-scatter.24.cloned.1.call-done = bf16[27,256,8]{1,0,2:T(8,128)(2,1)} async-done(((bf16[27,256,128]{1,0,2:T(8,128)(2,1)}), bf16[27,256,8]{1,0,2:T(8,128)(2,1)}) %reduce-scatter.24.cloned.1.call-update) | async-done | bytes 110608 | tf_op jit(solution)/shard_map/reduce_scatter | solution.py:871
  686.0 71.1 %reduce-scatter.14.cloned.1.call-done = bf16[48,2304]{1,0:T(8,128)(2,1)} async-done(((bf16[768,2304]{1,0:T(8,128)(2,1)}), bf16[48,2304]{1,0:T(8,128)(2,1)}) %reduce-scatter.14.cloned.1.call-update) | async-done | bytes 221200 | tf_op jit(solution)/shard_map/reduce_scatter | solution.py:838
  757.2 78.5 %reduce-scatter.20.cloned.1.call-done = bf16[192,768]{1,0:T(8,128)(2,1)} async-done(((bf16[3072,768]{1,0:T(8,128)(2,1)}), bf16[192,768]{1,0:T(8,128)(2,1)}) %reduce-scatter.20.cloned.1.call-update) | async-done | bytes 294928 | tf_op jit(solution)/shard_map/reduce_scatter | solution.py:862
  835.7 78.5 %reduce-scatter.18.cloned.1.call-done = bf16[48,3072]{1,0:T(8,128)(2,1)} async-done(((bf16[768,3072]{1,0:T(8,128)(2,1)}), bf16[48,3072]{1,0:T(8,128)(2,1)}) %reduce-scatter.18.cloned.1.call-update) | async-done | bytes 294928 | tf_op jit(solution)/shard_map/reduce_scatter | solution.py:856
  914.2 3.7 fusion.41
  917.9 53.1 %all-reduce.18 = (bf16[768]{0:T(1024)(128)(2,1)}, bf16[768]{0:T(1024)(128)(2,1)}, bf16[768]{0:T(1024)(128)(2,1)}, bf16[768]{0:T(1024)(128)(2,1)}, bf16[768]{0:T(...) all-reduce(bf16[768]{0:T(1024)(128)(2,1)} %get-tuple-element.250, ...), channel_id=2, replica_groups=mesh['seq'=2,'tok'=16] {'tok'}, use_global_device_ids=true, to_apply=%region_19.20.clone | all-reduce | flops 7680 | bytes 30720
  980.5 5.0 add_add_fusion.2
  986.3 45.9 %reduce-scatter.26.cloned.1.call-done = bf16[27,128,8]{1,0,2:T(8,128)(2,1)} async-done(((bf16[27,128,128]{1,0,2:T(8,128)(2,1)}), bf16[27,128,8]{1,0,2:T(8,128)(2,1)}) %reduce-scatter.26.cloned.1.call-update) | async-done | bytes 55312 | tf_op jit(solution)/shard_map/reduce_scatter | solution.py:874
  1032.2 10.5 all-reduce.19
  1053.2 24.0 %all-reduce.23.cloned.1.call-done = (bf16[27,256,8]{1,0,2:T(8,128)(2,1)}, bf16[48,2304]{1,0:T(8,128)(2,1)}, bf16[48,768]{1,0:T(8,128)(2,1)}, bf16[48,3072]{1,0:T...) async-done(((bf16[27,256,8]{1,0,2:T(8,128)(2,1)}, bf16[48,2304]{1,0:T(8,128)(2,1)}, bf16[48,768]{1,0:T(8,128)(2,1)}, bf16[48,3072]{1,0:T(8,128)(2,1)}, ...) | async-done | bytes 1093648 | tf_op jit(solution)/shard_map/psum | solution.py:895
  (286 shorter events, 157.1 us)
Async XLA Ops:
  7.2 637.8 %reduce-scatter.30.cloned.1.call-start = ((), (), s32[]{:S(2)}) async-start(), calls=%async_computation.17 | async-start | bytes 69632
  18.7 20.6 %copy-start.32 = (s32[3,45]{1,0:T(4,128)S(1)}, s32[3,45]{1,0:T(4,128)}, u32[]{:S(2)}) copy-start(s32[3,45]{1,0:T(4,128)} %param.38) | copy-start | bytes 1624
  18.7 76.6 %collective-permute-start.3 = (bf16[3,256,768]{2,1,0:T(8,128)(2,1)}, bf16[3,256,768]{2,1,0:T(8,128)(2,1)}, u32[]{:S(2)}, u32[]{:S(2)}) collective-permute-start(bf16[3,256,768]{2,1,0:T(8,128)(2,1)} %get-tuple-element.331), channel_id=1, source_target_pairs={{1,0},{2,1},{3,2},{4,3},{5,4},{6,5},{7,6},{8,7},{9,8},{10,9},{11,1... | collective-permute-start | bytes 3538952 | tf_op jit(solution)/shard_map/ppermute | solution.py:30
  20.7 77.3 %collective-permute-start.2 = (bf16[3,256,768]{2,1,0:T(8,128)(2,1)}, bf16[3,256,768]{2,1,0:T(8,128)(2,1)}, u32[]{:S(2)}, u32[]{:S(2)}) collective-permute-start(bf16[3,256,768]{2,1,0:T(8,128)(2,1)} %get-tuple-element.331), channel_id=1, source_target_pairs={{0,1},{1,2},{2,3},{3,4},{4,5},{5,6},{6,7},{7,8},{8,9},{9,10},{10,1... | collective-permute-start | bytes 3538952 | tf_op jit(solution)/shard_map/ppermute | solution.py:30
  24.2 83.4 %collective-permute-start.1 = (bf16[3,256,768]{2,1,0:T(8,128)(2,1)}, bf16[3,256,768]{2,1,0:T(8,128)(2,1)}, u32[]{:S(2)}, u32[]{:S(2)}) collective-permute-start(bf16[3,256,768]{2,1,0:T(8,128)(2,1)} %get-tuple-element.333), channel_id=1, source_target_pairs={{1,0},{2,1},{3,2},{4,3},{5,4},{6,5},{7,6},{8,7},{9,8},{10,9},{11,1... | collective-permute-start | bytes 3538952 | tf_op jit(solution)/shard_map/ppermute | solution.py:30
  26.3 81.3 %collective-permute-start = (bf16[3,256,768]{2,1,0:T(8,128)(2,1)}, bf16[3,256,768]{2,1,0:T(8,128)(2,1)}, u32[]{:S(2)}, u32[]{:S(2)}) collective-permute-start(bf16[3,256,768]{2,1,0:T(8,128)(2,1)} %get-tuple-element.333), channel_id=1, source_target_pairs={{0,1},{1,2},{2,3},{3,4},{4,5},{5,6},{6,7},{7,8},{8,9},{9,10},{10,1... | collective-permute-start | bytes 3538952 | tf_op jit(solution)/shard_map/ppermute | solution.py:30
  35.2 167.4 %collective-permute-start.7 = (bf16[3,48,1024]{2,1,0:T(8,128)(2,1)}, bf16[3,48,1024]{2,1,0:T(8,128)(2,1)}, u32[]{:S(2)}, u32[]{:S(2)}) collective-permute-start(bf16[3,48,1024]{2,1,0:T(8,128)(2,1)} %get-tuple-element.335), channel_id=1, source_target_pairs={{1,0},{2,1},{3,2},{4,3},{5,4},{6,5},{7,6},{8,7},{9,8},{10,9},{11,1... | collective-permute-start | bytes 884744 | tf_op jit(solution)/shard_map/ppermute | solution.py:30
  64.9 8.0 copy-start.33
  64.9 8.0 copy-start.43
  65.0 9.8 copy-start.44
  95.3 107.3 %collective-permute-start.6 = (bf16[3,48,1024]{2,1,0:T(8,128)(2,1)}, bf16[3,48,1024]{2,1,0:T(8,128)(2,1)}, u32[]{:S(2)}, u32[]{:S(2)}) collective-permute-start(bf16[3,48,1024]{2,1,0:T(8,128)(2,1)} %get-tuple-element.336), channel_id=1, source_target_pairs={{0,1},{1,2},{2,3},{3,4},{4,5},{5,6},{6,7},{7,8},{8,9},{9,10},{10,1... | collective-permute-start | bytes 884744 | tf_op jit(solution)/shard_map/ppermute | solution.py:30
  117.2 14.2 %copy-start.4 = (pred[3,256,768]{2,1,0:T(8,128)(4,1)S(1)}, pred[3,256,768]{2,1,0:T(8,128)(4,1)}, u32[]{:S(2)}) copy-start(pred[3,256,768]{2,1,0:T(8,128)(4,1)} %broadcast_compare_fusion) | copy-start | bytes 1769476
  131.4 14.7 %copy-start.18 = (f32[3,12,256]{2,1,0:T(8,128)}, f32[3,12,256]{2,1,0:T(8,128)S(1)}, u32[]{:S(2)}) copy-start(f32[3,12,256]{2,1,0:T(8,128)S(1)} %get-tuple-element.394) | copy-start | bytes 110596
  131.4 14.7 %copy-start.5 = (bf16[3,768,768]{1,2,0:T(8,128)(2,1)S(1)}, bf16[3,768,768]{1,2,0:T(8,128)(2,1)}, u32[]{:S(2)}) copy-start(bf16[3,768,768]{1,2,0:T(8,128)(2,1)} %copy.182) | copy-start | bytes 10616836
  131.4 31.1 %slice-start.2 = ((s8[4718592]{0:T(1024)(128)(4,1)}), s8[4194304]{0:T(1024)(128)(4,1)S(1)}, s32[]{:S(2)}) async-start(s8[4718592]{0:T(1024)(128)(4,1)} %bitcast.147), calls=%async_computation.21 | async-start | bytes 8388608
  146.1 13.9 %copy-start.20 = (f32[3,12,256]{2,1,0:T(8,128)}, f32[3,12,256]{2,1,0:T(8,128)S(1)}, u32[]{:S(2)}) copy-start(f32[3,12,256]{2,1,0:T(8,128)S(1)} %fusion) | copy-start | bytes 110596
  146.1 13.9 %copy-start.2 = (bf16[3,256,768]{2,1,0:T(8,128)(2,1)S(1)}, bf16[3,256,768]{2,1,0:T(8,128)(2,1)}, u32[]{:S(2)}) copy-start(bf16[3,256,768]{2,1,0:T(8,128)(2,1)} %param.36) | copy-start | bytes 3538948
  146.1 13.9 %copy-start.46 = (bf16[768,768]{1,0:T(8,128)(2,1)S(1)}, bf16[768,768]{1,0:T(8,128)(2,1)}, u32[]{:S(2)}) copy-start(bf16[768,768]{1,0:T(8,128)(2,1)} %param.43) | copy-start | bytes 3538948
  146.1 13.9 %copy-start.51 = (f32[768]{0:T(1024)S(1)}, f32[768]{0:T(1024)}, u32[]{:S(2)}) copy-start(f32[768]{0:T(1024)} %param.44) | copy-start | bytes 9220
  146.1 16.3 %slice-start.3 = ((s8[4718592]{0:T(1024)(128)(4,1)}), s8[524288]{0:T(1024)(128)(4,1)S(1)}, s32[]{:S(2)}) async-start(s8[4718592]{0:T(1024)(128)(4,1)} %bitcast.147), calls=%async_computation.22 | async-start | bytes 1048576
  160.1 32.1 %slice-start = ((s8[4718592]{0:T(1024)(128)(4,1)}), s8[4194304]{0:T(1024)(128)(4,1)S(1)}, s32[]{:S(2)}) async-start(s8[4718592]{0:T(1024)(128)(4,1)} %bitcast.145), calls=%async_computation.19 | async-start | bytes 8388608
  161.4 30.8 %copy-start.7 = (f32[3,256,768]{2,1,0:T(8,128)}, f32[3,256,768]{2,1,0:T(8,128)S(1)}, u32[]{:S(2)}) copy-start(f32[3,256,768]{2,1,0:T(8,128)S(1)} %get-tuple-element.397) | copy-start | bytes 7077892
  162.5 29.7 %slice-start.1 = ((s8[4718592]{0:T(1024)(128)(4,1)}), s8[524288]{0:T(1024)(128)(4,1)S(1)}, s32[]{:S(2)}) async-start(s8[4718592]{0:T(1024)(128)(4,1)} %bitcast.145), calls=%async_computation.20 | async-start | bytes 1048576
  169.1 23.1 %copy-start.9 = (f32[3,256,3072]{2,1,0:T(8,128)}, f32[3,256,3072]{2,1,0:T(8,128)S(1)}, u32[]{:S(2)}) copy-start(f32[3,256,3072]{2,1,0:T(8,128)S(1)} %get-tuple-element.398) | copy-start | bytes 28311556
  169.1 23.1 %copy-start.52 = (f32[768]{0:T(1024)S(1)}, f32[768]{0:T(1024)}, u32[]{:S(2)}) copy-start(f32[768]{0:T(1024)} %param.50) | copy-start | bytes 9220
  197.6 11.0 %copy-start.19 = (bf16[3,256,1024]{2,1,0:T(8,128)(2,1)}, bf16[3,256,1024]{2,1,0:T(8,128)(2,1)S(1)}, u32[]{:S(2)}) copy-start(bf16[3,256,1024]{2,1,0:T(8,128)(2,1)S(1)} %convolution_convert_fusion.up) | copy-start | bytes 4718596
  197.6 7.1 collective-permute-start.5
  200.5 8.0 collective-permute-start.4
  236.5 9.8 collective-permute-start.8
  238.4 14.5 %collective-permute-start.9 = (bf16[3,48,1536]{2,1,0:T(8,128)(2,1)}, bf16[3,48,1536]{2,1,0:T(8,128)(2,1)S(1)}, u32[]{:S(2)}, u32[]{:S(2)}) collective-permute-start(bf16[3,48,1536]{2,1,0:T(8,128)(2,1)} %get-tuple-element.127), channel_id=1, source_target_pairs={{1,0},{2,1},{3,2},{4,3},{5,4},{6,5},{7,6},{8,7},{9,8},{10,9},{11,1... | collective-permute-start | bytes 1327112 | tf_op jit(solution)/shard_map/ppermute | solution.py:30
  272.6 13.2 %collective-permute-start.10 = (bf16[3,48,1280]{2,1,0:T(8,128)(2,1)}, bf16[3,48,1280]{2,1,0:T(8,128)(2,1)}, u32[]{:S(2)}, u32[]{:S(2)}) collective-permute-start(bf16[3,48,1280]{2,1,0:T(8,128)(2,1)} %get-tuple-element.132), channel_id=1, source_target_pairs={{0,1},{1,2},{2,3},{3,4},{4,5},{5,6},{6,7},{7,8},{8,9},{9,10},{10,1... | collective-permute-start | bytes 1105928 | tf_op jit(solution)/shard_map/ppermute | solution.py:30
  274.5 11.3 %collective-permute-start.11 = (bf16[3,48,1280]{2,1,0:T(8,128)(2,1)}, bf16[3,48,1280]{2,1,0:T(8,128)(2,1)}, u32[]{:S(2)}, u32[]{:S(2)}) collective-permute-start(bf16[3,48,1280]{2,1,0:T(8,128)(2,1)} %get-tuple-element.133), channel_id=1, source_target_pairs={{1,0},{2,1},{3,2},{4,3},{5,4},{6,5},{7,6},{8,7},{9,8},{10,9},{11,1... | collective-permute-start | bytes 1105928 | tf_op jit(solution)/shard_map/ppermute | solution.py:30
  293.8 14.1 %collective-permute-start.12 = (bf16[3,48,1408]{2,1,0:T(8,128)(2,1)}, bf16[3,48,1408]{2,1,0:T(8,128)(2,1)}, u32[]{:S(2)}, u32[]{:S(2)}) collective-permute-start(bf16[3,48,1408]{2,1,0:T(8,128)(2,1)} %get-tuple-element.137), channel_id=1, source_target_pairs={{0,1},{1,2},{2,3},{3,4},{4,5},{5,6},{6,7},{7,8},{8,9},{9,10},{10,1... | collective-permute-start | bytes 1216520 | tf_op jit(solution)/shard_map/ppermute | solution.py:30
  295.7 12.4 %collective-permute-start.13 = (bf16[3,48,1408]{2,1,0:T(8,128)(2,1)}, bf16[3,48,1408]{2,1,0:T(8,128)(2,1)}, u32[]{:S(2)}, u32[]{:S(2)}) collective-permute-start(bf16[3,48,1408]{2,1,0:T(8,128)(2,1)} %get-tuple-element.138), channel_id=1, source_target_pairs={{1,0},{2,1},{3,2},{4,3},{5,4},{6,5},{7,6},{8,7},{9,8},{10,9},{11,1... | collective-permute-start | bytes 1216520 | tf_op jit(solution)/shard_map/ppermute | solution.py:30
  339.7 12.8 %collective-permute-start.14 = (bf16[3,48,1280]{2,1,0:T(8,128)(2,1)}, bf16[3,48,1280]{2,1,0:T(8,128)(2,1)}, u32[]{:S(2)}, u32[]{:S(2)}) collective-permute-start(bf16[3,48,1280]{2,1,0:T(8,128)(2,1)} %get-tuple-element.142), channel_id=1, source_target_pairs={{0,1},{1,2},{2,3},{3,4},{4,5},{5,6},{6,7},{7,8},{8,9},{9,10},{10,1... | collective-permute-start | bytes 1105928 | tf_op jit(solution)/shard_map/ppermute | solution.py:30
  341.7 12.3 %collective-permute-start.15 = (bf16[3,48,1280]{2,1,0:T(8,128)(2,1)}, bf16[3,48,1280]{2,1,0:T(8,128)(2,1)}, u32[]{:S(2)}, u32[]{:S(2)}) collective-permute-start(bf16[3,48,1280]{2,1,0:T(8,128)(2,1)} %get-tuple-element.143), channel_id=1, source_target_pairs={{1,0},{2,1},{3,2},{4,3},{5,4},{6,5},{7,6},{8,7},{9,8},{10,9},{11,1... | collective-permute-start | bytes 1105928 | tf_op jit(solution)/shard_map/ppermute | solution.py:30
  404.6 18.0 %slice-start.4 = ((s8[4718592]{0:T(1024)(128)(4,1)}), s8[4194304]{0:T(1024)(128)(4,1)S(1)}, s32[]{:S(2)}) async-start(s8[4718592]{0:T(1024)(128)(4,1)} %bitcast.149), calls=%async_computation.23 | async-start | bytes 8388608
  408.0 22.4 %copy-start.10 = (f32[3,256,768]{2,1,0:T(8,128)}, f32[3,256,768]{2,1,0:T(8,128)S(1)}, u32[]{:S(2)}) copy-start(f32[3,256,768]{2,1,0:T(8,128)S(1)} %fusion.53) | copy-start | bytes 7077892
  408.1 14.6 %copy-start.8 = (f32[3,256,768]{2,1,0:T(8,128)S(1)}, f32[3,256,768]{2,1,0:T(8,128)}, u32[]{:S(2)}) copy-start(f32[3,256,768]{2,1,0:T(8,128)} %copy-done.7) | copy-start | bytes 7077892
  408.1 14.6 %copy-start.35 = (f32[3,256]{1,0:T(4,128)S(1)}, f32[3,256]{1,0:T(4,128)}, u32[]{:S(2)}) copy-start(f32[3,256]{1,0:T(4,128)} %copy-done.34) | copy-start | bytes 9220
  408.1 14.6 %copy-start.42 = (f32[768]{0:T(1024)S(1)}, f32[768]{0:T(1024)}, u32[]{:S(2)}) copy-start(f32[768]{0:T(1024)} %param.45) | copy-start | bytes 9220
  408.1 14.5 %slice-start.5 = ((s8[4718592]{0:T(1024)(128)(4,1)}), s8[524288]{0:T(1024)(128)(4,1)S(1)}, s32[]{:S(2)}) async-start(s8[4718592]{0:T(1024)(128)(4,1)} %bitcast.149), calls=%async_computation.24 | async-start | bytes 1048576
  442.1 211.7 %reduce-scatter.16.cloned.1.call-start = ((), (), s32[]{:S(2)}) async-start(), calls=%async_computation.10 | async-start | bytes 1253376 | tf_op jit(solution)/shard_map/reduce_scatter | solution.py:844
  480.3 102.8 %collective-permute-start.18 = (bf16[3,256,768]{2,1,0:T(8,128)(2,1)}, bf16[3,256,768]{2,1,0:T(8,128)(2,1)}, u32[]{:S(2)}, u32[]{:S(2)}) collective-permute-start(bf16[3,256,768]{2,1,0:T(8,128)(2,1)} %get-tuple-element.329), channel_id=1, source_target_pairs={{1,0},{2,1},{3,2},{4,3},{5,4},{6,5},{7,6},{8,7},{9,8},{10,9},{11,1... | collective-permute-start | bytes 3538952 | tf_op jit(solution)/shard_map/ppermute | solution.py:30
  484.1 99.0 %collective-permute-start.19 = (bf16[3,256,768]{2,1,0:T(8,128)(2,1)}, bf16[3,256,768]{2,1,0:T(8,128)(2,1)}, u32[]{:S(2)}, u32[]{:S(2)}) collective-permute-start(bf16[3,256,768]{2,1,0:T(8,128)(2,1)} %get-tuple-element.330), channel_id=1, source_target_pairs={{0,1},{1,2},{2,3},{3,4},{4,5},{5,6},{6,7},{7,8},{8,9},{9,10},{10,1... | collective-permute-start | bytes 3538952 | tf_op jit(solution)/shard_map/ppermute | solution.py:30
  486.1 167.7 %reduce-scatter.22.cloned.1.call-start = ((), (), s32[]{:S(2)}) async-start(), calls=%async_computation.13 | async-start | bytes 1671168 | tf_op jit(solution)/shard_map/reduce_scatter | solution.py:868
  511.6 174.4 %reduce-scatter.24.cloned.1.call-start = ((), (), s32[]{:S(2)}) async-start(), calls=%async_computation.14 | async-start | bytes 2228224 | tf_op jit(solution)/shard_map/reduce_scatter | solution.py:871
  511.7 24.5 %copy-start.6 = (bf16[3,256,768]{1,2,0:T(8,128)(2,1)S(1)}, bf16[3,256,768]{1,2,0:T(8,128)(2,1)}, u32[]{:S(2)}) copy-start(bf16[3,256,768]{1,2,0:T(8,128)(2,1)} %copy.183) | copy-start | bytes 3538948
  560.1 197.1 %reduce-scatter.14.cloned.1.call-start = ((), (), s32[]{:S(2)}) async-start(), calls=%async_computation.9 | async-start | bytes 3760128 | tf_op jit(solution)/shard_map/reduce_scatter | solution.py:838
  563.3 34.6 %collective-permute-start.16 = (bf16[3,256,768]{2,1,0:T(8,128)(2,1)}, bf16[3,256,768]{2,1,0:T(8,128)(2,1)}, u32[]{:S(2)}, u32[]{:S(2)}) collective-permute-start(bf16[3,256,768]{2,1,0:T(8,128)(2,1)} %get-tuple-element.327), channel_id=1, source_target_pairs={{1,0},{2,1},{3,2},{4,3},{5,4},{6,5},{7,6},{8,7},{9,8},{10,9},{11,1... | collective-permute-start | bytes 3538952 | tf_op jit(solution)/shard_map/ppermute | solution.py:30
  567.1 30.9 %collective-permute-start.17 = (bf16[3,256,768]{2,1,0:T(8,128)(2,1)}, bf16[3,256,768]{2,1,0:T(8,128)(2,1)}, u32[]{:S(2)}, u32[]{:S(2)}) collective-permute-start(bf16[3,256,768]{2,1,0:T(8,128)(2,1)} %get-tuple-element.328), channel_id=1, source_target_pairs={{0,1},{1,2},{2,3},{3,4},{4,5},{5,6},{6,7},{7,8},{8,9},{9,10},{10,1... | collective-permute-start | bytes 3538952 | tf_op jit(solution)/shard_map/ppermute | solution.py:30
  585.9 14.8 %copy-start.13 = (bf16[3,256,768]{2,1,0:T(8,128)(2,1)}, bf16[3,256,768]{2,1,0:T(8,128)(2,1)S(1)}, u32[]{:S(2)}) copy-start(bf16[3,256,768]{2,1,0:T(8,128)(2,1)S(1)} %fusion.48) | copy-start | bytes 3538948
  585.9 15.9 %copy-start.3 = (bf16[3,256,768]{2,1,0:T(8,128)(2,1)S(1)}, bf16[3,256,768]{2,1,0:T(8,128)(2,1)}, u32[]{:S(2)}) copy-start(bf16[3,256,768]{2,1,0:T(8,128)(2,1)} %param.36) | copy-start | bytes 3538948
  585.9 15.8 %copy-start.12 = (bf16[3,256,768]{2,1,0:T(8,128)(2,1)S(1)}, bf16[3,256,768]{2,1,0:T(8,128)(2,1)}, u32[]{:S(2)}) copy-start(bf16[3,256,768]{2,1,0:T(8,128)(2,1)} %copy.207) | copy-start | bytes 3538948
  585.9 15.8 %copy-start.23 = (f32[3,256]{1,0:T(4,128)S(1)}, f32[3,256]{1,0:T(4,128)}, u32[]{:S(2)}) copy-start(f32[3,256]{1,0:T(4,128)} %copy-done.22) | copy-start | bytes 9220
  585.9 15.8 %copy-start.29 = (f32[3,256]{1,0:T(4,128)S(1)}, f32[3,256]{1,0:T(4,128)}, u32[]{:S(2)}) copy-start(f32[3,256]{1,0:T(4,128)} %copy-done.28) | copy-start | bytes 9220
  585.9 15.8 %copy-start.37 = (f32[768]{0:T(1024)S(1)}, f32[768]{0:T(1024)}, u32[]{:S(2)}) copy-start(f32[768]{0:T(1024)} %param.39) | copy-start | bytes 9220
  585.9 15.8 %copy-start.53 = (f32[768]{0:T(1024)S(1)}, f32[768]{0:T(1024)}, u32[]{:S(2)}) copy-start(f32[768]{0:T(1024)} %param.40) | copy-start | bytes 9220
  607.4 228.3 %reduce-scatter.20.cloned.1.call-start = ((), (), s32[]{:S(2)}) async-start(), calls=%async_computation.12 | async-start | bytes 5013504 | tf_op jit(solution)/shard_map/reduce_scatter | solution.py:862
  616.9 297.2 %reduce-scatter.18.cloned.1.call-start = ((), (), s32[]{:S(2)}) async-start(), calls=%async_computation.11 | async-start | bytes 5013504 | tf_op jit(solution)/shard_map/reduce_scatter | solution.py:856
  626.6 359.0 %reduce-scatter.28.cloned.1.call-start = ((), (), s32[]{:S(2)}) async-start(), calls=%async_computation.16 | async-start | bytes 208896
  631.1 401.1 %reduce-scatter.26.cloned.1.call-start = ((), (), s32[]{:S(2)}) async-start(), calls=%async_computation.15 | async-start | bytes 1114112 | tf_op jit(solution)/shard_map/reduce_scatter | solution.py:874
  636.5 440.6 %all-reduce.23.cloned.1.call-start = ((), (), s32[]{:S(2)}) async-start(), calls=%async_computation.18 | async-start | bytes 2228224 | tf_op jit(solution)/shard_map/psum | solution.py:895
  653.7 326.8 %copy-start.31 = (f32[3,256]{1,0:T(4,128)S(1)}, f32[3,256]{1,0:T(4,128)}, u32[]{:S(2)}) copy-start(f32[3,256]{1,0:T(4,128)} %copy-done.30) | copy-start | bytes 9220
  (30 other events, 102.2 us)
Sparse Core Ops, SparseCore 0:
  442.2 51.6 reduce-scatter.29
  497.9 56.9 reduce-scatter.15
  559.0 62.8 reduce-scatter.21
  625.5 60.5 reduce-scatter.23
  690.3 66.8 reduce-scatter.13
  761.4 74.2 reduce-scatter.19
  839.5 74.5 reduce-scatter.17
  918.6 52.9 reduce-scatter.27
  975.7 56.4 reduce-scatter.25
  1034.7 42.3 all-reduce.22

commit v2 on v1

--- a/solution.py
+++ b/solution.py
@@ -205,7 +205,10 @@
                 number = tap_x * 3 + tap_y
                 here = total_ref[number, :width, sub_lanes(tap_z, channels)]
                 there = total_ref[number, width:, sub_lanes(tap_z + 1, channels)]
-                grad_ref[26 - (number * 3 + tap_z)] = here + there
+                tap = 26 - (number * 3 + tap_z)
+                for half in range(width // channels):
+                    rows = slice(half * channels, (half + 1) * channels)
+                    grad_ref[tap, half] = jnp.transpose(here[rows] + there[rows])
 
 
 def kernel_call(body, seqs, inputs, shared, outputs, summed, scratch, flops):
@@ -585,7 +588,7 @@
         ),
         (backward_band(conv2_weight),),
         (field, low_field, table(2), pay(2), pay(2)),
-        (((27, channels, channels), wide),),
+        (((27, 1, channels, channels), wide),),
         conv_scratch(rows, channels)
         + [
             pltpu.VMEM((SUBS * channels, rows), low_type),
@@ -603,7 +606,7 @@
         ),
         (backward_band(conv1_weight), conv3_weight.T),
         (low_field, field),
-        (((27, width, channels), wide), ((width, channels), wide)),
+        (((27, 2, channels, channels), wide), ((width, channels), wide)),
         conv_scratch(rows, channels)
         + [
             pltpu.VMEM((SUBS * width, rows), low_type),
@@ -612,6 +615,210 @@
         2 * conv_flops(seqs, rows, channels, width),
     )
     return (section_out, up_grad, skip_grad, conv1_grad, conv2_grad, conv3_grad)
+
+
+PIECE_BYTES = 2400 * 1024
+
+
+def bit_count(size):
+    return size.bit_length() - 1
+
+
+def pieces_of(shapes):
+    pieces = []
+    for index, (shards, rows, lanes) in enumerate(shapes):
+        parts = max(1, round(shards * rows * lanes * 2 / PIECE_BYTES))
+        while rows % (16 * parts) != 0 and parts > 1:
+            parts -= 1
+        take = rows // parts
+        pieces.extend((index, part * take, take, lanes) for part in range(parts))
+    return pieces
+
+
+def all_of(count):
+    return (slice(None),) * count
+
+
+def reduce_kernel(pieces, arrays, tok_bits, seq_bits):
+    phases = tok_bits + seq_bits
+    mesh_id = pl.DeviceIdType.MESH
+
+    def body(*refs):
+        given = refs[:arrays]
+        results = refs[arrays : 2 * arrays]
+        count = len(pieces)
+        rest = refs[2 * arrays :]
+        kept = rest[:count]
+        landed = [rest[count + i * phases : count + (i + 1) * phases] for i in range(count)]
+        local_sem, send_sem, recv_sem = rest[count + count * phases :]
+        tok = lax.axis_index("tok")
+        seq = lax.axis_index("seq")
+
+        def bit_of(phase):
+            if phase < tok_bits:
+                return (tok // (1 << phase)) % 2
+            return (seq // (1 << (phase - tok_bits))) % 2
+
+        def partner(phase):
+            bit = bit_of(phase)
+            if phase < tok_bits:
+                return (seq, tok + (1 << phase) * (1 - 2 * bit))
+            return (seq + (1 << (phase - tok_bits)) * (1 - 2 * bit), tok)
+
+        barrier = pltpu.get_barrier_semaphore()
+        for phase in range(phases):
+            pl.semaphore_signal(barrier, inc=1, device_id=partner(phase), device_id_type=mesh_id)
+        pl.semaphore_wait(barrier, phases)
+
+        def local_copy(piece):
+            index, begin, take, _ = pieces[piece]
+            view = given[index].at[all_of(tok_bits - 1) + (bit_of(0), pl.ds(begin, take))]
+            return pltpu.make_async_copy(view, kept[piece], local_sem.at[piece])
+
+        def remote_copy(piece, phase):
+            index, begin, take, _ = pieces[piece]
+            if phase == 0:
+                view = given[index].at[all_of(tok_bits - 1) + (1 - bit_of(0), pl.ds(begin, take))]
+            elif phase < tok_bits:
+                view = landed[piece][phase - 1].at[all_of(tok_bits - 1 - phase) + (1 - bit_of(phase),)]
+            else:
+                view = landed[piece][phase - 1]
+            return pltpu.make_async_remote_copy(
+                src_ref=view,
+                dst_ref=landed[piece][phase],
+                send_sem=send_sem.at[piece, phase],
+                recv_sem=recv_sem.at[piece, phase],
+                device_id=partner(phase),
+                device_id_type=mesh_id,
+            )
+
+        def begin(piece):
+            remote_copy(piece, 0).start()
+            local_copy(piece).start()
+
+        def finish(piece, phase):
+            index, first, take, _ = pieces[piece]
+            remote_copy(piece, phase).wait_recv()
+            got = landed[piece][phase]
+            if phase == 0:
+                local_copy(piece).wait()
+
+            if phase < tok_bits:
+                kept_bits = tok_bits - 1 - phase
+
+                def step(block, carry):
+                    at = tuple((block // (1 << bit)) % 2 for bit in reversed(range(kept_bits)))
+                    if phase == 0:
+                        mine = kept[piece][at]
+                    else:
+                        mine = landed[piece][phase - 1][at + (bit_of(phase),)]
+                    got[at] = got[at] + mine
+                    return carry
+
+                lax.fori_loop(0, 1 << kept_bits, step, 0)
+            elif phase + 1 < phases:
+                got[...] = got[...] + landed[piece][phase - 1][...]
+            if phase + 1 < phases:
+                remote_copy(piece, phase + 1).start()
+            else:
+                total = got[...].astype(wide) + landed[piece][phase - 1][...].astype(wide)
+                results[index][pl.ds(first, take), :] = total
+
+        begin(0)
+        for step in range(count + phases - 1):
+            if step + 1 < count:
+                begin(step + 1)
+            for phase in range(phases):
+                if 0 <= step - phase < count:
+                    finish(step - phase, phase)
+        for piece in range(count):
+            for phase in range(phases):
+                remote_copy(piece, phase).wait_send()
+
+    return body
+
+
+def reduced(grads):
+    shards = lax.axis_size("tok")
+    tok_bits = bit_count(shards)
+    seq_bits = bit_count(lax.axis_size("seq"))
+    shapes = [g.shape for g in grads]
+    pieces = pieces_of(shapes)
+    scratch = [
+        pltpu.VMEM((2,) * (tok_bits - 1) + (take, lanes), low_type) for _, _, take, lanes in pieces
+    ]
+    for _, _, take, lanes in pieces:
+        for phase in range(tok_bits - 1):
+            bits = tok_bits - 1 - phase
+            scratch.append(pltpu.VMEM((2,) * bits + (take, lanes), low_type))
+        scratch += [pltpu.VMEM((take, lanes), low_type) for _ in range(1 + seq_bits)]
+    count, phases = len(pieces), tok_bits + seq_bits
+    scratch += [
+        pltpu.SemaphoreType.DMA((count,)),
+        pltpu.SemaphoreType.DMA((count, phases)),
+        pltpu.SemaphoreType.DMA((count, phases)),
+    ]
+    total = sum(math.prod(s) for s in shapes)
+    return pl.pallas_call(
+        reduce_kernel(pieces, len(grads), tok_bits, seq_bits),
+        in_specs=[pl.BlockSpec(memory_space=pl.ANY)] * len(grads),
+        out_specs=[pl.BlockSpec(memory_space=pltpu.VMEM)] * len(grads),
+        out_shape=[jax.ShapeDtypeStruct(s[1:], wide) for s in shapes],
+        scratch_shapes=scratch,
+        compiler_params=pltpu.CompilerParams(
+            vmem_limit_bytes=VMEM_LIMIT, collective_id=0, has_side_effects=True
+        ),
+        cost_estimate=pl.CostEstimate(flops=total, bytes_accessed=4 * total, transcendentals=0),
+    )(*[g.reshape((2,) * tok_bits + g.shape[1:]) for g in grads])
+
+
+def sharded_rows(grad):
+    shards = lax.axis_size("tok")
+    rows = grad.shape[0] // shards
+    grad = grad.astype(low_type)
+    if rows % 16 == 0:
+        return grad.reshape(shards, rows, grad.shape[1])
+    return grad.reshape(shards, rows * grad.shape[1] // 128, 128)
+
+
+def conv_rows(turned):
+    shards = lax.axis_size("tok")
+    taps, halves, channels, lanes = turned.shape
+    split = turned.reshape(taps, halves, shards, channels // shards, lanes)
+    return jnp.moveaxis(split, 2, 0).reshape(shards, -1, lanes)
+
+
+def conv_share(rows, taps, halves):
+    split = rows.reshape(taps, halves, -1, rows.shape[-1])
+    return jnp.moveaxis(split, 2, 3).reshape(taps, halves * rows.shape[-1], -1)
+
+
+def reduced_all(conv_grads, matrices, vectors):
+    shards = lax.axis_size("tok")
+    parts = [conv_rows(g) for g in conv_grads]
+    flat = jnp.concatenate([v.reshape(shards, -1) for v in vectors], axis=1)
+    used = flat.shape[1]
+    taken = sum(p.shape[1] for p in parts)
+    rows = -(-used // 128)
+    rows += -(rows + taken) % 16
+    flat = jnp.pad(flat, ((0, 0), (0, rows * 128 - used))).reshape(shards, rows, 128)
+    packed = jnp.concatenate([p.astype(low_type) for p in parts] + [flat.astype(low_type)], axis=1)
+    results = reduced([packed] + [sharded_rows(m) for m in matrices])
+    shares = []
+    cursor = 0
+    for part, grad in zip(parts, conv_grads):
+        rows_here = results[0][cursor : cursor + part.shape[1]]
+        shares.append(conv_share(rows_here, grad.shape[0], grad.shape[1]))
+        cursor += part.shape[1]
+    flat = results[0][cursor:].reshape(-1)
+    cursor = 0
+    pieces = []
+    for vector in vectors:
+        size = vector.size // shards
+        pieces.append(flat[cursor : cursor + size])
+        cursor += size
+    whole = [r.reshape(-1, m.shape[1]) for r, m in zip(results[1:], matrices)]
+    return (shares, whole, pieces)
 
 
 def crop_tables(crop_sides, inside, shape_info, first_row, row_count):
@@ -828,94 +1035,35 @@
     first_ln_pull = jax.vjp(layer_norm, token_values, ln1_gain, ln1_bias)[1]
     token_part, ln1_gain_grad, ln1_bias_grad = first_ln_pull(normed_one_grad)
     token_grad = resid_one_grad + token_part
-    weight_shares = (
-        lax.psum_scatter(
-            ln1_gain_grad.astype(jnp.bfloat16), "tok", scatter_dimension=0, tiled=True
-        ).astype(jnp.float32),
-        lax.psum_scatter(
-            ln1_bias_grad.astype(jnp.bfloat16), "tok", scatter_dimension=0, tiled=True
-        ).astype(jnp.float32),
-        lax.psum_scatter(
-            qkv_grad.astype(jnp.bfloat16), "tok", scatter_dimension=0, tiled=True
-        ).astype(jnp.float32),
-        lax.psum_scatter(
-            qv_bias_grad.astype(jnp.bfloat16), "tok", scatter_dimension=1, tiled=True
-        ).astype(jnp.float32),
-        lax.psum_scatter(
-            out_grad.astype(jnp.bfloat16), "tok", scatter_dimension=0, tiled=True
-        ).astype(jnp.float32),
-        lax.psum_scatter(
-            out_bias_grad.astype(jnp.bfloat16), "tok", scatter_dimension=0, tiled=True
-        ).astype(jnp.float32),
-        lax.psum_scatter(
-            ln2_gain_grad.astype(jnp.bfloat16), "tok", scatter_dimension=0, tiled=True
-        ).astype(jnp.float32),
-        lax.psum_scatter(
-            ln2_bias_grad.astype(jnp.bfloat16), "tok", scatter_dimension=0, tiled=True
-        ).astype(jnp.float32),
-        lax.psum_scatter(
-            fc1_grad.astype(jnp.bfloat16), "tok", scatter_dimension=0, tiled=True
-        ).astype(jnp.float32),
-        lax.psum_scatter(
-            fc1_bias_grad.astype(jnp.bfloat16), "tok", scatter_dimension=0, tiled=True
-        ).astype(jnp.float32),
-        lax.psum_scatter(
-            fc2_grad.astype(jnp.bfloat16), "tok", scatter_dimension=0, tiled=True
-        ).astype(jnp.float32),
-        lax.psum_scatter(
-            fc2_bias_grad.astype(jnp.bfloat16), "tok", scatter_dimension=0, tiled=True
-        ).astype(jnp.float32),
-        lax.psum_scatter(
-            deconv_grad.astype(jnp.bfloat16), "tok", scatter_dimension=0, tiled=True
-        ).astype(jnp.float32),
-        lax.psum_scatter(
-            conv1_grad.astype(jnp.bfloat16), "tok", scatter_dimension=2, tiled=True
-        ).astype(jnp.float32),
-        lax.psum_scatter(
-            conv2_grad.astype(jnp.bfloat16), "tok", scatter_dimension=2, tiled=True
-        ).astype(jnp.float32),
-        lax.psum_scatter(
-            conv3_grad.astype(jnp.bfloat16), "tok", scatter_dimension=1, tiled=True
-        ).astype(jnp.float32),
-    )
-    finished = (
-        lax.psum(weight_shares[0].astype(jnp.bfloat16), "seq").astype(jnp.float32),
-        lax.psum(weight_shares[1].astype(jnp.bfloat16), "seq").astype(jnp.float32),
-        lax.psum(weight_shares[2].astype(jnp.bfloat16), "seq").astype(jnp.float32),
-        lax.psum(weight_shares[3].astype(jnp.bfloat16), "seq").astype(jnp.float32),
-        lax.psum(weight_shares[4].astype(jnp.bfloat16), "seq").astype(jnp.float32),
-        lax.psum(weight_shares[5].astype(jnp.bfloat16), "seq").astype(jnp.float32),
-        lax.psum(weight_shares[6].astype(jnp.bfloat16), "seq").astype(jnp.float32),
-        lax.psum(weight_shares[7].astype(jnp.bfloat16), "seq").astype(jnp.float32),
-        lax.psum(weight_shares[8].astype(jnp.bfloat16), "seq").astype(jnp.float32),
-        lax.psum(weight_shares[9].astype(jnp.bfloat16), "seq").astype(jnp.float32),
-        lax.psum(weight_shares[10].astype(jnp.bfloat16), "seq").astype(jnp.float32),
-        lax.psum(weight_shares[11].astype(jnp.bfloat16), "seq").astype(jnp.float32),
-        lax.psum(weight_shares[12].astype(jnp.bfloat16), "seq").astype(jnp.float32),
-        lax.psum(weight_shares[13].astype(jnp.bfloat16), "seq").astype(jnp.float32),
-        lax.psum(weight_shares[14].astype(jnp.bfloat16), "seq").astype(jnp.float32),
-        lax.psum(weight_shares[15].astype(jnp.bfloat16), "seq").astype(jnp.float32),
+    conv3_turned = jnp.moveaxis(conv3_grad.reshape(1, 2, channels, channels), 2, 3)
+    conv_shares, shares, vectors = reduced_all(
+        (conv1_grad, conv2_grad, conv3_turned),
+        (deconv_grad, fc2_grad, fc1_grad, out_grad, qkv_grad),
+        (
+            ln1_gain_grad, ln1_bias_grad, qv_bias_grad[0], qv_bias_grad[1], out_bias_grad,
+            ln2_gain_grad, ln2_bias_grad, fc1_bias_grad, fc2_bias_grad,
+        ),
     )
     return (
         section_out,
         token_grad,
         skip_grad,
-        finished[0],
-        finished[1],
-        finished[2],
-        finished[3],
-        finished[4],
-        finished[5],
-        finished[6],
-        finished[7],
-        finished[8],
-        finished[9],
-        finished[10],
-        finished[11],
-        finished[12],
-        finished[13],
-        finished[14],
-        finished[15],
+        vectors[0],
+        vectors[1],
+        shares[4],
+        jnp.stack([vectors[2], vectors[3]]),
+        shares[3],
+        vectors[4],
+        vectors[5],
+        vectors[6],
+        shares[2],
+        vectors[7],
+        shares[1],
+        vectors[8],
+        shares[0],
+        conv_shares[0],
+        conv_shares[1],
+        conv_shares[2][0],
     )
 
 

time: 1100 us -> 816 us (0.74)
  waiting for transfers between devices: 357 us -> 27 us
  Pallas kernels: 132 us -> 277 us
  blocking collectives: 63.6 us -> 0 us
  other arithmetic: 178 us -> 157 us
  between operations: 16.9 us -> 2.07 us
    reduce_scatter x7 -> x0, waiting for transfers between devices: 306 us -> none  [the longest x1 78.5 us: local(): lax.psum_scatter(fc2_grad.astype(jnp.bfloat16), 'tok', scatter_dimension=...]
    pallas_call x0 -> x1, Pallas kernels: none -> 144 us  [reduced(): pl.pallas_call(reduce_kernel(pieces, len(grads), tok_bits, seq_bits), in_...]
    unnamed x1 -> x0, blocking collectives: 53.1 us -> none
    psum x1 -> x0, waiting for transfers between devices: 24 us -> none  [local(): lax.psum(weight_shares[13].astype(jnp.bfloat16), 'seq').astype(jnp.float32)]
    convert_element_type x16 -> x2, other arithmetic: 20.7 us -> 1.66 us  [reduced_all(): p.astype(low_type)]
    unnamed x146 -> x176, local copies, waits for them, and re-layouts: 33.5 us -> 17.4 us
    reshape x0 -> x10, local copies, waits for them, and re-layouts: none -> 11.3 us  [the longest x7 7.49 us: reduced_all(): flat = jnp.concatenate([v.reshape(shards, -1) for v in vectors], axis=1)]
  transfers between devices with their start and end apart: 30 -> 20, of which waited for: 13 -> 7; matrix products, arithmetic and copies ran while one was open for 37% -> 29% of each run, Pallas kernels for 0% -> 0%
where the time goes in v2:
time: 816 us; the launch traced here: 803 us
  Pallas kernels  277 us (34%)
  matrix products  169 us (21%)
  other arithmetic  157 us (19%)
  local copies, waits for them, and re-layouts  115 us (14%)
  starting transfers between devices  56.2 us (7%)
  waiting for transfers between devices  27 us (3%)
    pallas_call x1, Pallas kernels, reduced(): pl.pallas_call(reduce_kernel(pieces, len(grads), tok_bits, seq_bits), in_...  144 us
    pallas_call x5, Pallas kernels, kernel_call(): pl.pallas_call(body, grid=(seqs,), in_specs=[row_spec(a.shape) for a in i...  133 us
    ppermute x20, starting transfers between devices, passed_along(): return lax.ppermute(block, axis, route)  56.2 us
    select_n x4, other arithmetic, crop_tables(): columns.append(jnp.where(in_crop(shape_info, offset), own + step, -1))  31.4 us
    ppermute x20, waiting for transfers between devices, passed_along(): return lax.ppermute(block, axis, route)  27 us
    convert_element_type x1, other arithmetic, local(): score_low = (attn_probs * (probs_grad - row_inner)).astype(jnp.bfloat16)  24 us
    convert_element_type x1, other arithmetic, local(): act_low = jax.nn.gelu(pre_act, approximate=False).astype(jnp.bfloat16)  23.3 us
    dot_general x1, matrix products, local(): jnp.einsum('sqhd,skhd->shqk', attended_grad, window_values, preferred_ele...  22.7 us
  transfers between devices with their start and end apart: 20, of which 7 were waited for; matrix products, arithmetic and copies ran while one was open for 29% of the time, Pallas kernels for 0%

profile of v2, /device:TPU:30, one launch (start us, length us, event | category | flops | bytes accessed | tf_op | source)
XLA Modules:
  0.0 803.1 jit_solution(5377298674219790848)
XLA Ops:
  4.9 5.3 add_convert_fusion.1
  14.2 3.4 collective-permute-start.2
  19.7 3.2 collective-permute-start
  23.0 3.7 reshape.2225.skip
  41.2 18.2 %add_select_fusion.4 = (s32[3,256,1]{2,1,0:T(8,128)}, pred[3,256,1]{2,1,0:T(8,128)(4,1)S(1)}, pred[3,256,1]{2,1,0:T(8,128)(4,1)S(1)}, pred[3,256,1]{2,1,0:T(8,12...) fusion(s32[256]{0:T(256)} %get-tuple-element.309, ...), kind=kLoop, calls=%fused_computation.130 | loop fusion | flops 39936 | bytes 22784 | tf_op jit(solution)/shard_map/jit(_where)/select_n | solution.py:832
  59.4 7.9 add_select_fusion.13
  69.1 3.6 add_select_fusion.9
  75.7 7.3 stack.8.place
  86.3 3.9 fusion.18
  90.2 2.7 collective-permute-start.6
  93.0 3.5 pad_maximum_fusion.1
  96.4 6.1 copy.182
  102.5 3.5 pad_maximum_fusion
  106.0 6.1 copy.180
  112.0 14.2 %fusion.6 = (f32[3,12,256]{2,1,0:T(8,128)S(1)}, f32[3,12,256,768]{3,2,1,0:T(8,128)}) fusion(pred[3,256,768]{2,1,0:T(8,128)(4,1)} %broadcast_compare_fusion, bf16[3,256,12,64]{1,3,2,0:T(8,128)(2,1)} %bitcast.164, bf16[3,768,12,64]{1,3,2,0:T(8,128)(2,1)} %bitcast.159), kind=kOutput, calls=%fused_computation.12 | convolution fusion | flops 927194112 | bytes 33656832 | tf_op jit(solution)/shard_map/sqhd,skhd->shqk/dot_general | solution.py:93
  126.3 14.7 %fusion = f32[3,12,256]{2,1,0:T(8,128)S(1)} fusion(f32[3,12,256]{2,1,0:T(8,128)S(1)} %get-tuple-element.296, f32[3,12,256,768]{3,2,1,0:T(8,128)} %get-tuple-element.297, pred[3,256,768]{2,1,0:T(8,128)(4,1)S(1)} %copy-done.4), kind=kLoop, calls=%fused_computation.6 | loop fusion | flops 28302336 | bytes 28975104 | tf_op jit(solution)/shard_map/reduce_sum | solution.py:918
  141.0 13.7 %fusion.58 = bf16[3,12,64,256]{3,2,1,0:T(8,128)(2,1)S(1)} fusion(bf16[3,768,12,64]{1,3,2,0:T(8,128)(2,1)S(1)} %bitcast.163, f32[3,12,256]{2,1,0:T(8,128)S(1)} %fusion, f32[3,12,256]{2,1,0:T(8,128)S(1)} %get-tuple-element.296, f32[3,12,256,768]{3,2,1,0:T(8,128)} %get-tuple-element.297, pred[3,256,768]{2,1,0:T(8,128)(4,1)S(1)} %copy-done.4), kind=kOutput, calls=%fused_computation.112 | convolution fusion | flops 941948928 | bytes 33693696 | tf_op jit(solution)/shard_map/shqk,skhd->sqhd/dot_general | solution.py:921
  157.2 6.5 fusion.52
  163.7 23.3 %multiply_convert_fusion.1 = (bf16[3,256,3072]{2,1,0:T(8,128)(2,1)S(1)}, f32[3,256,3072]{2,1,0:T(8,128)}) fusion(f32[3,256,3072]{2,1,0:T(8,128)S(1)} %get-tuple-element.300, f32[3072]{0:T(1024)S(1)} %copy-done.50, u8[256,3072]{1,0:T(8,128)(4,1)S(1)} %get-tuple-element.164, u8[256,3072]{1,0:T(8,128)(4,1)S(1)} %get-tuple-element.163), kind=kLoop, calls=%fused_computation.26 | loop fusion | flops 167510016 | bytes 25178112 | tf_op jit(solution)/shard_map/convert_element_type | solution.py:935
  187.1 3.8 add_convert_fusion.2
  192.5 2.9 collective-permute-start.5
  199.5 3.8 collective-permute-done.4.up_left
  204.1 27.2 %shard_map.359 = (f32[3,256,1024]{2,1,0:T(8,128)}, f32[3,256,1024]{2,1,0:T(8,128)}, f32[3,48,512]{2,1,0:T(8,128)}, bf16[3,48,1536]{2,1,0:T(8,128)(2,1)}, bf16[3,48,1536]{2,1,0:T(8,128)(2,1)}) custom-call(bf16[3,256,1024]{2,1,0:T(8,128)(2,1)} %copy-done.27, bf16[3,48,1024]{2,1,0:T(8,128)(2,1)} %copy-done.67, bf16[3,48,1024]{2,1,0:T(8,128)(2,1)} %copy-done.66, ...), custom_call_target="tpu_custom_call" | custom-call | flops 20132659200 | bytes 16737280 | tf_op jit(solution)/shard_map/pallas_call | solution.py:223
  233.2 3.6 collective-permute-start.9
  239.2 4.0 copy.198
  245.5 3.7 reshape.2230.cotangent
  249.2 3.0 reverse_bitcast_fusion
  254.7 18.7 %shard_map.360 = (f32[3,256,1024]{2,1,0:T(8,128)}, f32[3,48,512]{2,1,0:T(8,128)}, f32[3,48,256]{2,1,0:T(8,128)}, bf16[3,48,1280]{2,1,0:T(8,128)(2,1)}, bf16[3,48,1280]{2,1,0:T(8,128)(2,1)}) custom-call(f32[3,256,1024]{2,1,0:T(8,128)} %get-tuple-element.131.first, bf16[3,48,1536]{2,1,0:T(8,128)(2,1)} %collective-permute-done.8.left_pay.first_left, ...), custom_call_target="tpu_custom_call" | custom-call | flops 10066329600 | bytes 11341824 | tf_op jit(solution)/shard_map/pallas_call | solution.py:223
  275.3 5.2 collective-permute-start.11
  284.0 5.8 collective-permute-done.11.right_pay.second_right
  289.8 8.0 shard_map.361
  299.7 3.8 collective-permute-start.13
  303.6 4.1 fusion.17
  307.6 3.9 collective-permute-done.13.grad_right
  312.2 32.0 %shard_map.362 = (f32[3,256,1024]{2,1,0:T(8,128)}, bf16[3,256,1024]{2,1,0:T(8,128)(2,1)}, f32[3,48,256]{2,1,0:T(8,128)}, bf16[3,48,1280]{2,1,0:T(8,128)(2,1)}, b...) custom-call(f32[3,256,1024]{2,1,0:T(8,128)} %get-tuple-element.142.grad, bf16[3,48,1408]{2,1,0:T(8,128)(2,1)} %copy-done.63, ...), custom_call_target="tpu_custom_call" | custom-call | flops 20132659200 | bytes 24858624 | tf_op jit(solution)/shard_map/pallas_call | solution.py:223
  346.3 3.7 collective-permute-start.15
  350.7 3.0 copy.219
  355.8 47.1 %shard_map.363 = (bf16[3,256,1024]{2,1,0:T(8,128)(2,1)}, f32[3,256,1024]{2,1,0:T(8,128)}, f32[27,2,128,128]{3,2,1,0:T(8,128)}, f32[256,128]{1,0:T(8,128)}) custom-call(f32[3,256,1024]{2,1,0:T(8,128)} %get-tuple-element.147.grad, bf16[3,48,1280]{2,1,0:T(8,128)(2,1)} %copy-done.65, bf16[3,48,1280]{2,1,0:T(8,128)(2,1)} %collective-permute-done.15.grad_right, ...), custom_call_target="tpu_custom_call" | custom-call | flops 34628173824 | bytes 26505216 | tf_op jit(solution)/shard_map/pallas_call | solution.py:223
  403.0 4.5 bitcast_convert_fusion.3
  409.0 13.5 %fusion.93 = (bf16[3072]{0:T(1024)(128)(2,1)}, bf16[3,256,3072]{2,1,0:T(8,128)(2,1)}) fusion(f32[3,256,3072]{2,1,0:T(8,128)} %get-tuple-element.220, bf16[3072,768]{1,0:T(8,128)(2,1)S(1)} %bitcast.200, f32[3,256,768]{2,1,0:T(8,128)S(1)} %fusion.53, f32[3,256,3072]{2,1,0:T(8,128)} %copy-done.9, f32[3072]{0:T(1024)S(1)} %copy-done.51), kind=kOutput, calls=%fused_computation.247 | convolution fusion | flops 3662214144 | bytes 30689280 | tf_op jit(solution)/shard_map/std,fd->stf/dot_general | solution.py:964
  422.5 8.4 %multiply_reduce_fusion.1 = (bf16[768]{0:T(1024)(128)(2,1)}, f32[3,256]{1,0:T(4,128)S(1)}, bf16[768]{0:T(1024)(128)(2,1)}, f32[3,256,768]{2,1,0:T(8,128)S(1)}) fusion(f32[3,256,768]{2,1,0:T(8,128)S(1)} %copy-done.8, f32[3,256]{1,0:T(4,128)S(1)} %fusion.70, f32[3,256]{1,0:T(4,128)S(1)} %broadcast_multiply_fusion.1, f32[768]{0:T(1024)S(1)} %copy-done.55, ...), kind=kOutput, calls=%fused_computation.95 | convolution fusion | flops 3628594944 | bytes 14171136 | tf_op jit(solution)/shard_map/stf,df->std/dot_general | solution.py:969
  430.9 6.3 bitcast_convert_fusion
  445.5 18.9 %fusion.2 = f32[3,12,64,768]{3,2,1,0:T(8,128)} fusion(bf16[3,256,12,64]{1,3,2,0:T(8,128)(2,1)} %bitcast.175, f32[3,12,256]{2,1,0:T(8,128)} %log_add_fusion, f32[3,12,256,768]{3,2,1,0:T(8,128)} %get-tuple-element.297, pred[3,256,768]{2,1,0:T(8,128)(4,1)} %broadcast_compare_fusion), kind=kOutput, calls=%fused_computation.8 | convolution fusion | flops 934281216 | bytes 37195776 | tf_op jit(solution)/shard_map/shqk,sqhd->skhd/dot_general | solution.py:1000
  464.4 22.7 %multiply_reduce_fusion = (f32[3,12,256]{2,1,0:T(8,128)S(1)}, f32[3,12,256,768]{3,2,1,0:T(8,128)}) fusion(f32[3,12,256]{2,1,0:T(8,128)S(1)} %copy-done.24, f32[3,12,256,768]{3,2,1,0:T(8,128)} %get-tuple-element.297, pred[3,256,768]{2,1,0:T(8,128)(4,1)S(1)} %copy-done.5, bf16[3,256,12,64]{1,3,2,0:T(8,128)(2,1)S(1)} %bitcast.176, ...), kind=kOutput, calls=%fused_computation.1 | convolution fusion | flops 941349888 | bytes 62005248 | tf_op jit(solution)/shard_map/sqhd,skhd->shqk/dot_general | solution.py:987
  487.1 24.0 %multiply_convert_fusion = bf16[3,12,256,768]{3,2,1,0:T(8,128)(2,1)} fusion(f32[3,12,256,768]{3,2,1,0:T(8,128)} %get-tuple-element.303, f32[3,12,256]{2,1,0:T(8,128)S(1)} %get-tuple-element.302, f32[3,12,256]{2,1,0:T(8,128)S(1)} %copy-done.24, f32[3,12,256,768]{3,2,1,0:T(8,128)} %get-tuple-element.297, pred[3,256,768]{2,1,0:T(8,128)(4,1)S(1)} %copy-done.5), kind=kLoop, calls=%fused_computation | loop fusion | flops 42467328 | bytes 71442432 | tf_op jit(solution)/shard_map/convert_element_type | solution.py:991
  511.1 11.5 %multiply_convert_fusion.2 = bf16[3,12,64,256]{3,2,1,0:T(8,128)(2,1)} fusion(bf16[3,768,12,64]{1,3,2,0:T(8,128)(2,1)} %bitcast.160, bf16[3,12,256,768]{3,2,1,0:T(8,128)(2,1)} %multiply_convert_fusion), kind=kOutput, calls=%fused_computation.97 | convolution fusion | flops 907149312 | bytes 18874368 | tf_op jit(solution)/shard_map/shqk,skhd->sqhd/dot_general | solution.py:993
  522.6 10.9 %broadcast_multiply_fusion = f32[3,12,64,768]{3,2,1,0:T(8,128)} fusion(bf16[3,256,12,64]{1,3,2,0:T(8,128)(2,1)} %bitcast.165, bf16[3,12,256,768]{3,2,1,0:T(8,128)(2,1)} %multiply_convert_fusion), kind=kOutput, calls=%fused_computation.66 | convolution fusion | flops 907739136 | bytes 22413312 | tf_op jit(solution)/shard_map/shqk,sqhd->skhd/dot_general | solution.py:997
  535.0 8.2 %copy.203 = f32[3,768,768]{2,1,0:T(8,128)} copy(f32[3,768,768]{1,2,0:T(8,128)} %bitcast.166) | data formatting | bytes 14155776 | tf_op jit(solution)/shard_map/reshape | solution.py:1004
  543.2 3.4 convert.63
  548.1 3.8 collective-permute-start.18
  553.9 8.1 %copy.201 = f32[3,768,768]{2,1,0:T(8,128)} copy(f32[3,768,768]{1,2,0:T(8,128)} %bitcast.161) | data formatting | bytes 14155776 | tf_op jit(solution)/shard_map/reshape | solution.py:1003
  562.0 3.4 convert.61
  574.8 3.0 copy.206
  584.3 3.6 collective-permute-start.16
  590.0 3.7 bitcast_convert_fusion.4
  593.7 8.0 bitcast_convert_fusion.1
  601.8 2.7 fusion.48
  604.5 10.1 %collective-permute-done.16 = bf16[3,256,768]{2,1,0:T(8,128)(2,1)S(1)} collective-permute-done((bf16[3,256,768]{2,1,0:T(8,128)(2,1)}, bf16[3,256,768]{2,1,0:T(8,128)(2,1)S(1)}, u32[]{:S(2)}, u32[]{:S(2)}) %collective-permute-start.16) | collective-permute-done | bytes 1179680 | tf_op jit(solution)/shard_map/ppermute | solution.py:30
  617.4 5.0 fusion.80
  622.5 5.6 bitcast_convert_fusion.2
  632.8 3.7 fusion.41
  640.1 3.0 pad_maximum_fusion.3.refs_0_
  643.1 144.0 %shard_map.364 = (f32[672,128]{1,0:T(8,128)}, f32[48,1024]{1,0:T(8,128)}, f32[192,768]{1,0:T(8,128)}, f32[48,3072]{1,0:T(8,128)}, f32[48,768]{1,0:T(8,128)}, /*index=5*/f32[48,2304]{1,0:T(8,128)}) custom-call(bf16[2,2,2,2,672,128]{5,4,3,2,1,0:T(8,128)(2,1)} %pad_maximum_fusion.3.refs_0_, bf16[2,2,2,2,48,1024]{5,4,3,2,1,0:T(8,128)(2,1)} %bitcast.185, ...), custom_call_target="tpu_custom_call" | custom-call | flops 9240576 | bytes 36962304 | tf_op jit(solution)/shard_map/pallas_call | solution.py:762
  793.5 5.0 add_add_fusion.2
  (289 shorter events, 118.2 us)
Async XLA Ops:
  2.3 7.9 copy-start.33
  12.1 20.6 %copy-start.43 = (s32[3,45]{1,0:T(4,128)S(1)}, s32[3,45]{1,0:T(4,128)}, u32[]{:S(2)}) copy-start(s32[3,45]{1,0:T(4,128)} %param.38) | copy-start | bytes 1624
  12.1 78.1 %collective-permute-start.3 = (bf16[3,256,768]{2,1,0:T(8,128)(2,1)}, bf16[3,256,768]{2,1,0:T(8,128)(2,1)}, u32[]{:S(2)}, u32[]{:S(2)}) collective-permute-start(bf16[3,256,768]{2,1,0:T(8,128)(2,1)} %get-tuple-element.225), channel_id=1, source_target_pairs={{1,0},{2,1},{3,2},{4,3},{5,4},{6,5},{7,6},{8,7},{9,8},{10,9},{11,1... | collective-permute-start | bytes 3538952 | tf_op jit(solution)/shard_map/ppermute | solution.py:30
  14.2 78.8 %collective-permute-start.2 = (bf16[3,256,768]{2,1,0:T(8,128)(2,1)}, bf16[3,256,768]{2,1,0:T(8,128)(2,1)}, u32[]{:S(2)}, u32[]{:S(2)}) collective-permute-start(bf16[3,256,768]{2,1,0:T(8,128)(2,1)} %get-tuple-element.225), channel_id=1, source_target_pairs={{0,1},{1,2},{2,3},{3,4},{4,5},{5,6},{6,7},{7,8},{8,9},{9,10},{10,1... | collective-permute-start | bytes 3538952 | tf_op jit(solution)/shard_map/ppermute | solution.py:30
  17.6 84.9 %collective-permute-start.1 = (bf16[3,256,768]{2,1,0:T(8,128)(2,1)}, bf16[3,256,768]{2,1,0:T(8,128)(2,1)}, u32[]{:S(2)}, u32[]{:S(2)}) collective-permute-start(bf16[3,256,768]{2,1,0:T(8,128)(2,1)} %get-tuple-element.227), channel_id=1, source_target_pairs={{1,0},{2,1},{3,2},{4,3},{5,4},{6,5},{7,6},{8,7},{9,8},{10,9},{11,1... | collective-permute-start | bytes 3538952 | tf_op jit(solution)/shard_map/ppermute | solution.py:30
  19.7 82.8 %collective-permute-start = (bf16[3,256,768]{2,1,0:T(8,128)(2,1)}, bf16[3,256,768]{2,1,0:T(8,128)(2,1)}, u32[]{:S(2)}, u32[]{:S(2)}) collective-permute-start(bf16[3,256,768]{2,1,0:T(8,128)(2,1)} %get-tuple-element.227), channel_id=1, source_target_pairs={{0,1},{1,2},{2,3},{3,4},{4,5},{5,6},{6,7},{7,8},{8,9},{9,10},{10,1... | collective-permute-start | bytes 3538952 | tf_op jit(solution)/shard_map/ppermute | solution.py:30
  28.6 168.8 %collective-permute-start.7 = (bf16[3,48,1024]{2,1,0:T(8,128)(2,1)}, bf16[3,48,1024]{2,1,0:T(8,128)(2,1)}, u32[]{:S(2)}, u32[]{:S(2)}) collective-permute-start(bf16[3,48,1024]{2,1,0:T(8,128)(2,1)} %get-tuple-element.229), channel_id=1, source_target_pairs={{1,0},{2,1},{3,2},{4,3},{5,4},{6,5},{7,6},{8,7},{9,8},{10,9},{11,1... | collective-permute-start | bytes 884744 | tf_op jit(solution)/shard_map/ppermute | solution.py:30
  59.4 7.9 copy-start.44
  59.4 7.9 copy-start.57
  59.4 9.7 %copy-start.58 = (s32[256]{0:T(256)S(1)}, s32[256]{0:T(256)}, u32[]{:S(2)}) copy-start(s32[256]{0:T(256)} %iota_add_fusion.2) | copy-start | bytes 3076
  90.2 107.2 %collective-permute-start.6 = (bf16[3,48,1024]{2,1,0:T(8,128)(2,1)}, bf16[3,48,1024]{2,1,0:T(8,128)(2,1)}, u32[]{:S(2)}, u32[]{:S(2)}) collective-permute-start(bf16[3,48,1024]{2,1,0:T(8,128)(2,1)} %get-tuple-element.230), channel_id=1, source_target_pairs={{0,1},{1,2},{2,3},{3,4},{4,5},{5,6},{6,7},{7,8},{8,9},{9,10},{10,1... | collective-permute-start | bytes 884744 | tf_op jit(solution)/shard_map/ppermute | solution.py:30
  112.0 14.2 %copy-start.4 = (pred[3,256,768]{2,1,0:T(8,128)(4,1)S(1)}, pred[3,256,768]{2,1,0:T(8,128)(4,1)}, u32[]{:S(2)}) copy-start(pred[3,256,768]{2,1,0:T(8,128)(4,1)} %broadcast_compare_fusion) | copy-start | bytes 1769476
  126.2 14.7 %copy-start.22 = (f32[3,12,256]{2,1,0:T(8,128)}, f32[3,12,256]{2,1,0:T(8,128)S(1)}, u32[]{:S(2)}) copy-start(f32[3,12,256]{2,1,0:T(8,128)S(1)} %get-tuple-element.296) | copy-start | bytes 110596
  126.2 14.7 %copy-start.6 = (bf16[3,768,768]{1,2,0:T(8,128)(2,1)S(1)}, bf16[3,768,768]{1,2,0:T(8,128)(2,1)}, u32[]{:S(2)}) copy-start(bf16[3,768,768]{1,2,0:T(8,128)(2,1)} %copy.180) | copy-start | bytes 10616836
  126.2 30.9 %slice-start.4 = ((s8[4718592]{0:T(1024)(128)(4,1)}), s8[4194304]{0:T(1024)(128)(4,1)S(1)}, s32[]{:S(2)}) async-start(s8[4718592]{0:T(1024)(128)(4,1)} %bitcast.201), calls=%async_computation.4 | async-start | bytes 8388608
  140.9 13.7 %copy-start.28 = (f32[3,12,256]{2,1,0:T(8,128)}, f32[3,12,256]{2,1,0:T(8,128)S(1)}, u32[]{:S(2)}) copy-start(f32[3,12,256]{2,1,0:T(8,128)S(1)} %fusion) | copy-start | bytes 110596
  141.0 13.7 %copy-start.2 = (bf16[3,256,768]{2,1,0:T(8,128)(2,1)S(1)}, bf16[3,256,768]{2,1,0:T(8,128)(2,1)}, u32[]{:S(2)}) copy-start(bf16[3,256,768]{2,1,0:T(8,128)(2,1)} %param.36) | copy-start | bytes 3538948
  141.0 13.7 %copy-start.61 = (bf16[768,768]{1,0:T(8,128)(2,1)S(1)}, bf16[768,768]{1,0:T(8,128)(2,1)}, u32[]{:S(2)}) copy-start(bf16[768,768]{1,0:T(8,128)(2,1)} %param.43) | copy-start | bytes 3538948
  141.0 13.7 %copy-start.68 = (f32[768]{0:T(1024)S(1)}, f32[768]{0:T(1024)}, u32[]{:S(2)}) copy-start(f32[768]{0:T(1024)} %param.44) | copy-start | bytes 9220
  141.0 16.1 %slice-start.5 = ((s8[4718592]{0:T(1024)(128)(4,1)}), s8[524288]{0:T(1024)(128)(4,1)S(1)}, s32[]{:S(2)}) async-start(s8[4718592]{0:T(1024)(128)(4,1)} %bitcast.201), calls=%async_computation.5 | async-start | bytes 1048576
  154.8 32.3 %slice-start = ((s8[4718592]{0:T(1024)(128)(4,1)}), s8[4194304]{0:T(1024)(128)(4,1)S(1)}, s32[]{:S(2)}) async-start(s8[4718592]{0:T(1024)(128)(4,1)} %bitcast.197), calls=%async_computation | async-start | bytes 8388608
  156.1 30.9 %copy-start.7 = (f32[3,256,768]{2,1,0:T(8,128)}, f32[3,256,768]{2,1,0:T(8,128)S(1)}, u32[]{:S(2)}) copy-start(f32[3,256,768]{2,1,0:T(8,128)S(1)} %get-tuple-element.299) | copy-start | bytes 7077892
  157.2 29.9 %slice-start.1 = ((s8[4718592]{0:T(1024)(128)(4,1)}), s8[524288]{0:T(1024)(128)(4,1)S(1)}, s32[]{:S(2)}) async-start(s8[4718592]{0:T(1024)(128)(4,1)} %bitcast.197), calls=%async_computation.1 | async-start | bytes 1048576
  163.7 23.3 %copy-start.9 = (f32[3,256,3072]{2,1,0:T(8,128)}, f32[3,256,3072]{2,1,0:T(8,128)S(1)}, u32[]{:S(2)}) copy-start(f32[3,256,3072]{2,1,0:T(8,128)S(1)} %get-tuple-element.300) | copy-start | bytes 28311556
  163.7 23.4 %copy-start.69 = (f32[768]{0:T(1024)S(1)}, f32[768]{0:T(1024)}, u32[]{:S(2)}) copy-start(f32[768]{0:T(1024)} %param.50) | copy-start | bytes 9220
  192.4 11.0 %copy-start.27 = (bf16[3,256,1024]{2,1,0:T(8,128)(2,1)}, bf16[3,256,1024]{2,1,0:T(8,128)(2,1)S(1)}, u32[]{:S(2)}) copy-start(bf16[3,256,1024]{2,1,0:T(8,128)(2,1)S(1)} %convolution_convert_fusion.up) | copy-start | bytes 4718596
  192.5 7.1 collective-permute-start.5
  195.3 8.0 %collective-permute-start.4 = (bf16[3,48,1024]{2,1,0:T(8,128)(2,1)S(1)}, bf16[3,48,1024]{2,1,0:T(8,128)(2,1)S(1)}, u32[]{:S(2)}, u32[]{:S(2)}) collective-permute-start(bf16[3,48,1024]{2,1,0:T(8,128)(2,1)S(1)} %get-tuple-element.232), channel_id=1, source_target_pairs={{0,1},{1,2},{2,3},{3,4},{4,5},{5,6},{6,7},{7,8},{8,9},{9,10},{10,1... | collective-permute-start | bytes 884744 | tf_op jit(solution)/shard_map/ppermute | solution.py:30
  231.3 22.7 %collective-permute-start.8 = (bf16[3,48,1536]{2,1,0:T(8,128)(2,1)}, bf16[3,48,1536]{2,1,0:T(8,128)(2,1)}, u32[]{:S(2)}, u32[]{:S(2)}) collective-permute-start(bf16[3,48,1536]{2,1,0:T(8,128)(2,1)} %get-tuple-element.132), channel_id=1, source_target_pairs={{0,1},{1,2},{2,3},{3,4},{4,5},{5,6},{6,7},{7,8},{8,9},{9,10},{10,1... | collective-permute-start | bytes 1327112 | tf_op jit(solution)/shard_map/ppermute | solution.py:30
  233.2 20.7 %collective-permute-start.9 = (bf16[3,48,1536]{2,1,0:T(8,128)(2,1)}, bf16[3,48,1536]{2,1,0:T(8,128)(2,1)}, u32[]{:S(2)}, u32[]{:S(2)}) collective-permute-start(bf16[3,48,1536]{2,1,0:T(8,128)(2,1)} %get-tuple-element.133), channel_id=1, source_target_pairs={{1,0},{2,1},{3,2},{4,3},{5,4},{6,5},{7,6},{8,7},{9,8},{10,9},{11,1... | collective-permute-start | bytes 1327112 | tf_op jit(solution)/shard_map/ppermute | solution.py:30
  239.2 9.9 %copy-start.52 = (f32[3,45]{1,0:T(4,128)S(1)}, f32[3,45]{1,0:T(4,128)}, u32[]{:S(2)}) copy-start(f32[3,45]{1,0:T(4,128)} %maximum_divide_fusion) | copy-start | bytes 1624
  273.4 10.6 %collective-permute-start.10 = (bf16[3,48,1280]{2,1,0:T(8,128)(2,1)}, bf16[3,48,1280]{2,1,0:T(8,128)(2,1)S(1)}, u32[]{:S(2)}, u32[]{:S(2)}) collective-permute-start(bf16[3,48,1280]{2,1,0:T(8,128)(2,1)} %get-tuple-element.138), channel_id=1, source_target_pairs={{0,1},{1,2},{2,3},{3,4},{4,5},{5,6},{6,7},{7,8},{8,9},{9,10},{10,1... | collective-permute-start | bytes 1105928 | tf_op jit(solution)/shard_map/ppermute | solution.py:30
  275.3 14.5 %collective-permute-start.11 = (bf16[3,48,1280]{2,1,0:T(8,128)(2,1)}, bf16[3,48,1280]{2,1,0:T(8,128)(2,1)}, u32[]{:S(2)}, u32[]{:S(2)}) collective-permute-start(bf16[3,48,1280]{2,1,0:T(8,128)(2,1)} %get-tuple-element.139), channel_id=1, source_target_pairs={{1,0},{2,1},{3,2},{4,3},{5,4},{6,5},{7,6},{8,7},{9,8},{10,9},{11,1... | collective-permute-start | bytes 1105928 | tf_op jit(solution)/shard_map/ppermute | solution.py:30
  297.8 9.8 %collective-permute-start.12 = (bf16[3,48,1408]{2,1,0:T(8,128)(2,1)}, bf16[3,48,1408]{2,1,0:T(8,128)(2,1)S(1)}, u32[]{:S(2)}, u32[]{:S(2)}) collective-permute-start(bf16[3,48,1408]{2,1,0:T(8,128)(2,1)} %get-tuple-element.143), channel_id=1, source_target_pairs={{0,1},{1,2},{2,3},{3,4},{4,5},{5,6},{6,7},{7,8},{8,9},{9,10},{10,1... | collective-permute-start | bytes 1216520 | tf_op jit(solution)/shard_map/ppermute | solution.py:30
  299.7 11.7 %collective-permute-start.13 = (bf16[3,48,1408]{2,1,0:T(8,128)(2,1)}, bf16[3,48,1408]{2,1,0:T(8,128)(2,1)S(1)}, u32[]{:S(2)}, u32[]{:S(2)}) collective-permute-start(bf16[3,48,1408]{2,1,0:T(8,128)(2,1)} %get-tuple-element.144), channel_id=1, source_target_pairs={{1,0},{2,1},{3,2},{4,3},{5,4},{6,5},{7,6},{8,7},{9,8},{10,9},{11,1... | collective-permute-start | bytes 1216520 | tf_op jit(solution)/shard_map/ppermute | solution.py:30
  312.2 37.8 %copy-start.23 = (f32[3,12,256]{2,1,0:T(8,128)S(1)}, f32[3,12,256]{2,1,0:T(8,128)}, u32[]{:S(2)}) copy-start(f32[3,12,256]{2,1,0:T(8,128)} %copy-done.22) | copy-start | bytes 110596
  312.2 37.8 %copy-start.29 = (f32[3,12,256]{2,1,0:T(8,128)S(1)}, f32[3,12,256]{2,1,0:T(8,128)}, u32[]{:S(2)}) copy-start(f32[3,12,256]{2,1,0:T(8,128)} %copy-done.28) | copy-start | bytes 110596
  344.2 9.5 %copy-start.18 = (f32[27,1,128,128]{3,2,1,0:T(8,128)S(1)}, f32[27,1,128,128]{3,2,1,0:T(8,128)}, u32[]{:S(2)}) copy-start(f32[27,1,128,128]{3,2,1,0:T(8,128)} %get-tuple-element.155) | copy-start | bytes 5308420
  344.2 10.7 %collective-permute-start.14 = (bf16[3,48,1280]{2,1,0:T(8,128)(2,1)}, bf16[3,48,1280]{2,1,0:T(8,128)(2,1)S(1)}, u32[]{:S(2)}, u32[]{:S(2)}) collective-permute-start(bf16[3,48,1280]{2,1,0:T(8,128)(2,1)} %get-tuple-element.148), channel_id=1, source_target_pairs={{0,1},{1,2},{2,3},{3,4},{4,5},{5,6},{6,7},{7,8},{8,9},{9,10},{10,1... | collective-permute-start | bytes 1105928 | tf_op jit(solution)/shard_map/ppermute | solution.py:30
  346.3 9.5 %collective-permute-start.15 = (bf16[3,48,1280]{2,1,0:T(8,128)(2,1)}, bf16[3,48,1280]{2,1,0:T(8,128)(2,1)}, u32[]{:S(2)}, u32[]{:S(2)}) collective-permute-start(bf16[3,48,1280]{2,1,0:T(8,128)(2,1)} %get-tuple-element.149), channel_id=1, source_target_pairs={{1,0},{2,1},{3,2},{4,3},{5,4},{6,5},{7,6},{8,7},{9,8},{10,9},{11,1... | collective-permute-start | bytes 1105928 | tf_op jit(solution)/shard_map/ppermute | solution.py:30
  408.9 29.2 %copy-start.10 = (f32[3,256,768]{2,1,0:T(8,128)}, f32[3,256,768]{2,1,0:T(8,128)S(1)}, u32[]{:S(2)}) copy-start(f32[3,256,768]{2,1,0:T(8,128)S(1)} %fusion.53) | copy-start | bytes 7077892
  408.9 13.6 %copy-start.8 = (f32[3,256,768]{2,1,0:T(8,128)S(1)}, f32[3,256,768]{2,1,0:T(8,128)}, u32[]{:S(2)}) copy-start(f32[3,256,768]{2,1,0:T(8,128)} %copy-done.7) | copy-start | bytes 7077892
  408.9 13.6 %copy-start.55 = (f32[768]{0:T(1024)S(1)}, f32[768]{0:T(1024)}, u32[]{:S(2)}) copy-start(f32[768]{0:T(1024)} %param.45) | copy-start | bytes 9220
  422.5 8.4 %copy-start.71 = (f32[768]{0:T(1024)S(1)}, f32[768]{0:T(1024)}, u32[]{:S(2)}) copy-start(f32[768]{0:T(1024)} %param.46) | copy-start | bytes 9220
  422.5 8.4 %copy-start.74 = (bf16[3,256,3072]{2,1,0:T(8,128)(2,1)S(1)}, bf16[3,256,3072]{2,1,0:T(8,128)(2,1)}, u32[]{:S(2)}) copy-start(bf16[3,256,3072]{2,1,0:T(8,128)(2,1)} %get-tuple-element.306) | copy-start | bytes 14155780
  445.5 18.9 %copy-start.5 = (pred[3,256,768]{2,1,0:T(8,128)(4,1)S(1)}, pred[3,256,768]{2,1,0:T(8,128)(4,1)}, u32[]{:S(2)}) copy-start(pred[3,256,768]{2,1,0:T(8,128)(4,1)} %broadcast_compare_fusion) | copy-start | bytes 1769476
  445.5 18.9 %copy-start.14 = (bf16[3,256,768]{1,2,0:T(8,128)(2,1)S(1)}, bf16[3,256,768]{1,2,0:T(8,128)(2,1)}, u32[]{:S(2)}) copy-start(bf16[3,256,768]{1,2,0:T(8,128)(2,1)} %copy.200) | copy-start | bytes 3538948
  445.5 18.9 %copy-start.24 = (f32[3,12,256]{2,1,0:T(8,128)S(1)}, f32[3,12,256]{2,1,0:T(8,128)}, u32[]{:S(2)}) copy-start(f32[3,12,256]{2,1,0:T(8,128)} %log_add_fusion) | copy-start | bytes 110596
  522.6 10.9 %copy-start.16 = (f32[27,2,128,128]{3,2,1,0:T(8,128)S(1)}, f32[27,2,128,128]{3,2,1,0:T(8,128)}, u32[]{:S(2)}) copy-start(f32[27,2,128,128]{3,2,1,0:T(8,128)} %get-tuple-element.154) | copy-start | bytes 10616836
  548.1 53.6 %collective-permute-start.18 = (bf16[3,256,768]{2,1,0:T(8,128)(2,1)}, bf16[3,256,768]{2,1,0:T(8,128)(2,1)}, u32[]{:S(2)}, u32[]{:S(2)}) collective-permute-start(bf16[3,256,768]{2,1,0:T(8,128)(2,1)} %get-tuple-element.223), channel_id=1, source_target_pairs={{1,0},{2,1},{3,2},{4,3},{5,4},{6,5},{7,6},{8,7},{9,8},{10,9},{11,1... | collective-permute-start | bytes 3538952 | tf_op jit(solution)/shard_map/ppermute | solution.py:30
  551.9 49.8 %collective-permute-start.19 = (bf16[3,256,768]{2,1,0:T(8,128)(2,1)}, bf16[3,256,768]{2,1,0:T(8,128)(2,1)}, u32[]{:S(2)}, u32[]{:S(2)}) collective-permute-start(bf16[3,256,768]{2,1,0:T(8,128)(2,1)} %get-tuple-element.224), channel_id=1, source_target_pairs={{0,1},{1,2},{2,3},{3,4},{4,5},{5,6},{6,7},{7,8},{8,9},{9,10},{10,1... | collective-permute-start | bytes 3538952 | tf_op jit(solution)/shard_map/ppermute | solution.py:30
  566.9 7.2 copy-start.53
  584.3 30.3 %collective-permute-start.16 = (bf16[3,256,768]{2,1,0:T(8,128)(2,1)}, bf16[3,256,768]{2,1,0:T(8,128)(2,1)S(1)}, u32[]{:S(2)}, u32[]{:S(2)}) collective-permute-start(bf16[3,256,768]{2,1,0:T(8,128)(2,1)} %get-tuple-element.221), channel_id=1, source_target_pairs={{1,0},{2,1},{3,2},{4,3},{5,4},{6,5},{7,6},{8,7},{9,8},{10,9},{11,1... | collective-permute-start | bytes 3538952 | tf_op jit(solution)/shard_map/ppermute | solution.py:30
  588.0 26.6 %collective-permute-start.17 = (bf16[3,256,768]{2,1,0:T(8,128)(2,1)}, bf16[3,256,768]{2,1,0:T(8,128)(2,1)S(1)}, u32[]{:S(2)}, u32[]{:S(2)}) collective-permute-start(bf16[3,256,768]{2,1,0:T(8,128)(2,1)} %get-tuple-element.222), channel_id=1, source_target_pairs={{0,1},{1,2},{2,3},{3,4},{4,5},{5,6},{6,7},{7,8},{8,9},{9,10},{10,1... | collective-permute-start | bytes 3538952 | tf_op jit(solution)/shard_map/ppermute | solution.py:30
  604.5 12.3 %copy-start.13 = (bf16[3,256,768]{2,1,0:T(8,128)(2,1)S(1)}, bf16[3,256,768]{2,1,0:T(8,128)(2,1)}, u32[]{:S(2)}) copy-start(bf16[3,256,768]{2,1,0:T(8,128)(2,1)} %copy.205) | copy-start | bytes 3538948
  604.5 12.9 %copy-start.3 = (bf16[3,256,768]{2,1,0:T(8,128)(2,1)S(1)}, bf16[3,256,768]{2,1,0:T(8,128)(2,1)}, u32[]{:S(2)}) copy-start(bf16[3,256,768]{2,1,0:T(8,128)(2,1)} %param.36) | copy-start | bytes 3538948
  604.5 12.9 %copy-start.34 = (f32[3,256]{1,0:T(4,128)S(1)}, f32[3,256]{1,0:T(4,128)}, u32[]{:S(2)}) copy-start(f32[3,256]{1,0:T(4,128)} %copy-done.33) | copy-start | bytes 9220
  604.5 12.9 %copy-start.47 = (f32[768]{0:T(1024)S(1)}, f32[768]{0:T(1024)}, u32[]{:S(2)}) copy-start(f32[768]{0:T(1024)} %param.39) | copy-start | bytes 9220
  622.5 8.3 %copy-start.36 = (f32[3,256]{1,0:T(4,128)S(1)}, f32[3,256]{1,0:T(4,128)}, u32[]{:S(2)}) copy-start(f32[3,256]{1,0:T(4,128)} %copy-done.35) | copy-start | bytes 9220
  643.1 150.4 %copy-start.49 = (f32[3,256]{1,0:T(4,128)S(1)}, f32[3,256]{1,0:T(4,128)}, u32[]{:S(2)}) copy-start(f32[3,256]{1,0:T(4,128)} %get-tuple-element.168) | copy-start | bytes 9220
  643.1 150.4 %copy-start.42 = (f32[3,256]{1,0:T(4,128)S(1)}, f32[3,256]{1,0:T(4,128)}, u32[]{:S(2)}) copy-start(f32[3,256]{1,0:T(4,128)} %copy-done.41) | copy-start | bytes 9220
  643.1 150.4 %copy-start.48 = (f32[768]{0:T(1024)S(1)}, f32[768]{0:T(1024)}, u32[]{:S(2)}) copy-start(f32[768]{0:T(1024)} %param.39) | copy-start | bytes 9220
  793.5 7.1 copy-start.21
  793.5 7.9 copy-start.20
  (39 other events, 133.0 us)

commit v3 on v2

--- a/solution.py
+++ b/solution.py
@@ -40,62 +40,6 @@
     ]
 
 
-def crop_bounds(sides):
-    volumes = sides * sides * sides
-    ends_at = jnp.cumsum(volumes, axis=-1, dtype=jnp.int32)
-    return (ends_at - volumes, ends_at)
-
-
-def locate(sides, places):
-    starts, ends_at = crop_bounds(sides)
-    inside = (places[:, :, None] >= starts[:, None, :]) & (places[:, :, None] < ends_at[:, None, :])
-    numbers = jnp.arange(sides.shape[-1], dtype=jnp.int32)
-    found = jnp.any(inside, axis=-1)
-    segment = jnp.sum(jnp.where(inside, numbers, 0), axis=-1, dtype=jnp.int32)
-    segment = jnp.where(found, segment, -1)
-    side_of = jnp.sum(jnp.where(inside, sides[:, None, :], 0), axis=-1, dtype=jnp.int32)
-    first_of = jnp.sum(jnp.where(inside, starts[:, None, :], 0), axis=-1, dtype=jnp.int32)
-    return (inside, segment, side_of, first_of)
-
-
-def geometry(side_of, first_of, places):
-    local_pos = places - first_of
-    safe_side = jnp.maximum(side_of, 1)
-    return (
-        local_pos // (safe_side * safe_side),
-        local_pos // safe_side % safe_side,
-        local_pos % safe_side,
-        side_of,
-        side_of == side_big,
-    )
-
-
-def step_sizes(offset):
-    near_step = offset[0] * side_small * side_small + offset[1] * side_small + offset[2]
-    far_step = offset[0] * side_big * side_big + offset[1] * side_big + offset[2]
-    return (near_step, far_step)
-
-
-def in_crop(shape_info, offset):
-    row_pos, column, depth_pos, side_of, is_big = shape_info
-    inside_crop = (row_pos + offset[0] >= 0) & (row_pos + offset[0] < side_of)
-    inside_crop = inside_crop & (column + offset[1] >= 0) & (column + offset[1] < side_of)
-    return inside_crop & (depth_pos + offset[2] >= 0) & (depth_pos + offset[2] < side_of)
-
-
-def layer_norm(values_in, gain, shift):
-    centered = values_in - jnp.mean(values_in, axis=-1, keepdims=True)
-    variance = jnp.mean(centered * centered, axis=-1, keepdims=True)
-    return centered * lax.rsqrt(variance + norm_eps) * gain + shift
-
-
-def crop_scores(query_heads, key_heads, same_crop):
-    raw_scores = jnp.einsum(
-        "sqhd,skhd->shqk", query_heads, key_heads, preferred_element_type=jnp.float32
-    )
-    return jnp.where(same_crop, raw_scores * (1.0 / math.sqrt(HEAD_DIM)), far_below)
-
-
 EDGE = 48
 WINDOW = 256
 TILE = 128
@@ -128,20 +72,34 @@
     return slice(number * width, (number + 1) * width)
 
 
-def banded(taps):
-    begin = jnp.pad(taps, ((0, 0), (0, 0), (0, 1), (0, 0), (0, 0)))
-    later = jnp.pad(taps, ((0, 0), (0, 0), (1, 0), (0, 0), (0, 0)))
-    both = jnp.concatenate([begin, later], axis=-1)
-    return both.reshape(3, 12 * taps.shape[3], 2 * taps.shape[4])
-
-
-def forward_band(weight):
-    return banded(weight.reshape((3, 3, 3) + weight.shape[1:]))
-
-
-def backward_band(weight):
-    taps = weight.reshape((3, 3, 3) + weight.shape[1:])
-    return banded(taps[::-1, ::-1, ::-1].swapaxes(3, 4))
+def all_taps():
+    return [(x, y, z) for x in range(3) for y in range(3) for z in range(3)]
+
+
+def forward_band(weight, band_ref):
+    inner, outer = weight.shape[1:]
+    band_ref[...] = jnp.zeros_like(band_ref)
+    for tap_x, tap_y, tap_z in all_taps():
+        for side in range(2):
+            rows = sub_lanes(tap_y * 4 + tap_z + side, inner)
+            lanes = sub_lanes(side, outer)
+            band_ref[tap_x, rows, lanes] = weight[tap_x * 9 + tap_y * 3 + tap_z]
+
+
+def backward_band(weight, band_ref):
+    inner, outer = weight.shape[1:]
+    band_ref[...] = jnp.zeros_like(band_ref)
+    for tap_x, tap_y, tap_z in all_taps():
+        for side in range(2):
+            rows = sub_lanes(side, inner)
+            lanes = sub_lanes(tap_y * 4 + tap_z + side, outer)
+            band_ref[tap_x, rows, lanes] = weight[26 - (tap_x * 9 + tap_y * 3 + tap_z)]
+
+
+def once(fill, *refs):
+    @pl.when(pl.program_id(0) == 0)
+    def _():
+        fill(*refs)
 
 
 def window_positions(step):
@@ -172,12 +130,12 @@
                     p_ref[own, to : to + count] = got.astype(low_type)
 
 
-def window_conv(p_ref, band_ref, pair, width):
+def window_conv(p_ref, band_ref, pair, width, product):
     first, second = pair
     total = None
     for tap in range(3):
         begin = ((first + tap) * 4 + second) * 4 * width
-        term = dot(p_ref[:, begin : begin + 12 * width], band_ref[tap])
+        term = product(p_ref[:, begin : begin + 12 * width], band_ref[tap])
         total = term if total is None else total + term
     return total
 
@@ -216,7 +174,9 @@
         return pl.BlockSpec((1,) + tuple(shape[1:]), lambda i: (i,) + (0,) * (len(shape) - 1))
 
     def whole_spec(shape):
-        return pl.BlockSpec(tuple(shape), lambda i: (0,) * len(shape))
+        return pl.BlockSpec(
+            tuple(shape), lambda i: (0,) * len(shape), pipeline_mode=pl.Buffered(1)
+        )
 
     moved = sum(math.prod(a.shape) * a.dtype.itemsize for a in list(inputs) + list(shared))
     moved += sum(math.prod(s) * jnp.dtype(t).itemsize for s, t in list(outputs) + list(summed))
@@ -232,10 +192,11 @@
     )(*inputs, *shared)
 
 
-def conv_scratch(rows, width):
+def conv_scratch(rows, width, band_shape):
     return [
         pltpu.VMEM((rows + 192, SUBS * width), low_type),
         pltpu.VMEM((rows, 64 * width), low_type),
+        pltpu.VMEM((3,) + band_shape, low_type),
     ]
 
 
@@ -279,9 +240,10 @@
     width = 2 * channels
 
     def body(
-        up, up_left, up_right, skip, skip_left, skip_right, place, crop_t, band, side,
-        first_out, side_out, sums, low_pay, high_pay, x_ref, p_ref,
+        up, up_left, up_right, skip, skip_left, skip_right, place, crop_t, weight, side,
+        first_out, side_out, sums, low_pay, high_pay, x_ref, p_ref, band_ref,
     ):
+        once(forward_band, weight, band_ref)
         for number in range(SUBS):
             for half, (own, left, right) in enumerate(
                 ((up, up_left, up_right), (skip, skip_left, skip_right))
@@ -295,7 +257,7 @@
         fill_windows(x_ref, place, p_ref, rows, width)
         total = [jnp.zeros((rows, channels), wide) for _ in range(4)]
         for index, pair in enumerate(all_pairs()):
-            result = window_conv(p_ref, band, pair, width)
+            result = window_conv(p_ref, band_ref, pair, width, dot)
             first_out[0, :, sub_lanes(index, width)] = result
             for half in range(2):
                 number = 2 * index + half
@@ -314,9 +276,10 @@
 
 def second_conv_kernel(rows, channels):
     def body(
-        first, left_pay, right_pay, own_sums, inverse, owner, place, crop_t, band,
-        second_out, stats, sums, low_pay, high_pay, x_ref, p_ref,
+        first, left_pay, right_pay, own_sums, inverse, owner, place, crop_t, weight,
+        second_out, stats, sums, low_pay, high_pay, x_ref, p_ref, band_ref,
     ):
+        once(forward_band, weight, band_ref)
         taken = [taken_sums(own_sums, left_pay, right_pay, n, channels) for n in range(4)]
         mean, scale = mean_and_scale(taken[0], taken[1], inverse[0])
         side_mean, side_scale = mean_and_scale(taken[2], taken[3], inverse[0])
@@ -339,7 +302,7 @@
         fill_windows(x_ref, place, p_ref, rows, channels)
         total = [jnp.zeros((rows, channels), wide) for _ in range(2)]
         for index, pair in enumerate(all_pairs()):
-            result = window_conv(p_ref, band, pair, channels)
+            result = window_conv(p_ref, band_ref, pair, channels, dot)
             second_out[0, :, sub_lanes(index, 2 * channels)] = result
             for half in range(2):
                 value = result[:, sub_lanes(half, channels)]
@@ -388,10 +351,11 @@
 def second_back_kernel(rows, channels, seqs):
     def body(
         grad, grad_left, grad_right, own_sums, second, second_left, second_right, side_field, first,
-        stats, second_stats, inverse, owner, place, crop_t, band,
+        stats, second_stats, inverse, owner, place, crop_t, weight,
         first_grad, side_grad, sums, low_pay, high_pay, weight_grad,
-        x_ref, p_ref, left_ref, total_ref,
+        x_ref, p_ref, band_ref, left_ref, total_ref,
     ):
+        once(backward_band, weight, band_ref)
         means = [
             taken_sums(own_sums, grad_left, grad_right, n, channels) * inverse[0] for n in range(3)
         ]
@@ -427,7 +391,7 @@
         fill_windows(x_ref, place, p_ref, rows, channels)
         total = [jnp.zeros((rows, channels), wide) for _ in range(2)]
         for index, pair in enumerate(all_pairs()):
-            result = window_conv(p_ref, band, pair, channels)
+            result = window_conv(p_ref, band_ref, pair, channels, dot_t)
             for half in range(2):
                 number = 2 * index + half
                 lanes = sub_lanes(number, channels)
@@ -458,10 +422,11 @@
 
     def body(
         grad, grad_left, grad_right, own_sums, first, first_left, first_right, stats, inverse, owner,
-        place, side_grad, up, skip, band, side_weight,
+        place, side_grad, up, skip, weight, side_weight,
         up_grad, skip_grad, weight_grad, side_weight_grad,
-        x_ref, p_ref, left_ref, total_ref,
+        x_ref, p_ref, band_ref, left_ref, total_ref,
     ):
+        once(backward_band, weight, band_ref)
         means = [
             taken_sums(own_sums, grad_left, grad_right, n, channels) * inverse[0] for n in range(2)
         ]
@@ -487,12 +452,12 @@
         x_ref[2 * EDGE + rows :, :] = jnp.zeros((96, SUBS * channels), low_type)
         fill_windows(x_ref, place, p_ref, rows, channels)
         for index, pair in enumerate(all_pairs()):
-            result = window_conv(p_ref, band, pair, channels)
+            result = window_conv(p_ref, band_ref, pair, channels, dot_t)
             for half in range(2):
                 number = 2 * index + half
                 lanes = sub_lanes(number, channels)
                 value = result[:, sub_lanes(half, width)]
-                value = value + dot(side_grad[0, :, lanes], side_weight[...])
+                value = value + dot_t(side_grad[0, :, lanes], side_weight[...])
                 up_grad[0, :, lanes] = value[:, :channels].astype(low_type)
                 skip_grad[0, :, lanes] = value[:, channels:]
 
@@ -547,10 +512,10 @@
         first_conv_kernel(rows, channels),
         seqs,
         (upsampled, up_left, up_right, skip, skip_left, skip_right, place, crop_t),
-        (forward_band(conv1_weight), conv3_weight),
+        (conv1_weight, conv3_weight),
         (field, field, table(4), pay(4), pay(4)),
         (),
-        conv_scratch(rows, width),
+        conv_scratch(rows, width, (12 * width, 2 * channels)),
         conv_flops(seqs, rows, width, channels),
     )
     first_left, first_right = exchanged(low_pay, high_pay)
@@ -558,10 +523,10 @@
         second_conv_kernel(rows, channels),
         seqs,
         (first, first_left, first_right, with_far(sums, reaches), inverse, owner, place, crop_t),
-        (forward_band(conv2_weight),),
+        (conv2_weight,),
         (field, table(4), table(2), pay(2), pay(2)),
         (),
-        conv_scratch(rows, channels),
+        conv_scratch(rows, channels, (12 * channels, 2 * channels)),
         conv_flops(seqs, rows, channels, channels),
     )
     second_left, second_right = exchanged(low_pay, high_pay)
@@ -586,10 +551,10 @@
             grad, grad_left, grad_right, with_far(sums, reaches), second, second_left, second_right,
             side_field, first, stats, second_stats, inverse, owner, place, crop_t,
         ),
-        (backward_band(conv2_weight),),
+        (conv2_weight,),
         (field, low_field, table(2), pay(2), pay(2)),
         (((27, 1, channels, channels), wide),),
-        conv_scratch(rows, channels)
+        conv_scratch(rows, channels, (2 * channels, 12 * channels))
         + [
             pltpu.VMEM((SUBS * channels, rows), low_type),
             pltpu.VMEM((9, 2 * channels, 4 * channels), wide),
@@ -604,10 +569,10 @@
             first_grad, back_left, back_right, with_far(sums, reaches), first, first_left,
             first_right, stats, inverse, owner, place, side_grad, upsampled, skip,
         ),
-        (backward_band(conv1_weight), conv3_weight.T),
+        (conv1_weight, conv3_weight),
         (low_field, field),
         (((27, 2, channels, channels), wide), ((width, channels), wide)),
-        conv_scratch(rows, channels)
+        conv_scratch(rows, channels, (2 * width, 12 * channels))
         + [
             pltpu.VMEM((SUBS * width, rows), low_type),
             pltpu.VMEM((9, 2 * width, 4 * channels), wide),
@@ -821,24 +786,370 @@
     return (shares, whole, pieces)
 
 
-def crop_tables(crop_sides, inside, shape_info, first_row, row_count):
+REACH = 224
+QUERY_TILE = 128
+
+
+def dot_t(left, right):
+    return lax.dot_general(
+        left, right, (((1,), (1,)), ((), ())), preferred_element_type=wide
+    )
+
+
+def counted(shape, axis):
+    return lax.broadcasted_iota(jnp.int32, shape, axis).astype(wide)
+
+
+def geometry_kernel(rows, crops):
+    reach_rows = rows + 2 * REACH
+    tile = min(rows, QUERY_TILE)
+    window = tile + 2 * REACH
+
+    def body(side_row, side_column, place, owner, crop_t, inverse, bias):
+        first_row = (lax.axis_index("tok") * rows).astype(wide)
+        sides_r = side_row[0].astype(wide)
+        sides_c = side_column[0].astype(wide)
+        volume_r = sides_r * sides_r * sides_r
+        volume_c = sides_c * sides_c * sides_c
+        shape = (crops, crops)
+        start_r = jnp.sum(
+            jnp.where(counted(shape, 0) < counted(shape, 1), volume_c, 0.0), axis=0, keepdims=True
+        )
+        start_c = jnp.sum(
+            jnp.where(counted(shape, 1) < counted(shape, 0), volume_r, 0.0), axis=1, keepdims=True
+        )
+
+        def inside_of(length, begin):
+            at = counted((length, crops), 0) + begin
+            return ((at >= start_r) & (at < start_r + volume_r), at)
+
+        wide_inside, _ = inside_of(rows + 2 * EDGE, first_row - EDGE)
+        owner[0] = jnp.where(wide_inside, 1.0, 0.0).astype(low_type)
+        inside, _ = inside_of(rows, first_row)
+        side = jnp.sum(jnp.where(inside, sides_r, 0.0), axis=1, keepdims=True)
+        first = jnp.sum(jnp.where(inside, start_r, 0.0), axis=1, keepdims=True)
+        own = counted((rows, 1), 0)
+        offset = own + first_row - first
+        safe = jnp.maximum(side, 1.0)
+        row_pos = jnp.floor((offset + 0.5) / (safe * safe))
+        offset = offset - row_pos * safe * safe
+        column = jnp.floor((offset + 0.5) / safe)
+        depth_pos = offset - column * safe
+        lane = counted((1, 32), 1)
+        step_x = jnp.floor((lane + 0.5) / 9.0)
+        step_y = jnp.floor((lane - 9.0 * step_x + 0.5) / 3.0)
+        step_z = lane - 9.0 * step_x - 3.0 * step_y - 1.0
+        step_x, step_y = (step_x - 1.0, step_y - 1.0)
+        valid = None
+        for at, step in ((row_pos, step_x), (column, step_y), (depth_pos, step_z)):
+            moved = at + step
+            here = (moved >= 0.0) & (moved < side)
+            valid = here if valid is None else valid & here
+        target = own + EDGE + (step_x * safe + step_y) * safe + step_z
+        place[0] = jnp.where(valid, target, -1.0).astype(jnp.int32)
+        at = counted((crops, rows), 1) + first_row
+        inside_t = (at >= start_c) & (at < start_c + volume_c)
+        crop_t[0] = jnp.where(inside_t, 1.0, 0.0).astype(low_type)
+        inverse[0] = jnp.broadcast_to(1.0 / jnp.maximum(8.0 * volume_c, 1.0), (crops, 128))
+        key_inside, _ = inside_of(reach_rows, first_row - REACH)
+        key_first = jnp.sum(jnp.where(key_inside, start_r + 1.0, 0.0), axis=1, keepdims=True)
+        query_first = jnp.sum(jnp.where(inside_t, start_c + 1.0, 0.0), axis=0, keepdims=True)
+        for number in range(rows // tile):
+            base = number * tile
+            same = key_first[base : base + window] == query_first[:, base : base + tile]
+            bias[0, number] = jnp.where(same, 0.0, far_below)
+
+    return body
+
+
+def geometry_tables(crop_sides, rows):
     seqs, crops = crop_sides.shape
-    spare = CROP_ROWS - crops
-    own = jnp.arange(row_count, dtype=jnp.int32)[None, :] + EDGE
-    columns = []
-    for offset in all_offsets():
-        near_step, far_step = step_sizes(offset)
-        step = jnp.where(shape_info[4], far_step, near_step)
-        columns.append(jnp.where(in_crop(shape_info, offset), own + step, -1))
-    place = jnp.stack(columns, axis=-1).astype(jnp.int32)
-    wide_places = first_row - EDGE + jnp.arange(row_count + 2 * EDGE, dtype=jnp.int32)
-    wide_places = jnp.broadcast_to(wide_places, (seqs, row_count + 2 * EDGE))
-    owner = jnp.pad(locate(crop_sides, wide_places)[0], ((0, 0), (0, 0), (0, spare)))
-    crop_t = jnp.pad(inside.swapaxes(1, 2), ((0, 0), (0, spare), (0, 0)))
-    counts = jnp.maximum(8.0 * (crop_sides * crop_sides * crop_sides).astype(wide), 1.0)
-    inverse = jnp.pad(1.0 / counts, ((0, 0), (0, spare)), constant_values=1.0)
-    inverse = jnp.broadcast_to(inverse[:, :, None], (seqs, CROP_ROWS, 128))
-    return (place, owner.astype(low_type), crop_t.astype(low_type), inverse)
+    sides = jnp.pad(crop_sides, ((0, 0), (0, CROP_ROWS - crops)))
+    tile = min(rows, QUERY_TILE)
+    return kernel_call(
+        geometry_kernel(rows, CROP_ROWS),
+        seqs,
+        (sides[:, None, :], sides[:, :, None]),
+        (),
+        (
+            ((seqs, rows, 32), jnp.int32),
+            ((seqs, rows + 2 * EDGE, CROP_ROWS), low_type),
+            ((seqs, CROP_ROWS, rows), low_type),
+            ((seqs, CROP_ROWS, 128), wide),
+            ((seqs, rows // tile, tile + 2 * REACH, tile), wide),
+        ),
+        (),
+        [],
+        0,
+    )
+
+
+def normed_rows(values):
+    centered = values - jnp.mean(values, axis=-1, keepdims=True)
+    variance = jnp.mean(centered * centered, axis=-1, keepdims=True)
+    scale = lax.rsqrt(variance + norm_eps)
+    return (centered * scale, scale)
+
+
+def norm_pull(grad, normed, scale, gain):
+    inner = grad * gain
+    first = jnp.mean(inner, axis=-1, keepdims=True)
+    second = jnp.mean(inner * normed, axis=-1, keepdims=True)
+    return scale * (inner - first - normed * second)
+
+
+def error_function(value):
+    bounded = jnp.clip(value, -3.832506856900711, 3.832506856900711)
+    square = bounded * bounded
+    top = 0.00022905065861350646
+    for term in (0.0034082910107109506, 0.050955695062380861, 0.18520832239976145, 1.128379143519084):
+        top = top * square + term
+    bottom = -1.1791602954361697e-7
+    for term in (
+        0.000023547966471313185, 0.0010179625278914885, 0.014070470171167667,
+        0.11098505178285362, 0.49746925110067538, 1.0,
+    ):
+        bottom = bottom * square + term
+    return bounded * top / bottom
+
+
+def gelu_parts(value):
+    cumulative = 0.5 + 0.5 * error_function(value * math.sqrt(0.5))
+    density = jnp.exp(-0.5 * value * value) * (1.0 / math.sqrt(2.0 * math.pi))
+    return (value * cumulative, cumulative + value * density)
+
+
+def head_lanes(block, half):
+    lane = lax.broadcasted_iota(jnp.int32, block.shape, 1)
+    chosen = lane < HEAD_DIM if half == 0 else lane >= HEAD_DIM
+    return jnp.where(chosen, block, jnp.zeros_like(block))
+
+
+def turned(block):
+    return jnp.transpose(block.astype(wide))
+
+
+def forward_kernel(rows, model_width, hidden):
+    tile = min(rows, QUERY_TILE)
+    window = tile + 2 * REACH
+    chunk = 768
+    scale = 1.0 / math.sqrt(HEAD_DIM)
+
+    def body(
+        tokens, left, right, bias, ln1_gain, ln1_bias, qkv_weight, qkv_bias, out_weight, out_bias,
+        ln2_gain, ln2_bias, fc1_weight, fc1_bias, fc2_weight, fc2_bias, deconv_weight,
+        normed_out, queries, keys, values, attended, log_totals, resid_out, second_out,
+        act_out, slope_out, resid_low, upsampled, near_ref, turned_ref,
+    ):
+        begin = 0
+        for field in (left, tokens, right):
+            length = field.shape[1]
+            normed = normed_rows(field[0].astype(wide))[0] * ln1_gain[...] + ln1_bias[...]
+            near_ref[begin : begin + length, :] = normed.astype(low_type)
+            begin += length
+        own = near_ref[REACH : REACH + rows, :]
+        normed_out[0] = own
+        part = slice(0, model_width)
+        queries[0] = (dot(own, qkv_weight[:, part]) + qkv_bias[:, part]).astype(low_type)
+        part = slice(model_width, 2 * model_width)
+        keys[0] = (dot(near_ref[...], qkv_weight[:, part]) + qkv_bias[:, part]).astype(low_type)
+        part = slice(2 * model_width, 3 * model_width)
+        found = dot(near_ref[...], qkv_weight[:, part]) + qkv_bias[:, part]
+        values[0] = found.astype(low_type)
+        for pair in range(model_width // 128):
+            lanes = sub_lanes(pair, 128)
+            turned_ref[lanes, :] = turned(values[0, :, lanes]).astype(low_type)
+        for number in range(rows // tile):
+            base = number * tile
+            at = slice(base, base + tile)
+            near = slice(base, base + window)
+            for pair in range(model_width // 128):
+                lanes = sub_lanes(pair, 128)
+                query = queries[0, at, lanes] * scale
+                key = keys[0, near, lanes]
+                halves = []
+                for half in range(2):
+                    head = 2 * pair + half
+                    scores = dot_t(key, head_lanes(query, half)) + bias[0, number]
+                    top = jnp.max(scores, axis=0, keepdims=True)
+                    weights = jnp.exp(scores - top)
+                    total = jnp.sum(weights, axis=0, keepdims=True)
+                    log_totals[0, head : head + 1, at] = top + jnp.log(total)
+                    probs = (weights * (1.0 / total)).astype(low_type)
+                    value = turned_ref[head * HEAD_DIM : (head + 1) * HEAD_DIM, near]
+                    halves.append(dot(value, probs))
+                both = jnp.concatenate(halves, axis=0)
+                attended[0, at, lanes] = jnp.transpose(both).astype(low_type)
+        resid = tokens[0].astype(wide) + dot(attended[0], out_weight[...]) + out_bias[...]
+        resid_out[0] = resid
+        second = normed_rows(resid)[0] * ln2_gain[...] + ln2_bias[...]
+        second_out[0] = second.astype(low_type)
+        total = resid + fc2_bias[...]
+        for number in range(hidden // chunk):
+            lanes = sub_lanes(number, chunk)
+            pre = dot(second_out[0], fc1_weight[:, lanes]) + fc1_bias[:, lanes]
+            act, slope = gelu_parts(pre)
+            act_out[0, :, lanes] = act.astype(low_type)
+            slope_out[0, :, lanes] = slope.astype(low_type)
+            total = total + dot(act_out[0, :, lanes], fc2_weight[lanes, :])
+        resid_low[0] = total.astype(low_type)
+        upsampled[0] = dot(resid_low[0], deconv_weight[...]).astype(low_type)
+
+    return body
+
+
+def backward_kernel(rows, model_width, hidden):
+    tile = min(rows, QUERY_TILE)
+    window = tile + 2 * REACH
+    chunk = 768
+    scale = 1.0 / math.sqrt(HEAD_DIM)
+
+    def body(
+        up_grad, slope, resid, queries, keys, values, log_totals, bias,
+        deconv_weight, fc2_weight, fc1_weight, out_weight, ln2_gain,
+        branch_out, pre_out, resid_grad, mixed_out, query_grad, key_own, value_own, low_pay, high_pay,
+        fc2_sum, fc1_sum, out_sum, gain_sum, shift_sum,
+        near_key, near_value, turned_ref, pulled_ref,
+    ):
+        @pl.when(pl.program_id(0) == 0)
+        def _():
+            for ref in (fc2_sum, fc1_sum, out_sum, gain_sum, shift_sum):
+                ref[...] = jnp.zeros_like(ref)
+
+        def column_sum(field):
+            return jnp.sum(field, axis=0, keepdims=True)
+
+        incoming = dot_t(up_grad[0], deconv_weight[...])
+        branch = incoming.astype(low_type)
+        branch_out[0] = branch
+        fc2_sum[...] += column_sum(branch.astype(wide))
+        total = None
+        for number in range(hidden // chunk):
+            lanes = sub_lanes(number, chunk)
+            act_grad = dot_t(branch_out[0], fc2_weight[lanes, :])
+            pre = (act_grad * slope[0, :, lanes].astype(wide)).astype(low_type)
+            pre_out[0, :, lanes] = pre
+            fc1_sum[:, lanes] += column_sum(pre.astype(wide))
+            term = dot_t(pre_out[0, :, lanes], fc1_weight[:, lanes])
+            total = term if total is None else total + term
+        normed, norm_scale = normed_rows(resid[0])
+        gain_sum[...] += column_sum(total * normed)
+        shift_sum[...] += column_sum(total)
+        mixed = incoming + norm_pull(total, normed, norm_scale, ln2_gain[...])
+        resid_grad[0] = mixed
+        mixed = mixed.astype(low_type)
+        mixed_out[0] = mixed
+        out_sum[...] += column_sum(mixed.astype(wide))
+        pulled_ref[...] = dot_t(mixed_out[0], out_weight[...]).astype(low_type)
+        for pair in range(model_width // 128):
+            lanes = sub_lanes(pair, 128)
+            turned_ref[lanes, :] = turned(keys[0, :, lanes]).astype(low_type)
+        near_key[...] = jnp.zeros_like(near_key)
+        near_value[...] = jnp.zeros_like(near_value)
+        for number in range(rows // tile):
+            base = number * tile
+            at = slice(base, base + tile)
+            near = slice(base, base + window)
+            for pair in range(model_width // 128):
+                lanes = sub_lanes(pair, 128)
+                query = queries[0, at, lanes] * scale
+                pulled = pulled_ref[at, lanes]
+                key = keys[0, near, lanes]
+                value = values[0, near, lanes]
+                halves = []
+                key_term = None
+                value_term = None
+                for half in range(2):
+                    head = 2 * pair + half
+                    one_query = head_lanes(query, half)
+                    one_pull = head_lanes(pulled, half)
+                    scores = dot_t(key, one_query) + bias[0, number]
+                    probs = jnp.exp(scores - log_totals[0, head : head + 1, at])
+                    probs_grad = dot_t(value, one_pull)
+                    inner = jnp.sum(probs * probs_grad, axis=0, keepdims=True)
+                    score_grad = (probs * (probs_grad - inner)).astype(low_type)
+                    here = dot(score_grad, one_query)
+                    key_term = here if key_term is None else key_term + here
+                    here = dot(probs.astype(low_type), one_pull)
+                    value_term = here if value_term is None else value_term + here
+                    key_turned = turned_ref[head * HEAD_DIM : (head + 1) * HEAD_DIM, near]
+                    halves.append(dot(key_turned, score_grad) * scale)
+                near_key[near, lanes] += key_term
+                near_value[near, lanes] += value_term
+                both = jnp.concatenate(halves, axis=0)
+                query_grad[0, at, lanes] = jnp.transpose(both).astype(low_type)
+        for field, own_out, begin in (
+            (near_key, key_own, 0),
+            (near_value, value_own, model_width),
+        ):
+            lanes = slice(begin, begin + model_width)
+            own_out[0] = field[REACH : REACH + rows, :]
+            low_pay[0, :, lanes] = field[:REACH, :].astype(low_type)
+            high_pay[0, :, lanes] = field[REACH + rows :, :].astype(low_type)
+
+    return body
+
+
+def token_kernel(rows, model_width, joined):
+    def body(*refs):
+        tokens, resid_grad, query_grad, key_own, value_own = refs[:5]
+        rest = refs[5:]
+        if joined:
+            from_left, from_right = rest[:2]
+            rest = rest[2:]
+        (qkv_weight, ln1_gain, grad_out, token_grad, bias_sum, gain_sum, shift_sum) = rest[:7]
+
+        @pl.when(pl.program_id(0) == 0)
+        def _():
+            for ref in (bias_sum, gain_sum, shift_sum):
+                ref[...] = jnp.zeros_like(ref)
+
+        grad_out[0, :, :model_width] = query_grad[0]
+        for number, own in enumerate((key_own, value_own)):
+            lanes = sub_lanes(number, model_width)
+            to = sub_lanes(number + 1, model_width)
+            value = own[0]
+            if joined:
+                spare = jnp.zeros((rows - REACH, model_width), wide)
+                value = value + jnp.concatenate([from_left[0, :, lanes].astype(wide), spare], axis=0)
+                value = value + jnp.concatenate([spare, from_right[0, :, lanes].astype(wide)], axis=0)
+            grad_out[0, :, to] = value.astype(low_type)
+        bias_sum[...] += jnp.sum(grad_out[0].astype(wide), axis=0, keepdims=True)
+        total = dot_t(grad_out[0], qkv_weight[...])
+        normed, norm_scale = normed_rows(tokens[0].astype(wide))
+        gain_sum[...] += jnp.sum(total * normed, axis=0, keepdims=True)
+        shift_sum[...] += jnp.sum(total, axis=0, keepdims=True)
+        token_grad[0] = resid_grad[0] + norm_pull(total, normed, norm_scale, ln1_gain[...])
+
+    return body
+
+
+def near_rows(field):
+    rows = field.shape[1]
+    lefts, rights = ([], [])
+    distance, missing = (1, REACH)
+    while missing > 0:
+        take = min(rows, missing)
+        lefts.insert(0, passed_along(field[:, rows - take :], "tok", distance))
+        rights.append(passed_along(field[:, :take], "tok", -distance))
+        distance, missing = (distance + 1, missing - take)
+    if len(lefts) == 1:
+        return (lefts[0], rights[0])
+    return (jnp.concatenate(lefts, axis=1), jnp.concatenate(rights, axis=1))
+
+
+def returned_rows(own, low_pay, high_pay):
+    rows = own.shape[1]
+    distance, missing = (1, REACH)
+    while missing > 0:
+        take = min(rows, missing)
+        low_piece = low_pay[:, missing - take : missing]
+        begin = REACH - missing
+        high_piece = high_pay[:, begin : begin + take]
+        own = own.at[:, rows - take :].add(passed_along(low_piece, "tok", -distance).astype(wide))
+        own = own.at[:, :take].add(passed_along(high_piece, "tok", distance).astype(wide))
+        distance, missing = (distance + 1, missing - take)
+    return own
 
 
 def local(
@@ -865,182 +1176,141 @@
 ):
     seq_count, row_count, model_width = tokens.shape
     channels = conv2_weight.shape[2]
-    score_scale = 1.0 / math.sqrt(HEAD_DIM)
-    first_row = lax.axis_index("tok") * row_count
-    places = jnp.broadcast_to(
-        first_row + jnp.arange(row_count, dtype=jnp.int32), (seq_count, row_count)
-    )
-    inside, segment, side_of, first_of = locate(crop_sides, places)
-    shape_info = geometry(side_of, first_of, places)
+    hidden = fc1_weight.shape[1]
     reaches = (key_reach + row_count - 1) // row_count
-    token_values = tokens.astype(jnp.float32)
-    normed_low = layer_norm(token_values, ln1_gain, ln1_bias).astype(jnp.bfloat16)
+    reach_rows = row_count + 2 * REACH
+    near_left, near_right = near_rows(tokens)
+    place, owner, crop_t, inverse, bias = geometry_tables(crop_sides, row_count)
+
+    def flat(vector):
+        return vector.reshape(1, -1)
+
+    def block(lanes, kind, rows=row_count):
+        return ((seq_count, rows, lanes), kind)
+
     qkv_bias = jnp.concatenate([qv_bias[0], jnp.zeros_like(qv_bias[0]), qv_bias[1]])
-    projected = (
-        jnp.einsum("std,de->ste", normed_low, qkv_weight, preferred_element_type=jnp.float32)
-        + qkv_bias
-    ).astype(jnp.bfloat16)
-    queries = projected[:, :, :model_width]
-    keys = projected[:, :, model_width : 2 * model_width]
-    values = projected[:, :, 2 * model_width :]
-    key_parts = [keys]
-    value_parts = [values]
-    place_parts = [places]
-    moves = []
-    for distance in range(1, reaches + 1):
-        row_take = row_count
-        for shift_by in (distance, -distance):
-            if shift_by > 0:
-                key_send = keys
-                value_send = values
-                got_first = first_row - (distance - 1) * row_count - row_take
-            else:
-                key_send = keys
-                value_send = values
-                got_first = first_row + distance * row_count
-            got_keys, got_values = passed_along((key_send, value_send), "tok", shift_by)
-            key_parts.append(got_keys)
-            value_parts.append(got_values)
-            place_parts.append(
-                jnp.broadcast_to(
-                    got_first + jnp.arange(row_take, dtype=jnp.int32), (seq_count, row_take)
-                )
-            )
-            moves.append((shift_by, row_take))
-    window_keys = jnp.concatenate(key_parts, axis=1).reshape(seq_count, -1, HEADS, HEAD_DIM)
-    window_values = jnp.concatenate(value_parts, axis=1).reshape(seq_count, -1, HEADS, HEAD_DIM)
-    key_crop = locate(crop_sides, jnp.concatenate(place_parts, axis=1))[1]
-    same_crop = segment[:, None, :, None] == key_crop[:, None, None, :]
-    query_heads = queries.reshape(seq_count, row_count, HEADS, HEAD_DIM)
-    scores = crop_scores(query_heads, window_keys, same_crop)
-    row_max = jnp.max(scores, axis=-1, keepdims=True)
-    weights = jnp.exp(scores - row_max)
-    totals = jnp.sum(weights, axis=-1, keepdims=True)
-    log_total = row_max + jnp.log(totals)
-    probs_low = (weights / totals).astype(jnp.bfloat16)
-    attended = jnp.einsum(
-        "shqk,skhd->sqhd", probs_low, window_values, preferred_element_type=jnp.float32
-    )
-    attended = attended.astype(jnp.bfloat16).reshape(seq_count, row_count, model_width)
-    resid_one = (
-        token_values
-        + jnp.einsum("std,de->ste", attended, out_weight, preferred_element_type=jnp.float32)
-        + out_bias
-    )
-    normed_two = layer_norm(resid_one, ln2_gain, ln2_bias).astype(jnp.bfloat16)
-    pre_act = (
-        jnp.einsum("std,df->stf", normed_two, fc1_weight, preferred_element_type=jnp.float32)
-        + fc1_bias
-    )
-    act_low = jax.nn.gelu(pre_act, approximate=False).astype(jnp.bfloat16)
-    resid_two = (
-        resid_one
-        + jnp.einsum("stf,fd->std", act_low, fc2_weight, preferred_element_type=jnp.float32)
-        + fc2_bias
-    )
-    resid_low = resid_two.astype(jnp.bfloat16)
-    upsampled = jnp.einsum(
-        "std,de->ste", resid_low, deconv_weight, preferred_element_type=jnp.float32
-    )
-    upsampled = upsampled.astype(jnp.bfloat16)
-    geometry_in = crop_tables(crop_sides, inside, shape_info, first_row, row_count)
+    matrix_flops = 2 * seq_count * row_count * model_width
+    (
+        normed_low, queries, keys, values, attended, log_totals, resid_one, normed_two,
+        act_low, slope_low, resid_low, upsampled,
+    ) = kernel_call(
+        forward_kernel(row_count, model_width, hidden),
+        seq_count,
+        (tokens, near_left, near_right, bias),
+        (
+            flat(ln1_gain), flat(ln1_bias), qkv_weight, flat(qkv_bias), out_weight, flat(out_bias),
+            flat(ln2_gain), flat(ln2_bias), fc1_weight, flat(fc1_bias), fc2_weight, flat(fc2_bias),
+            deconv_weight,
+        ),
+        (
+            block(model_width, low_type),
+            block(model_width, low_type),
+            block(model_width, low_type, reach_rows),
+            block(model_width, low_type, reach_rows),
+            block(model_width, low_type),
+            block(row_count, wide, 16),
+            block(model_width, wide),
+            block(model_width, low_type),
+            block(hidden, low_type),
+            block(hidden, low_type),
+            block(model_width, low_type),
+            block(8 * channels, low_type),
+        ),
+        (),
+        [
+            pltpu.VMEM((reach_rows, model_width), low_type),
+            pltpu.VMEM((model_width, reach_rows), low_type),
+        ],
+        matrix_flops * (8 * model_width + 2 * hidden + 8 * channels),
+    )
     section_out, up_grad, skip_grad, conv1_grad, conv2_grad, conv3_grad = conv_section(
         upsampled,
         skip_features.reshape(seq_count, row_count, 8 * channels),
         cotangent.reshape(seq_count, row_count, 8 * channels),
         (conv1_weight, conv2_weight, conv3_weight),
-        geometry_in,
+        (place, owner, crop_t, inverse),
         reaches,
     )
     section_out = section_out.reshape(seq_count, row_count, 8, channels)
     skip_grad = skip_grad.reshape(seq_count, row_count, 8, channels)
-    deconv_grad = jnp.einsum("std,ste->de", resid_low, up_grad, preferred_element_type=jnp.float32)
-    resid_two_grad = jnp.einsum(
-        "ste,de->std", up_grad, deconv_weight, preferred_element_type=jnp.float32
-    )
-    branch_low = resid_two_grad.astype(jnp.bfloat16)
-    fc2_bias_grad = jnp.sum(branch_low.astype(jnp.float32), axis=(0, 1))
-    fc2_grad = jnp.einsum("stf,std->fd", act_low, branch_low, preferred_element_type=jnp.float32)
-    act_grad = jnp.einsum("std,fd->stf", branch_low, fc2_weight, preferred_element_type=jnp.float32)
-    gelu_pull = jax.vjp(partial(jax.nn.gelu, approximate=False), pre_act)[1]
-    pre_low = gelu_pull(act_grad)[0].astype(jnp.bfloat16)
-    fc1_bias_grad = jnp.sum(pre_low.astype(jnp.float32), axis=(0, 1))
-    fc1_grad = jnp.einsum("std,stf->df", normed_two, pre_low, preferred_element_type=jnp.float32)
-    normed_two_grad = jnp.einsum(
-        "stf,df->std", pre_low, fc1_weight, preferred_element_type=jnp.float32
-    )
-    second_ln_pull = jax.vjp(layer_norm, resid_one, ln2_gain, ln2_bias)[1]
-    resid_part, ln2_gain_grad, ln2_bias_grad = second_ln_pull(normed_two_grad)
-    resid_one_grad = resid_two_grad + resid_part
-    mixed_low = resid_one_grad.astype(jnp.bfloat16)
-    out_bias_grad = jnp.sum(mixed_low.astype(jnp.float32), axis=(0, 1))
-    out_grad = jnp.einsum("std,ste->de", attended, mixed_low, preferred_element_type=jnp.float32)
-    attended_grad = jnp.einsum(
-        "ste,de->std", mixed_low, out_weight, preferred_element_type=jnp.float32
-    )
-    attended_grad = attended_grad.astype(jnp.bfloat16).reshape(
-        seq_count, row_count, HEADS, HEAD_DIM
-    )
-    scores_again = crop_scores(query_heads, window_keys, same_crop)
-    attn_probs = jnp.exp(scores_again - log_total)
-    probs_again = attn_probs.astype(jnp.bfloat16)
-    probs_grad = jnp.einsum(
-        "sqhd,skhd->shqk", attended_grad, window_values, preferred_element_type=jnp.float32
-    )
-    row_inner = jnp.sum(attn_probs * probs_grad, axis=-1, keepdims=True)
-    score_low = (attn_probs * (probs_grad - row_inner)).astype(jnp.bfloat16)
-    query_grad = (
-        jnp.einsum("shqk,skhd->sqhd", score_low, window_keys, preferred_element_type=jnp.float32)
-        * score_scale
-    )
-    key_grad = (
-        jnp.einsum("shqk,sqhd->skhd", score_low, query_heads, preferred_element_type=jnp.float32)
-        * score_scale
-    )
-    value_grad = jnp.einsum(
-        "shqk,sqhd->skhd", probs_again, attended_grad, preferred_element_type=jnp.float32
-    )
-    key_grad = key_grad.reshape(seq_count, -1, model_width)
-    value_grad = value_grad.reshape(seq_count, -1, model_width)
-    key_own = key_grad[:, :row_count]
-    value_own = value_grad[:, :row_count]
-    cursor = row_count
-    for shift_by, row_take in moves:
-        key_piece = key_grad[:, cursor : cursor + row_take]
-        value_piece = value_grad[:, cursor : cursor + row_take]
-        cursor = cursor + row_take
-        back_keys, back_values = (
-            passed_along(key_piece.astype(jnp.bfloat16), "tok", -shift_by).astype(key_piece.dtype),
-            passed_along(value_piece.astype(jnp.bfloat16), "tok", -shift_by).astype(
-                value_piece.dtype
-            ),
+    (
+        branch_low, pre_low, resid_grad, mixed_low, query_grad, key_own, value_own, low_pay, high_pay,
+        fc2_bias_grad, fc1_bias_grad, out_bias_grad, ln2_gain_grad, ln2_bias_grad,
+    ) = kernel_call(
+        backward_kernel(row_count, model_width, hidden),
+        seq_count,
+        (up_grad, slope_low, resid_one, queries, keys, values, log_totals, bias),
+        (deconv_weight, fc2_weight, fc1_weight, out_weight, flat(ln2_gain)),
+        (
+            block(model_width, low_type),
+            block(hidden, low_type),
+            block(model_width, wide),
+            block(model_width, low_type),
+            block(model_width, low_type),
+            block(model_width, wide),
+            block(model_width, wide),
+            block(2 * model_width, low_type, REACH),
+            block(2 * model_width, low_type, REACH),
+        ),
+        (
+            ((1, model_width), wide),
+            ((1, hidden), wide),
+            ((1, model_width), wide),
+            ((1, model_width), wide),
+            ((1, model_width), wide),
+        ),
+        [
+            pltpu.VMEM((reach_rows, model_width), wide),
+            pltpu.VMEM((reach_rows, model_width), wide),
+            pltpu.VMEM((model_width, reach_rows), low_type),
+            pltpu.VMEM((row_count, model_width), low_type),
+        ],
+        matrix_flops * (12 * model_width + 2 * hidden + 8 * channels),
+    )
+    joined = row_count >= REACH
+    returned = ()
+    if joined:
+        returned = exchanged(low_pay, high_pay)
+    else:
+        both = jnp.concatenate([key_own, value_own], axis=-1)
+        both = returned_rows(both, low_pay, high_pay)
+        key_own, value_own = (both[:, :, :model_width], both[:, :, model_width:])
+    qkv_grad_low, token_grad, column_sums, ln1_gain_grad, ln1_bias_grad = kernel_call(
+        token_kernel(row_count, model_width, joined),
+        seq_count,
+        (tokens, resid_grad, query_grad, key_own, value_own) + tuple(returned),
+        (qkv_weight, flat(ln1_gain)),
+        (block(3 * model_width, low_type), block(model_width, wide)),
+        (
+            ((1, 3 * model_width), wide),
+            ((1, model_width), wide),
+            ((1, model_width), wide),
+        ),
+        [],
+        matrix_flops * 3 * model_width,
+    )
+
+    def weight_product(left, right):
+        return jnp.einsum(
+            "rd,re->de",
+            left.reshape(-1, left.shape[-1]),
+            right.reshape(-1, right.shape[-1]),
+            preferred_element_type=wide,
         )
-        if shift_by > 0:
-            key_own = key_own.at[:, row_count - row_take :].add(back_keys)
-            value_own = value_own.at[:, row_count - row_take :].add(back_values)
-        else:
-            key_own = key_own.at[:, :row_take].add(back_keys)
-            value_own = value_own.at[:, :row_take].add(back_values)
-    qkv_grad_low = jnp.concatenate(
-        [query_grad.reshape(seq_count, row_count, model_width), key_own, value_own], axis=-1
-    ).astype(jnp.bfloat16)
-    qkv_grad = jnp.einsum(
-        "std,ste->de", normed_low, qkv_grad_low, preferred_element_type=jnp.float32
-    )
-    column_sums = jnp.sum(qkv_grad_low.astype(jnp.float32), axis=(0, 1))
-    qv_bias_grad = jnp.stack([column_sums[:model_width], column_sums[2 * model_width :]])
-    normed_one_grad = jnp.einsum(
-        "ste,de->std", qkv_grad_low, qkv_weight, preferred_element_type=jnp.float32
-    )
-    first_ln_pull = jax.vjp(layer_norm, token_values, ln1_gain, ln1_bias)[1]
-    token_part, ln1_gain_grad, ln1_bias_grad = first_ln_pull(normed_one_grad)
-    token_grad = resid_one_grad + token_part
+
+    deconv_grad = weight_product(resid_low, up_grad)
+    fc2_grad = weight_product(act_low, branch_low)
+    fc1_grad = weight_product(normed_two, pre_low)
+    out_grad = weight_product(attended, mixed_low)
+    qkv_grad = weight_product(normed_low, qkv_grad_low)
+    query_sums = column_sums[:, :model_width]
+    value_sums = column_sums[:, 2 * model_width :]
     conv3_turned = jnp.moveaxis(conv3_grad.reshape(1, 2, channels, channels), 2, 3)
     conv_shares, shares, vectors = reduced_all(
         (conv1_grad, conv2_grad, conv3_turned),
         (deconv_grad, fc2_grad, fc1_grad, out_grad, qkv_grad),
         (
-            ln1_gain_grad, ln1_bias_grad, qv_bias_grad[0], qv_bias_grad[1], out_bias_grad,
+            ln1_gain_grad, ln1_bias_grad, query_sums, value_sums, out_bias_grad,
             ln2_gain_grad, ln2_bias_grad, fc1_bias_grad, fc2_bias_grad,
         ),
     )

time: 816 us -> 592 us (0.73)
  other arithmetic: 157 us -> 7.06 us
  matrix products: 169 us -> 27.1 us
  Pallas kernels: 277 us -> 410 us
  local copies, waits for them, and re-layouts: 115 us -> 36.9 us
  waiting for transfers between devices: 27 us -> 54.2 us
  starting transfers between devices: 56.2 us -> 43.8 us
    dot_general x21 -> x5, matrix products: 169 us -> 27.1 us  [weight_product(): jnp.einsum('rd,re->de', left.reshape(-1, left.shape[-1]), right.reshape(-...]
    pallas_call x5 -> x9, Pallas kernels: 133 us -> 262 us  [kernel_call(): pl.pallas_call(body, grid=(seqs,), in_specs=[row_spec(a.shape) for a in i...]
    convert_element_type x4 -> x0, other arithmetic: 49.5 us -> none  [the longest x1 24 us: local(): score_low = (attn_probs * (probs_grad - row_inner)).astype(jnp.bfloat16)]
    select_n x6 -> x0, other arithmetic: 32.8 us -> none  [the longest x4 31.4 us: crop_tables(): columns.append(jnp.where(in_crop(shape_info, offset), own + step, -1))]
    ppermute x20 -> x16, waiting for transfers between devices: 27 us -> 54.2 us  [passed_along(): return lax.ppermute(block, axis, route)]
    reduce_sum x10 -> x0, other arithmetic: 25.7 us -> none  [the longest x1 14.7 us: local(): totals = jnp.sum(weights, axis=-1, keepdims=True)]
    reshape x5 -> x7, local copies, waits for them, and re-layouts: 24.9 us -> 4.12 us  [flat(): return vector.reshape(1, -1)]
    concatenate x7 -> x0, other arithmetic: 18.4 us -> none  [the longest x4 11.5 us: banded(): both = jnp.concatenate([begin, later], axis=-1)]
  transfers between devices with their start and end apart: 20 -> 16, of which waited for: 7 -> 12; matrix products, arithmetic and copies ran while one was open for 29% -> 7% of each run, Pallas kernels for 0% -> 12%
where the time goes in v3:
time: 592 us; the launch traced here: 580 us
  Pallas kernels  410 us (69%)
  waiting for transfers between devices  54.2 us (9%)
  starting transfers between devices  43.8 us (7%)
  local copies, waits for them, and re-layouts  36.9 us (6%)
  matrix products  27.1 us (5%)
  other arithmetic  7.06 us (1%)
    pallas_call x9, Pallas kernels, kernel_call(): pl.pallas_call(body, grid=(seqs,), in_specs=[row_spec(a.shape) for a in i...  262 us
    pallas_call x1, Pallas kernels, reduced(): pl.pallas_call(reduce_kernel(pieces, len(grads), tok_bits, seq_bits), in_...  147 us
    ppermute x16, waiting for transfers between devices, passed_along(): return lax.ppermute(block, axis, route)  54.2 us
    ppermute x16, starting transfers between devices, passed_along(): return lax.ppermute(block, axis, route)  43.8 us
    dot_general x5, matrix products, weight_product(): jnp.einsum('rd,re->de', left.reshape(-1, left.shape[-1]), right.reshape(-...  27.1 us
    unnamed x99, local copies, waits for them, and re-layouts  13.6 us
  transfers between devices with their start and end apart: 16, of which 12 were waited for; matrix products, arithmetic and copies ran while one was open for 7% of the time, Pallas kernels for 12%

profile of v3, /device:TPU:30, one launch (start us, length us, event | category | flops | bytes accessed | tf_op | source)
XLA Modules:
  0.0 580.3 jit_solution(10069907890144611020)
XLA Ops:
  0.7 3.1 fusion.2
  3.8 1.9 collective-permute-start.1
  5.8 3.5 collective-permute-start
  9.2 0.7 reshape.175.skip
  10.0 2.2 collective-permute-start.5
  12.3 2.1 collective-permute-start.4
  19.2 0.7 copy.47.side_column
  19.9 3.4 shard_map.339
  23.3 9.0 %collective-permute-done.1.right = bf16[3,224,768]{2,1,0:T(8,128)(2,1)} collective-permute-done((bf16[3,224,768]{2,1,0:T(8,128)(2,1)}, bf16[3,224,768]{2,1,0:T(8,128)(2,1)}, u32[]{:S(2)}, u32[]{:S(2)}) %collective-permute-start.1) | collective-permute-done | bytes 1032224 | tf_op jit(solution)/shard_map/ppermute | solution.py:30
  32.3 65.8 %shard_map.340 = (bf16[3,256,768]{2,1,0:T(8,128)(2,1)}, bf16[3,256,768]{2,1,0:T(8,128)(2,1)}, bf16[3,704,768]{2,1,0:T(8,128)(2,1)}, bf16[3,704,768]{2,1,0:T(8,12...) custom-call(bf16[3,256,768]{2,1,0:T(8,128)(2,1)} %refs_0_.1, ...), custom_call_target="tpu_custom_call" | custom-call | flops 15703474176 | bytes 46586880 | tf_op jit(solution)/shard_map/pallas_call | solution.py:183
  98.1 1.1 fusion.1
  99.2 3.8 collective-permute-start.3
  103.0 1.9 collective-permute-start.2
  105.0 5.4 collective-permute-done.3.up_right
  111.8 27.1 %shard_map.341 = (f32[3,256,1024]{2,1,0:T(8,128)}, f32[3,256,1024]{2,1,0:T(8,128)}, f32[3,48,512]{2,1,0:T(8,128)}, bf16[3,48,1536]{2,1,0:T(8,128)(2,1)}, bf16[3,48,1536]{2,1,0:T(8,128)(2,1)}) custom-call(bf16[3,256,1024]{2,1,0:T(8,128)(2,1)} %get-tuple-element.88.up, bf16[3,48,1024]{2,1,0:T(8,128)(2,1)} %copy-done.37, bf16[3,48,1024]{2,1,0:T(8,128)(2,1)} %copy-done.36, ...), custom_call_target="tpu_custom_call" | custom-call | flops 20132659200 | bytes 13803520 | tf_op jit(solution)/shard_map/pallas_call | solution.py:183
  138.9 1.9 collective-permute-start.6
  140.8 3.6 collective-permute-start.7
  144.5 4.3 collective-permute-done.6.left_pay.first_left
  148.7 4.6 collective-permute-done.7.right_pay.first_right
  153.3 0.8 copy-done.29
  154.1 18.6 %shard_map.342 = (f32[3,256,1024]{2,1,0:T(8,128)}, f32[3,48,512]{2,1,0:T(8,128)}, f32[3,48,256]{2,1,0:T(8,128)}, bf16[3,48,1280]{2,1,0:T(8,128)(2,1)}, bf16[3,48,1280]{2,1,0:T(8,128)(2,1)}) custom-call(f32[3,256,1024]{2,1,0:T(8,128)} %get-tuple-element.91.first, bf16[3,48,1536]{2,1,0:T(8,128)(2,1)} %copy-done.28, bf16[3,48,1536]{2,1,0:T(8,128)(2,1)} %copy-done.29, ...), custom_call_target="tpu_custom_call" | custom-call | flops 10066329600 | bytes 9882624 | tf_op jit(solution)/shard_map/pallas_call | solution.py:183
  172.7 1.9 collective-permute-start.8
  174.7 3.7 collective-permute-start.9
  178.4 2.1 reshape.176.cotangent
  180.4 1.4 collective-permute-done.8.left_pay.second_left
  181.8 2.1 collective-permute-done.9.right_pay.second_right
  183.9 0.7 copy-done.10
  184.6 8.0 %shard_map.343 = (bf16[3,256,1024]{2,1,0:T(8,128)(2,1)}, f32[3,256,1024]{2,1,0:T(8,128)}, f32[3,48,256]{2,1,0:T(8,128)}, f32[3,48,384]{2,1,0:T(8,128)}, bf16[3,4...) custom-call(f32[3,256,1024]{2,1,0:T(8,128)} %get-tuple-element.97.second, ...), custom_call_target="tpu_custom_call" | custom-call | flops 15728640 | bytes 15191040 | tf_op jit(solution)/shard_map/pallas_call | solution.py:183
  192.6 1.9 collective-permute-start.10
  194.6 3.7 collective-permute-start.11
  198.3 3.9 collective-permute-done.10.grad_left
  202.2 3.3 collective-permute-done.11.grad_right
  205.4 0.7 copy-done.31
  206.2 32.4 %shard_map.344 = (f32[3,256,1024]{2,1,0:T(8,128)}, bf16[3,256,1024]{2,1,0:T(8,128)(2,1)}, f32[3,48,256]{2,1,0:T(8,128)}, bf16[3,48,1280]{2,1,0:T(8,128)(2,1)}, b...) custom-call(f32[3,256,1024]{2,1,0:T(8,128)} %get-tuple-element.104.grad, bf16[3,48,1408]{2,1,0:T(8,128)(2,1)} %copy-done.30, ...), custom_call_target="tpu_custom_call" | custom-call | flops 20132659200 | bytes 23399424 | tf_op jit(solution)/shard_map/pallas_call | solution.py:183
  238.6 2.1 collective-permute-start.12
  240.6 3.7 collective-permute-start.13
  244.4 1.6 copy.62
  246.1 1.1 copy.49
  247.8 2.5 collective-permute-done.13.grad_right
  250.3 0.7 copy-done.33
  251.0 47.2 %shard_map.345 = (bf16[3,256,1024]{2,1,0:T(8,128)(2,1)}, f32[3,256,1024]{2,1,0:T(8,128)}, f32[27,2,128,128]{3,2,1,0:T(8,128)}, f32[256,128]{1,0:T(8,128)}) custom-call(f32[3,256,1024]{2,1,0:T(8,128)} %get-tuple-element.109.grad, bf16[3,48,1280]{2,1,0:T(8,128)(2,1)} %copy-done.32, bf16[3,48,1280]{2,1,0:T(8,128)(2,1)} %copy-done.33, ...), custom_call_target="tpu_custom_call" | custom-call | flops 34628173824 | bytes 23571456 | tf_op jit(solution)/shard_map/pallas_call | solution.py:183
  298.2 48.8 %shard_map.346 = (bf16[3,256,768]{2,1,0:T(8,128)(2,1)}, bf16[3,256,3072]{2,1,0:T(8,128)(2,1)}, f32[3,256,768]{2,1,0:T(8,128)}, bf16[3,256,768]{2,1,0:T(8,128)(2,...) custom-call(bf16[3,256,1024]{2,1,0:T(8,128)(2,1)} %get-tuple-element, ...), custom_call_target="tpu_custom_call" | custom-call | flops 19327352832 | bytes 49818624 | tf_op jit(solution)/shard_map/pallas_call | solution.py:183
  347.1 0.7 convert_reduce_fusion
  347.8 2.4 convert_bitcast_fusion
  350.3 1.9 collective-permute-start.14
  352.2 3.9 collective-permute-start.15
  356.2 2.2 bitcast_convert_fusion.4
  358.5 2.4 copy.63
  363.6 4.5 bitcast_convert_fusion.3
  368.1 8.1 %bitcast_convert_fusion.1 = bf16[3072,768]{1,0:T(8,128)(2,1)} fusion(bf16[3,256,3072]{2,1,0:T(8,128)(2,1)} %get-tuple-element.141, bf16[3,256,768]{2,1,0:T(8,128)(2,1)S(1)} %copy-done.42), kind=kOutput, calls=%fused_computation.1 | convolution fusion | flops 3626237952 | bytes 10616832 | tf_op jit(solution)/shard_map/rd,re->de/dot_general | solution.py:1294
  376.3 5.6 bitcast_convert_fusion
  381.9 16.7 %collective-permute-done.15.refs_6_ = bf16[3,224,1536]{2,1,0:T(8,128)(2,1)} collective-permute-done((bf16[3,224,1536]{2,1,0:T(8,128)(2,1)}, bf16[3,224,1536]{2,1,0:T(8,128)(2,1)}, u32[]{:S(2)}, u32[]{:S(2)}) %collective-permute-start.15) | collective-permute-done | bytes 2064416 | tf_op jit(solution)/shard_map/ppermute | solution.py:30
  398.6 11.1 %shard_map.347 = (bf16[3,256,2304]{2,1,0:T(8,128)(2,1)}, f32[3,256,768]{2,1,0:T(8,128)}, f32[1,2304]{1,0:T(1,128)}, f32[1,768]{1,0:T(1,128)}, f32[1,768]{1,0:T(1,128)}) custom-call(bf16[3,256,768]{2,1,0:T(8,128)(2,1)} %refs_0_.1, f32[3,256,768]{2,1,0:T(8,128)} %get-tuple-element.121.refs_1_, bf16[3,256,768]{2,1,0:T(8,128)(2,1)} %get-tuple-element.122.refs_2_, ...), custom_call_target="tpu_custom_call" | custom-call | flops 2717908992 | bytes 23021568 | tf_op jit(solution)/shard_map/pallas_call | solution.py:183
  411.7 6.6 %bitcast_convert_fusion.2 = bf16[768,2304]{1,0:T(8,128)(2,1)} fusion(bf16[3,256,768]{2,1,0:T(8,128)(2,1)S(1)} %copy-done.38, bf16[3,256,2304]{2,1,0:T(8,128)(2,1)} %get-tuple-element.148), kind=kOutput, calls=%fused_computation.2 | convolution fusion | flops 2719678464 | bytes 8257536 | tf_op jit(solution)/shard_map/rd,re->de/dot_general | solution.py:1294
  418.3 1.6 pad_maximum_fusion.refs_0_
  419.9 147.4 %shard_map.348 = (f32[672,128]{1,0:T(8,128)}, f32[48,1024]{1,0:T(8,128)}, f32[192,768]{1,0:T(8,128)}, f32[48,3072]{1,0:T(8,128)}, f32[48,768]{1,0:T(8,128)}, /*index=5*/f32[48,2304]{1,0:T(8,128)}) custom-call(bf16[2,2,2,2,672,128]{5,4,3,2,1,0:T(8,128)(2,1)} %pad_maximum_fusion.refs_0_, bf16[2,2,2,2,48,1024]{5,4,3,2,1,0:T(8,128)(2,1)} %bitcast.91, ...), custom_call_target="tpu_custom_call" | custom-call | flops 9240576 | bytes 36962304 | tf_op jit(solution)/shard_map/pallas_call | solution.py:727
  567.3 0.8 slice_bitcast_fusion.2
  569.4 1.3 slice_bitcast_fusion.1
  570.7 1.6 slice_bitcast_fusion
  572.2 1.6 slice.91
  574.5 1.8 copy.70
  576.3 1.6 copy.71
  577.8 0.8 copy.72
  578.7 0.8 copy.73
  (132 shorter events, 14.2 us)
Async XLA Ops:
  0.7 8.6 %copy-start.4 = (bf16[3,256,8,128]{3,2,1,0:T(8,128)(2,1)S(1)}, bf16[3,256,8,128]{3,2,1,0:T(8,128)(2,1)}, u32[]{:S(2)}) copy-start(bf16[3,256,8,128]{3,2,1,0:T(8,128)(2,1)} %param.21) | copy-start | bytes 4718596
  3.8 28.6 %collective-permute-start.1 = (bf16[3,224,768]{2,1,0:T(8,128)(2,1)}, bf16[3,224,768]{2,1,0:T(8,128)(2,1)}, u32[]{:S(2)}, u32[]{:S(2)}) collective-permute-start(bf16[3,224,768]{2,1,0:T(8,128)(2,1)} %get-tuple-element.163), channel_id=1, source_target_pairs={{1,0},{2,1},{3,2},{4,3},{5,4},{6,5},{7,6},{8,7},{9,8},{10,9},{11,1... | collective-permute-start | bytes 3096584 | tf_op jit(solution)/shard_map/ppermute | solution.py:30
  5.7 8.7 %copy-start.17 = (f32[768]{0:T(1024)S(1)}, f32[768]{0:T(1024)}, u32[]{:S(2)}) copy-start(f32[768]{0:T(1024)} %param.23) | copy-start | bytes 9220
  5.7 9.3 %copy-start.18 = (f32[768]{0:T(1024)S(1)}, f32[768]{0:T(1024)}, u32[]{:S(2)}) copy-start(f32[768]{0:T(1024)} %param.29) | copy-start | bytes 9220
  5.7 9.9 %copy-start.19 = (f32[768]{0:T(1024)S(1)}, f32[768]{0:T(1024)}, u32[]{:S(2)}) copy-start(f32[768]{0:T(1024)} %param.24) | copy-start | bytes 9220
  5.7 10.5 %copy-start.20 = (f32[768]{0:T(1024)S(1)}, f32[768]{0:T(1024)}, u32[]{:S(2)}) copy-start(f32[768]{0:T(1024)} %param.28) | copy-start | bytes 9220
  5.7 11.1 %copy-start.21 = (f32[768]{0:T(1024)S(1)}, f32[768]{0:T(1024)}, u32[]{:S(2)}) copy-start(f32[768]{0:T(1024)} %param.30) | copy-start | bytes 9220
  5.7 11.6 %copy-start.22 = (f32[768]{0:T(1024)S(1)}, f32[768]{0:T(1024)}, u32[]{:S(2)}) copy-start(f32[768]{0:T(1024)} %param.34) | copy-start | bytes 9220
  5.7 12.2 %copy-start.27 = (s32[3,45]{1,0:T(4,128)S(1)}, s32[3,45]{1,0:T(4,128)}, u32[]{:S(2)}) copy-start(s32[3,45]{1,0:T(4,128)} %param.22) | copy-start | bytes 1624
  5.8 12.8 %copy-start.16 = (f32[2,768]{1,0:T(2,128)S(1)}, f32[2,768]{1,0:T(2,128)}, u32[]{:S(2)}) copy-start(f32[2,768]{1,0:T(2,128)} %param.26) | copy-start | bytes 18436
  5.8 26.6 %collective-permute-start = (bf16[3,224,768]{2,1,0:T(8,128)(2,1)}, bf16[3,224,768]{2,1,0:T(8,128)(2,1)}, u32[]{:S(2)}, u32[]{:S(2)}) collective-permute-start(bf16[3,224,768]{2,1,0:T(8,128)(2,1)} %get-tuple-element.164), channel_id=1, source_target_pairs={{0,1},{1,2},{2,3},{3,4},{4,5},{5,6},{6,7},{7,8},{8,9},{9,10},{10,1... | collective-permute-start | bytes 3096584 | tf_op jit(solution)/shard_map/ppermute | solution.py:30
  10.0 88.1 %copy-start.2 = (bf16[3,256,1024]{2,1,0:T(8,128)(2,1)}, bf16[3,256,1024]{2,1,0:T(8,128)(2,1)S(1)}, u32[]{:S(2)}) copy-start(bf16[3,256,1024]{2,1,0:T(8,128)(2,1)S(1)} %reshape.175.skip) | copy-start | bytes 4718596
  10.0 94.9 %collective-permute-start.5 = (bf16[3,48,1024]{2,1,0:T(8,128)(2,1)S(1)}, bf16[3,48,1024]{2,1,0:T(8,128)(2,1)S(1)}, u32[]{:S(2)}, u32[]{:S(2)}) collective-permute-start(bf16[3,48,1024]{2,1,0:T(8,128)(2,1)S(1)} %get-tuple-element.159), channel_id=1, source_target_pairs={{1,0},{2,1},{3,2},{4,3},{5,4},{6,5},{7,6},{8,7},{9,8},{10,9},{11,1... | collective-permute-start | bytes 884744 | tf_op jit(solution)/shard_map/ppermute | solution.py:30
  12.3 92.7 %collective-permute-start.4 = (bf16[3,48,1024]{2,1,0:T(8,128)(2,1)S(1)}, bf16[3,48,1024]{2,1,0:T(8,128)(2,1)S(1)}, u32[]{:S(2)}, u32[]{:S(2)}) collective-permute-start(bf16[3,48,1024]{2,1,0:T(8,128)(2,1)S(1)} %get-tuple-element.160), channel_id=1, source_target_pairs={{0,1},{1,2},{2,3},{3,4},{4,5},{5,6},{6,7},{7,8},{8,9},{9,10},{10,1... | collective-permute-start | bytes 884744 | tf_op jit(solution)/shard_map/ppermute | solution.py:30
  99.2 11.2 %collective-permute-start.3 = (bf16[3,48,1024]{2,1,0:T(8,128)(2,1)S(1)}, bf16[3,48,1024]{2,1,0:T(8,128)(2,1)S(1)}, u32[]{:S(2)}, u32[]{:S(2)}) collective-permute-start(bf16[3,48,1024]{2,1,0:T(8,128)(2,1)S(1)} %get-tuple-element.161), channel_id=1, source_target_pairs={{1,0},{2,1},{3,2},{4,3},{5,4},{6,5},{7,6},{8,7},{9,8},{10,9},{11,1... | collective-permute-start | bytes 884744 | tf_op jit(solution)/shard_map/ppermute | solution.py:30
  103.0 8.0 %collective-permute-start.2 = (bf16[3,48,1024]{2,1,0:T(8,128)(2,1)S(1)}, bf16[3,48,1024]{2,1,0:T(8,128)(2,1)S(1)}, u32[]{:S(2)}, u32[]{:S(2)}) collective-permute-start(bf16[3,48,1024]{2,1,0:T(8,128)(2,1)S(1)} %get-tuple-element.162), channel_id=1, source_target_pairs={{0,1},{1,2},{2,3},{3,4},{4,5},{5,6},{6,7},{7,8},{8,9},{9,10},{10,1... | collective-permute-start | bytes 884744 | tf_op jit(solution)/shard_map/ppermute | solution.py:30
  105.0 6.1 %copy-start.34 = (bf16[3,48,1024]{2,1,0:T(8,128)(2,1)}, bf16[3,48,1024]{2,1,0:T(8,128)(2,1)S(1)}, u32[]{:S(2)}) copy-start(bf16[3,48,1024]{2,1,0:T(8,128)(2,1)S(1)} %collective-permute-done.5.skip_right) | copy-start | bytes 884740
  105.0 6.1 %copy-start.35 = (bf16[3,48,1024]{2,1,0:T(8,128)(2,1)}, bf16[3,48,1024]{2,1,0:T(8,128)(2,1)S(1)}, u32[]{:S(2)}) copy-start(bf16[3,48,1024]{2,1,0:T(8,128)(2,1)S(1)} %collective-permute-done.4.skip_left) | copy-start | bytes 884740
  110.4 0.7 copy-start.36
  111.1 0.7 copy-start.37
  138.9 9.8 %collective-permute-start.6 = (bf16[3,48,1536]{2,1,0:T(8,128)(2,1)}, bf16[3,48,1536]{2,1,0:T(8,128)(2,1)S(1)}, u32[]{:S(2)}, u32[]{:S(2)}) collective-permute-start(bf16[3,48,1536]{2,1,0:T(8,128)(2,1)} %get-tuple-element.92), channel_id=1, source_target_pairs={{0,1},{1,2},{2,3},{3,4},{4,5},{5,6},{6,7},{7,8},{8,9},{9,10},{10,1... | collective-permute-start | bytes 1327112 | tf_op jit(solution)/shard_map/ppermute | solution.py:30
  140.8 12.5 %collective-permute-start.7 = (bf16[3,48,1536]{2,1,0:T(8,128)(2,1)}, bf16[3,48,1536]{2,1,0:T(8,128)(2,1)S(1)}, u32[]{:S(2)}, u32[]{:S(2)}) collective-permute-start(bf16[3,48,1536]{2,1,0:T(8,128)(2,1)} %get-tuple-element.93), channel_id=1, source_target_pairs={{1,0},{2,1},{3,2},{4,3},{5,4},{6,5},{7,6},{8,7},{9,8},{10,9},{11,1... | collective-permute-start | bytes 1327112 | tf_op jit(solution)/shard_map/ppermute | solution.py:30
  148.7 4.6 copy-start.28
  153.3 0.8 copy-start.29
  154.1 24.3 %copy-start.5 = (bf16[3,256,8,128]{3,2,1,0:T(8,128)(2,1)S(1)}, bf16[3,256,8,128]{3,2,1,0:T(8,128)(2,1)}, u32[]{:S(2)}) copy-start(bf16[3,256,8,128]{3,2,1,0:T(8,128)(2,1)} %param.39) | copy-start | bytes 4718596
  172.7 9.1 %collective-permute-start.8 = (bf16[3,48,1280]{2,1,0:T(8,128)(2,1)}, bf16[3,48,1280]{2,1,0:T(8,128)(2,1)S(1)}, u32[]{:S(2)}, u32[]{:S(2)}) collective-permute-start(bf16[3,48,1280]{2,1,0:T(8,128)(2,1)} %get-tuple-element.100), channel_id=1, source_target_pairs={{0,1},{1,2},{2,3},{3,4},{4,5},{5,6},{6,7},{7,8},{8,9},{9,10},{10,1... | collective-permute-start | bytes 1105928 | tf_op jit(solution)/shard_map/ppermute | solution.py:30
  174.7 9.2 %collective-permute-start.9 = (bf16[3,48,1280]{2,1,0:T(8,128)(2,1)}, bf16[3,48,1280]{2,1,0:T(8,128)(2,1)S(1)}, u32[]{:S(2)}, u32[]{:S(2)}) collective-permute-start(bf16[3,48,1280]{2,1,0:T(8,128)(2,1)} %get-tuple-element.101), channel_id=1, source_target_pairs={{1,0},{2,1},{3,2},{4,3},{5,4},{6,5},{7,6},{8,7},{9,8},{10,9},{11,1... | collective-permute-start | bytes 1105928 | tf_op jit(solution)/shard_map/ppermute | solution.py:30
  181.8 2.1 copy-start.9
  183.9 0.7 copy-start.10
  192.6 9.5 %collective-permute-start.10 = (bf16[3,48,1408]{2,1,0:T(8,128)(2,1)}, bf16[3,48,1408]{2,1,0:T(8,128)(2,1)S(1)}, u32[]{:S(2)}, u32[]{:S(2)}) collective-permute-start(bf16[3,48,1408]{2,1,0:T(8,128)(2,1)} %get-tuple-element.105), channel_id=1, source_target_pairs={{0,1},{1,2},{2,3},{3,4},{4,5},{5,6},{6,7},{7,8},{8,9},{9,10},{10,1... | collective-permute-start | bytes 1216520 | tf_op jit(solution)/shard_map/ppermute | solution.py:30
  194.6 10.9 %collective-permute-start.11 = (bf16[3,48,1408]{2,1,0:T(8,128)(2,1)}, bf16[3,48,1408]{2,1,0:T(8,128)(2,1)S(1)}, u32[]{:S(2)}, u32[]{:S(2)}) collective-permute-start(bf16[3,48,1408]{2,1,0:T(8,128)(2,1)} %get-tuple-element.106), channel_id=1, source_target_pairs={{1,0},{2,1},{3,2},{4,3},{5,4},{6,5},{7,6},{8,7},{9,8},{10,9},{11,1... | collective-permute-start | bytes 1216520 | tf_op jit(solution)/shard_map/ppermute | solution.py:30
  202.2 3.3 copy-start.30
  205.4 0.7 copy-start.31
  206.2 38.2 %copy-start.6 = (bf16[3,256,1024]{2,1,0:T(8,128)(2,1)S(1)}, bf16[3,256,1024]{2,1,0:T(8,128)(2,1)}, u32[]{:S(2)}) copy-start(bf16[3,256,1024]{2,1,0:T(8,128)(2,1)} %get-tuple-element.103) | copy-start | bytes 4718596
  238.6 7.4 %copy-start.3 = (f32[27,1,128,128]{3,2,1,0:T(8,128)S(1)}, f32[27,1,128,128]{3,2,1,0:T(8,128)}, u32[]{:S(2)}) copy-start(f32[27,1,128,128]{3,2,1,0:T(8,128)} %get-tuple-element.130) | copy-start | bytes 5308420
  238.6 9.2 %collective-permute-start.12 = (bf16[3,48,1280]{2,1,0:T(8,128)(2,1)}, bf16[3,48,1280]{2,1,0:T(8,128)(2,1)S(1)}, u32[]{:S(2)}, u32[]{:S(2)}) collective-permute-start(bf16[3,48,1280]{2,1,0:T(8,128)(2,1)} %get-tuple-element.110), channel_id=1, source_target_pairs={{0,1},{1,2},{2,3},{3,4},{4,5},{5,6},{6,7},{7,8},{8,9},{9,10},{10,1... | collective-permute-start | bytes 1105928 | tf_op jit(solution)/shard_map/ppermute | solution.py:30
  240.6 9.6 %collective-permute-start.13 = (bf16[3,48,1280]{2,1,0:T(8,128)(2,1)}, bf16[3,48,1280]{2,1,0:T(8,128)(2,1)S(1)}, u32[]{:S(2)}, u32[]{:S(2)}) collective-permute-start(bf16[3,48,1280]{2,1,0:T(8,128)(2,1)} %get-tuple-element.111), channel_id=1, source_target_pairs={{1,0},{2,1},{3,2},{4,3},{5,4},{6,5},{7,6},{8,7},{9,8},{10,9},{11,1... | collective-permute-start | bytes 1105928 | tf_op jit(solution)/shard_map/ppermute | solution.py:30
  247.8 2.5 copy-start.32
  250.3 0.7 copy-start.33
  347.8 8.3 %copy-start.40 = (bf16[3,256,768]{2,1,0:T(8,128)(2,1)S(1)}, bf16[3,256,768]{2,1,0:T(8,128)(2,1)}, u32[]{:S(2)}) copy-start(bf16[3,256,768]{2,1,0:T(8,128)(2,1)} %get-tuple-element.145) | copy-start | bytes 3538948
  347.8 8.3 %copy-start.41 = (bf16[3,256,768]{2,1,0:T(8,128)(2,1)S(1)}, bf16[3,256,768]{2,1,0:T(8,128)(2,1)}, u32[]{:S(2)}) copy-start(bf16[3,256,768]{2,1,0:T(8,128)(2,1)} %get-tuple-element.146) | copy-start | bytes 3538948
  350.3 31.7 %collective-permute-start.14 = (bf16[3,224,1536]{2,1,0:T(8,128)(2,1)}, bf16[3,224,1536]{2,1,0:T(8,128)(2,1)}, u32[]{:S(2)}, u32[]{:S(2)}) collective-permute-start(bf16[3,224,1536]{2,1,0:T(8,128)(2,1)} %get-tuple-element.125), channel_id=1, source_target_pairs={{0,1},{1,2},{2,3},{3,4},{4,5},{5,6},{6,7},{7,8},{8,9},{9,10},{10,1... | collective-permute-start | bytes 6193160 | tf_op jit(solution)/shard_map/ppermute | solution.py:30
  352.2 46.4 %collective-permute-start.15 = (bf16[3,224,1536]{2,1,0:T(8,128)(2,1)}, bf16[3,224,1536]{2,1,0:T(8,128)(2,1)}, u32[]{:S(2)}, u32[]{:S(2)}) collective-permute-start(bf16[3,224,1536]{2,1,0:T(8,128)(2,1)} %get-tuple-element.126), channel_id=1, source_target_pairs={{1,0},{2,1},{3,2},{4,3},{5,4},{6,5},{7,6},{8,7},{9,8},{10,9},{11,1... | collective-permute-start | bytes 6193160 | tf_op jit(solution)/shard_map/ppermute | solution.py:30
  356.1 2.3 copy-start.25
  356.1 2.2 copy-start.26
  356.1 2.3 copy-start.23
  356.2 2.3 copy-start.24
  356.2 2.3 copy-start.1
  358.5 2.4 copy-start.13
  363.6 4.5 copy-start.42
  363.6 12.7 %slice-start = ((s8[4718592]{0:T(1024)(128)(4,1)}), s8[4194304]{0:T(1024)(128)(4,1)S(1)}, s32[]{:S(2)}) async-start(s8[4718592]{0:T(1024)(128)(4,1)} %bitcast.101), calls=%async_computation | async-start | bytes 8388608
  368.1 8.2 %slice-start.1 = ((s8[4718592]{0:T(1024)(128)(4,1)}), s8[524288]{0:T(1024)(128)(4,1)S(1)}, s32[]{:S(2)}) async-start(s8[4718592]{0:T(1024)(128)(4,1)} %bitcast.101), calls=%async_computation.1 | async-start | bytes 1048576
  368.1 8.2 %copy-start.39 = (bf16[3,256,768]{2,1,0:T(8,128)(2,1)S(1)}, bf16[3,256,768]{2,1,0:T(8,128)(2,1)}, u32[]{:S(2)}) copy-start(bf16[3,256,768]{2,1,0:T(8,128)(2,1)} %get-tuple-element.143) | copy-start | bytes 3538948
  398.6 12.9 %copy-start.14 = (bf16[16,48]{1,0:T(8,128)(2,1)S(1)}, bf16[16,48]{1,0:T(8,128)(2,1)}, u32[]{:S(2)}) copy-start(bf16[16,48]{1,0:T(8,128)(2,1)} %reshape.188) | copy-start | bytes 4612
  398.6 12.9 %copy-start.15 = (bf16[16,48]{1,0:T(8,128)(2,1)S(1)}, bf16[16,48]{1,0:T(8,128)(2,1)}, u32[]{:S(2)}) copy-start(bf16[16,48]{1,0:T(8,128)(2,1)} %reshape.186) | copy-start | bytes 4612
  398.6 13.1 %copy-start.38 = (bf16[3,256,768]{2,1,0:T(8,128)(2,1)S(1)}, bf16[3,256,768]{2,1,0:T(8,128)(2,1)}, u32[]{:S(2)}) copy-start(bf16[3,256,768]{2,1,0:T(8,128)(2,1)} %get-tuple-element.147) | copy-start | bytes 3538948
  411.7 6.6 %copy-start = (bf16[27,1,16,8,128]{4,3,0,2,1:T(8,128)(2,1)S(1)}, bf16[27,1,16,8,128]{4,3,0,2,1:T(8,128)(2,1)}, u32[]{:S(2)}) copy-start(bf16[27,1,16,8,128]{4,3,0,2,1:T(8,128)(2,1)} %copy.49) | copy-start | bytes 2654212
  411.7 6.6 %copy-start.11 = (bf16[16,1,2,8,128]{4,3,2,0,1:T(8,128)(2,1)S(1)}, bf16[16,1,2,8,128]{4,3,2,0,1:T(8,128)(2,1)}, u32[]{:S(2)}) copy-start(bf16[16,1,2,8,128]{4,3,2,0,1:T(8,128)(2,1)} %copy.51) | copy-start | bytes 196612
  567.3 10.5 %copy-start.8 = (f32[48,3072]{1,0:T(8,128)S(1)}, f32[48,3072]{1,0:T(8,128)}, u32[]{:S(2)}) copy-start(f32[48,3072]{1,0:T(8,128)} %get-tuple-element.211) | copy-start | bytes 1769476
  567.3 11.3 %copy-start.7 = (f32[192,768]{1,0:T(8,128)S(1)}, f32[192,768]{1,0:T(8,128)}, u32[]{:S(2)}) copy-start(f32[192,768]{1,0:T(8,128)} %get-tuple-element.213) | copy-start | bytes 1769476
  570.7 8.8 %copy-start.12 = (f32[48,1024]{1,0:T(8,128)S(1)}, f32[48,1024]{1,0:T(8,128)}, u32[]{:S(2)}) copy-start(f32[48,1024]{1,0:T(8,128)} %get-tuple-element.215) | copy-start | bytes 589828
